TPU v7x, 32 devices: a whole 2x2x4 slice. The times are simulated.
32 devices in a mesh: pop: 4 (over y, core), col: 8 (over z, x).
Axes of the slice: x: 2, y: 2, z: 4, core: 2. Of those that a mesh axis runs over, the one named last changes fastest.
Arguments:
- tokens: bfloat16 [3584, 4096], P('pop'), may hold values from -6 to 6
- weight: bfloat16 [4096, 16384], P(None, ('col', 'pop')), may hold values from -0.09375 to 0.09375
- old_left: bfloat16 [448, 4, 4096], P('pop', None, 'col'), may hold values from -6 to 6
- old_right: bfloat16 [448, 4, 16384], P('pop', None, 'col'), may hold values from -6 to 6
- selected: int32 [4, 8], P('pop'), may hold values from 0 to 111, as said below
- shaping: float32 [4, 8], P('pop'), may hold values from -3 to 3
- new_left: bfloat16 [448, 4, 4096], P('pop', None, 'col'), may hold values from -6 to 6
- new_right: bfloat16 [448, 4, 16384], P('pop', None, 'col'), may hold values from -6 to 6
Outputs:
- updated: bfloat16 [4096, 16384], P(None, ('col', 'pop'))
- activations: bfloat16 [3584, 16384], P('pop', 'col')
Inputs may be any that keep to these rules, and one draw needn't show every extreme that they name: `selected`: each row names 8 different members of its group.
All inputs are finite; a program needn't handle non-finite values.
Results may differ from a plain program's by a relative error of at most 0.0055.
Values may be sent and summed in bfloat16 or wider, within the bound.
No kernel may reach another device: no remote copies, remote signals or barrier semaphores. Data moves between devices by JAX's collectives and lax.ppermute only.
A program may use at most 128 MiB of HBM per device.

v0:
```python
import math

import jax
import jax.numpy as jnp
from jax import lax
from jax.sharding import PartitionSpec as P

D = 4096
RANK = 4


noise_scale = 0.5


def contract_members(left_rows, right_rows):
    return lax.dot_general(
        left_rows, right_rows, (((0,), (0,)), ((), ())), preferred_element_type=jnp.float32
    )


def local(tokens, weight, old_left, old_right, selected, shaping, new_left, new_right):
    groups = lax.axis_size("pop")
    picked = selected[0]
    count = picked.shape[0]
    factor = 1.0 / math.sqrt(D * RANK * count * groups)
    weights_here = shaping[0] * factor
    chosen_left = jnp.take(old_left, picked, axis=0)
    chosen_right = jnp.take(old_right, picked, axis=0)
    scaled_local = (chosen_left.astype(jnp.float32) * weights_here[:, None, None]).astype(
        jnp.bfloat16
    )
    scaled_left = lax.all_gather(scaled_local, "col", axis=2, tiled=True)
    every_left = lax.all_gather(scaled_left, "pop", axis=0, tiled=True)
    narrow_right = lax.all_to_all(chosen_right, "pop", split_axis=2, concat_axis=0, tiled=True)
    delta = contract_members(
        every_left.reshape(-1, D), narrow_right.reshape(-1, narrow_right.shape[2])
    )
    updated = (weight.astype(jnp.float32) + delta).astype(jnp.bfloat16)
    base = jnp.dot(
        tokens,
        lax.all_gather(updated, "pop", axis=1, tiled=True),
        preferred_element_type=jnp.float32,
    )
    members_here = new_left.shape[0]
    slab = new_left.shape[2]
    offset = lax.axis_index("col") * slab
    token_slab = lax.dynamic_slice_in_dim(tokens, offset, slab, 1).reshape(members_here, -1, slab)
    partial_proj = jnp.einsum(
        "mtd,mrd->mtr", token_slab, new_left, preferred_element_type=jnp.float32
    )
    proj = lax.psum(partial_proj, "col").astype(jnp.bfloat16)
    side = jnp.einsum("mtr,mrh->mth", proj, new_right, preferred_element_type=jnp.float32).reshape(
        base.shape
    )
    pre = base + noise_scale / math.sqrt(D * RANK) * side
    return (updated, (jnp.maximum(pre, 0.0) ** 2).astype(jnp.bfloat16))


def solution(mesh):
    placed = (
        P("pop", None),
        P(None, ("col", "pop")),
        P("pop", None, "col"),
        P("pop", None, "col"),
        P("pop", None),
        P("pop", None),
        P("pop", None, "col"),
        P("pop", None, "col"),
    )
    return jax.shard_map(
        local,
        mesh=mesh,
        in_specs=placed,
        out_specs=(P(None, ("col", "pop")), P("pop", "col")),
        check_vma=False,
    )
```

profile of v0, /device:TPU:0, one launch (start us, length us, event | category | flops | bytes accessed | tf_op | source)
XLA Modules:
  0.0 219.5 jit_solution(4909113252714720285)
XLA Ops:
  7.2 0.0 copy-start
  7.2 0.0 all-gather.3.cloned.1.call-start
  7.2 0.8 fusion.7
  8.0 0.7 compare_and_fusion
  8.7 0.7 multiply_bitcast_fusion.1
  9.3 1.6 gather_fusion
  10.9 0.1 multiply_convert_fusion
  11.0 34.5 %all_gather.9 = bf16[8,4,4096]{2,1,0:T(4,128)(2,1)} all-gather(bf16[8,4,512]{2,1,0:T(4,128)(2,1)S(1)} %multiply_convert_fusion), channel_id=1, replica_groups=mesh['pop'=4,'col'=8] {'col'}, dimensions={2}, use_global_device_ids=true | all-gather | bytes 294912 | tf_op jit(solution)/shard_map/all_gather | solution.py:32
  45.6 0.0 all-gather.3.cloned.1.call-update
  45.6 0.0 all-gather.5.cloned.1.call-start
  45.6 2.2 gather_fusion.1
  47.8 0.1 broadcast_select_fusion
  47.9 2.5 %copy.22 = bf16[8,4,2048]{0,1,2:T(4,128)(2,1)} copy(bf16[8,4,2048]{2,1,0:T(4,128)(2,1)S(1)} %broadcast_select_fusion) | data formatting | bytes 262144 | tf_op jit(solution)/shard_map/jit(_take)/select_n | solution.py:28
  50.4 3.4 %reshape.77 = bf16[4,2,8192]{2,1,0:T(2,128)(2,1)S(1)} reshape(bf16[2048,4,8]{2,1,0:T(4,128)(2,1)} %bitcast.32) | data formatting | bytes 262144
  53.8 8.9 %all_to_all.15 = bf16[4,2,8192]{2,1,0:T(2,128)(2,1)S(1)} all-to-all(bf16[4,2,8192]{2,1,0:T(2,128)(2,1)S(1)} %reshape.77), channel_id=1, replica_groups=mesh['pop'=4,'col'=8] {'pop'}, dimensions={0} | all-to-all | bytes 262144 | tf_op jit(solution)/shard_map/all_to_all | solution.py:34
  62.8 3.4 %reshape.78 = bf16[2048,4,8]{2,1,0:T(4,128)(2,1)} reshape(bf16[4,2,8192]{2,1,0:T(2,128)(2,1)S(1)} %all_to_all.15) | data formatting | bytes 262144
  66.2 3.1 %copy.23 = bf16[8,4,4,512]{3,1,0,2:T(4,128)(2,1)S(1)} copy(bf16[8,4,4,512]{0,1,3,2:T(4,128)(2,1)} %bitcast.33) | data formatting | bytes 262144 | tf_op jit(solution)/shard_map/all_to_all | solution.py:34
  69.4 0.0 all-gather.3.cloned.1.call-done
  69.4 1.3 reshape.58
  70.8 0.0 copy-start.1
  70.8 5.5 %add_convert_fusion = bf16[4096,512]{1,0:T(8,128)(2,1)} fusion(bf16[4096,512]{1,0:T(8,128)(2,1)} %param.9, bf16[128,4096]{1,0:T(8,128)(2,1)S(1)} %reshape.58, bf16[128,512]{1,0:T(8,128)(2,1)S(1)} %reshape.59), kind=kOutput, calls=%fused_computation.2 | convolution fusion | flops 543162368 | bytes 9568256 | tf_op jit(solution)/shard_map/dot_general | solution.py:16
  76.3 0.0 all-gather.5.cloned.1.call-update
  76.4 0.0 copy-done.1
  76.4 1.7 fusion.3
  78.1 39.6 %psum.7 = bf16[112,8,4]{1,2,0:T(4,128)(2,1)S(1)} all-reduce(f32[112,8,4]{1,2,0:T(4,128)S(1)} %fusion.3), channel_id=1, replica_groups=mesh['pop'=4,'col'=8] {'col'}, use_global_device_ids=true, to_apply=%region_0.1 | all-reduce | flops 3584 | bytes 21504 | tf_op jit(solution)/shard_map/psum | solution.py:51
  117.7 0.0 copy-done
  117.7 3.8 %multiply_bitcast_fusion = f32[896,2048]{1,0:T(8,128)} fusion(bf16[112,4,2048]{2,1,0:T(4,128)(2,1)S(1)} %copy-done, bf16[112,8,4]{1,2,0:T(4,128)(2,1)S(1)} %psum.7), kind=kOutput, calls=%fused_computation.7 | convolution fusion | flops 16515072 | bytes 9182208 | tf_op jit(solution)/shard_map/mtr,mrh->mth/dot_general | solution.py:52
  121.5 8.6 %copy.24 = f32[896,2048]{0,1:T(8,128)} copy(f32[896,2048]{1,0:T(8,128)} %multiply_bitcast_fusion) | data formatting | bytes 14680064 | tf_op jit(solution)/shard_map/mul | solution.py:55
  130.1 52.3 %all-gather.5.cloned.1.call-done = bf16[4096,2048]{1,0:T(8,128)(2,1)} async-done(((bf16[4096,512]{1,0:T(8,128)(2,1)}), bf16[4096,2048]{1,0:T(8,128)(2,1)}) %all-gather.5.cloned.1.call-update) | async-done | bytes 16777232 | tf_op jit(solution)/shard_map/all_gather | solution.py:41
  182.4 24.2 %fusion.2 = bf16[896,2048]{0,1:T(8,128)(2,1)} fusion(f32[896,2048]{0,1:T(8,128)} %copy.24, bf16[4096,2048]{1,0:T(8,128)(2,1)} %all-gather.5.cloned.1.call-done, bf16[896,4096]{1,0:T(8,128)(2,1)} %param.8), kind=kOutput, calls=%fused_computation.6 | convolution fusion | flops 15039725568 | bytes 35127296 | tf_op jit(solution)/shard_map/dot_general | solution.py:39
  206.6 6.0 %copy.25 = bf16[896,2048]{1,0:T(8,128)(2,1)} copy(bf16[896,2048]{0,1:T(8,128)(2,1)} %fusion.2) | data formatting | bytes 7340032
  (2 shorter events, 0.0 us)
Async XLA Ops:
  7.2 110.5 %copy-start = (bf16[112,4,2048]{2,1,0:T(4,128)(2,1)S(1)}, bf16[112,4,2048]{2,1,0:T(4,128)(2,1)}, u32[]{:S(2)}) copy-start(bf16[112,4,2048]{2,1,0:T(4,128)(2,1)} %param.15) | copy-start | bytes 5505028
  7.2 62.3 %all-gather.3.cloned.1.call-start = ((), (), s32[]{:S(2)}) async-start(), calls=%async_computation.1 | async-start | bytes 1310720 | tf_op jit(solution)/shard_map/all_gather | solution.py:33
  45.6 136.8 %all-gather.5.cloned.1.call-start = ((), (), s32[]{:S(2)}) async-start(), calls=%async_computation.2 | async-start | bytes 20971520 | tf_op jit(solution)/shard_map/all_gather | solution.py:41
  70.8 5.6 %copy-start.1 = (bf16[112,4,512]{2,1,0:T(4,128)(2,1)S(1)}, bf16[112,4,512]{2,1,0:T(4,128)(2,1)}, u32[]{:S(2)}) copy-start(bf16[112,4,512]{2,1,0:T(4,128)(2,1)} %param.14) | copy-start | bytes 1376260
Sparse Core Ops, SparseCore 0:
  45.7 19.0 all-gather.2
  76.5 105.8 all-gather.4
where the time goes:
time: 220 us; the launch traced here: 219 us
  blocking collectives  83.1 us (38%)
  waiting for transfers between devices  52.3 us (24%)
  matrix products  35.2 us (16%)
  local copies, waits for them, and re-layouts  32.3 us (15%)
  between operations  14.1 us (6%)
  other arithmetic  2.32 us (1%)
    all_gather x1, waiting for transfers between devices, local(): lax.all_gather(updated, 'pop', axis=1, tiled=True)  52.3 us
    psum x1, blocking collectives, local(): proj = lax.psum(partial_proj, 'col').astype(jnp.bfloat16)  39.6 us
    all_gather x1, blocking collectives, local(): scaled_left = lax.all_gather(scaled_local, 'col', axis=2, tiled=True)  34.5 us
    dot_general x1, matrix products, local(): jnp.dot(tokens, lax.all_gather(updated, 'pop', axis=1, tiled=True), prefe...  24.2 us
    unnamed x7, local copies, waits for them, and re-layouts  12.9 us
    all_to_all x1, blocking collectives, local(): lax.all_to_all(chosen_right, 'pop', split_axis=2, concat_axis=0, tiled=True)  8.95 us
    mul x1, local copies, waits for them, and re-layouts, local(): pre = base + noise_scale / math.sqrt(D * RANK) * side  8.62 us
    dot_general x1, matrix products, contract_members(): lax.dot_general(left_rows, right_rows, (((0,), (0,)), ((), ())), preferre...  5.54 us
  transfers between devices with their start and end apart: 2, of which 1 were waited for; matrix products, arithmetic and copies ran while one was open for 13% of the time, Pallas kernels for 0%

commit v1 on v0

v1 whole, which is shorter than its diff:
```python
import functools
import math

import jax
import jax.numpy as jnp
from jax import lax
from jax.experimental import pallas as pl
from jax.experimental.pallas import tpu as pltpu
from jax.sharding import PartitionSpec as P

noise_scale = 0.5
PIECES = (1, 1, 3, 8, 2, 1)
LIMIT = 20 * 2**20
WIDE = 58 * 2**20


def params():
    return pltpu.CompilerParams(dimension_semantics=("arbitrary",), vmem_limit_bytes=LIMIT)


def cost():
    return pl.CostEstimate(flops=1, bytes_accessed=1, transcendentals=0)


def swap(array, axis, bit):
    return lax.ppermute(array, axis, [(i, i ^ bit) for i in range(lax.axis_size(axis))])


def bits(size, least=1):
    bit = least
    while bit < size:
        yield bit
        bit *= 2


MARK = jax.ShapeDtypeStruct((8, 128), jnp.float32)


def vmem():
    return pl.BlockSpec(memory_space=pltpu.VMEM)


def anywhere():
    return pl.BlockSpec(memory_space=pl.ANY)


def gate_kernel(mark_at, *refs):
    refs[mark_at][...] = jnp.zeros(MARK.shape, MARK.dtype)


def gate(array, *after):
    return pl.pallas_call(
        functools.partial(gate_kernel, len(after) + 2),
        in_specs=[anywhere()] * (1 + len(after)),
        out_specs=[anywhere(), vmem()],
        out_shape=[jax.ShapeDtypeStruct(array.shape, array.dtype), MARK],
        input_output_aliases={0: 0},
        compiler_params=pltpu.CompilerParams(vmem_limit_bytes=2**20),
        cost_estimate=cost(),
    )(array, *after)


def cut_kernel(start, wt, after, out, mark, sem):
    copy = pltpu.make_async_copy(wt.at[pl.ds(start, out.shape[0])], out, sem)
    copy.start()
    copy.wait()
    mark[...] = jnp.zeros(MARK.shape, MARK.dtype)


def cut(weight, start, depth, after):
    return pl.pallas_call(
        functools.partial(cut_kernel, start),
        in_specs=[anywhere()] * 2,
        out_specs=[vmem()] * 2,
        out_shape=[jax.ShapeDtypeStruct((depth, weight.shape[1]), weight.dtype), MARK],
        scratch_shapes=[pltpu.SemaphoreType.DMA],
        compiler_params=pltpu.CompilerParams(vmem_limit_bytes=WIDE),
        cost_estimate=cost(),
    )(weight, after)


def copy_kernel(wt, after, out):
    out[...] = wt[...]


def copy_of(weight, after):
    depth, width = weight.shape
    block = pl.BlockSpec((depth // 4, width), lambda k: (k, 0))
    return pl.pallas_call(
        copy_kernel,
        grid=(4,),
        in_specs=[block, anywhere()],
        out_specs=block,
        out_shape=jax.ShapeDtypeStruct(weight.shape, weight.dtype),
        compiler_params=pltpu.CompilerParams(
            dimension_semantics=("arbitrary",), vmem_limit_bytes=WIDE
        ),
        cost_estimate=cost(),
    )(weight, after)


def pick_kernel(factor, picked, shaping, lefts, rights, wt, packed, left, right, mark, sem):
    count, rank, _ = lefts.shape
    chosen, width = picked.shape[1], packed.shape[1]
    tall = chosen * rank
    first = tall * (left.shape[1] + right.shape[1]) // width
    depth = packed.shape[0] - first
    copy = pltpu.make_async_copy(wt.at[pl.ds(0, depth)], packed.at[pl.ds(first, depth)], sem)
    copy.start()
    scaled, plain = [], []
    for slot in range(chosen):
        member = picked[0, slot]
        scale = shaping[0, slot] * factor
        scaled.append(lefts[member].astype(jnp.float32) * scale)
        plain.append(rights[member].astype(jnp.float32))
    scaled = jnp.concatenate(scaled, 0).astype(jnp.bfloat16)
    plain = jnp.concatenate(plain, 0).astype(jnp.bfloat16)
    left[...] = scaled
    right[...] = plain
    at = 0
    for whole in (scaled, plain):
        for block in range(whole.shape[1] // width):
            packed[at : at + tall, :] = whole[:, block * width : (block + 1) * width]
            at += tall
    mark[...] = jnp.zeros(MARK.shape, MARK.dtype)
    copy.wait()


def pick(factor, selected, shaping, old_left, old_right, weight, depth):
    tall = selected.shape[1] * old_left.shape[1]
    slab, wide, width = old_left.shape[2], old_right.shape[2], weight.shape[1]
    rows = tall * (slab + wide) // width + depth
    return pl.pallas_call(
        functools.partial(pick_kernel, factor),
        in_specs=[pl.BlockSpec(memory_space=pltpu.SMEM)] * 2 + [vmem()] * 2 + [anywhere()],
        out_specs=[vmem()] * 4,
        out_shape=[
            jax.ShapeDtypeStruct((rows, width), weight.dtype),
            jax.ShapeDtypeStruct((tall, slab), weight.dtype),
            jax.ShapeDtypeStruct((tall, wide), weight.dtype),
            MARK,
        ],
        scratch_shapes=[pltpu.SemaphoreType.DMA],
        compiler_params=pltpu.CompilerParams(vmem_limit_bytes=WIDE),
        cost_estimate=cost(),
    )(selected, shaping, old_left, old_right, weight)


def unpack(packed, tall, slab, wide):
    width = packed.shape[1]
    blocks = [slab // width, wide // width]
    got, at = [], 0
    for count in blocks:
        got.append(
            jnp.concatenate([packed[at + tall * i : at + tall * (i + 1)] for i in range(count)], 1)
        )
        at += tall * count
    return (*got, packed[at:])


def mine(shape, rank, each):
    row = lax.broadcasted_iota(jnp.int32, shape, 0)
    token = lax.broadcasted_iota(jnp.int32, shape, 1)
    return lax.div(row, rank) == lax.div(token, each)


def proj_kernel(rank, each, where, left, tok, after, out):
    full = lax.dot_general(
        left[...], tok[...], (((1,), (1,)), ((), ())), preferred_element_type=jnp.float32
    )
    full = jnp.where(mine(full.shape, rank, each), full, 0.0)
    out[...] = full.reshape(-1, *out.shape).sum(0)


def project(tokens, lefts, rank, each, where, after):
    rows, slab = tokens.shape[0], lefts.shape[1]
    return pl.pallas_call(
        functools.partial(proj_kernel, rank, each),
        grid_spec=pltpu.PrefetchScalarGridSpec(
            num_scalar_prefetch=1,
            grid=(1,),
            in_specs=[
                pl.BlockSpec(lefts.shape, lambda k, at: (0, 0)),
                pl.BlockSpec((rows, slab), lambda k, at: (0, at[1])),
                pl.BlockSpec(memory_space=pl.ANY),
            ],
            out_specs=pl.BlockSpec((2 * rank, rows), lambda k, at: (0, 0)),
        ),
        out_shape=jax.ShapeDtypeStruct((2 * rank, rows), jnp.float32),
        compiler_params=params(),
        cost_estimate=cost(),
    )(where, lefts, tokens, after)


def turn_kernel(where, left, out):
    out[...] = left[...].T


def turn(left, where):
    blocks, sels, slab = left.shape
    return pl.pallas_call(
        turn_kernel,
        grid_spec=pltpu.PrefetchScalarGridSpec(
            num_scalar_prefetch=1,
            grid=(blocks,),
            in_specs=[pl.BlockSpec((None, sels, slab), lambda k, at: (k ^ at[1], 0, 0))],
            out_specs=pl.BlockSpec((slab, sels), lambda k, at: (k, 0)),
        ),
        out_shape=jax.ShapeDtypeStruct((blocks * slab, sels), left.dtype),
        compiler_params=params(),
        cost_estimate=cost(),
    )(where, left)


def spread_kernel(rank, each, proj, out):
    narrow = proj[...].astype(jnp.bfloat16).astype(jnp.float32)
    full = jnp.tile(narrow, (out.shape[1] // narrow.shape[0], 1))
    out[...] = jnp.where(mine(full.shape, rank, each), full, 0.0).T.astype(jnp.bfloat16)


def spread_out(proj, members, rank, each):
    return pl.pallas_call(
        functools.partial(spread_kernel, rank, each),
        in_specs=[pl.BlockSpec(memory_space=pltpu.VMEM)],
        out_specs=pl.BlockSpec(memory_space=pltpu.VMEM),
        out_shape=jax.ShapeDtypeStruct((proj.shape[1], members * rank), jnp.bfloat16),
        compiler_params=pltpu.CompilerParams(vmem_limit_bytes=LIMIT),
        cost_estimate=cost(),
    )(proj)


def columns(ref, at, width):
    return ref[:, pl.ds(pl.multiple_of(at * width, width), width)]


def refresh(wt, left, right):
    delta = jnp.dot(left, right, preferred_element_type=jnp.float32)
    return (wt.astype(jnp.float32) + delta).astype(jnp.bfloat16)


def finish(total):
    return (jnp.maximum(total, 0.0) ** 2).astype(jnp.bfloat16)


def begin(scale, spread, rights, at, width):
    side = jnp.dot(spread[...], columns(rights, at, width), preferred_element_type=jnp.float32)
    return scale * side


def full_kernel(scale, keep, begun, where, tok, wt, left, right, spread, rights, *refs):
    out, mark, held = refs[1 if begun else 2], refs[-2], refs[-1]
    width, unit = wt.shape[1], wt.shape[0]
    step = pl.program_id(0)

    @pl.when(step == 0)
    def _():
        mark[...] = jnp.zeros(MARK.shape, MARK.dtype)
        held[...] = begin(scale, spread, rights, where[0], width)

    at = pl.multiple_of(step * unit, unit)
    fresh = refresh(wt[...], left[pl.ds(at, unit), :], columns(right, where[0], width))
    if keep:
        refs[-3][...] = fresh
    held[...] += jnp.dot(tok[:, pl.ds(at, unit)], fresh, preferred_element_type=jnp.float32)

    @pl.when(step == pl.num_programs(0) - 1)
    def _():
        out[...] = finish(held[...])


def first_kernel(scale, start, where, tok, wt, left, right, spread, rights, after, out):
    width, unit = wt.shape[1], wt.shape[0]
    fresh = refresh(wt[...], left[start : start + unit, :], columns(right, where[0], width))
    out[...] = begin(scale, spread, rights, where[0], width) + jnp.dot(
        tok[:, start : start + unit], fresh, preferred_element_type=jnp.float32
    )


def middle_kernel(start, where, tok, wt, left, right, before, after, out):
    width, unit = wt.shape[1], wt.shape[0]
    fresh = refresh(wt[...], left[start : start + unit, :], columns(right, where[0], width))
    out[...] = before[...] + jnp.dot(
        tok[:, start : start + unit], fresh, preferred_element_type=jnp.float32
    )


def last_kernel(start, where, tok, wt, left, right, before, after, acts, out, kept):
    width, unit = wt.shape[1], wt.shape[0]
    step, part = pl.program_id(0), out.shape[0]

    @pl.when(step == 0)
    def _():
        kept[...] = refresh(
            wt[...], left[start : start + unit, :], columns(right, where[0], width)
        )

    rows = pl.ds(pl.multiple_of(step * part, part), part)
    out[...] = finish(
        before[rows, :]
        + jnp.dot(
            tok[rows, start : start + unit], kept[...], preferred_element_type=jnp.float32
        )
    )


def call(kernel, where, grid, specs, args, out_specs, out_shape, aliases=None, scratch=()):
    return pl.pallas_call(
        kernel,
        grid_spec=pltpu.PrefetchScalarGridSpec(
            num_scalar_prefetch=1,
            grid=grid,
            in_specs=specs,
            out_specs=out_specs,
            scratch_shapes=list(scratch),
        ),
        out_shape=out_shape,
        input_output_aliases=aliases or {},
        compiler_params=params(),
        cost_estimate=cost(),
    )(where, *args)


def run_block(where, tokens, wt, left, right, start, scale, spread, rights, acts, before, after, keep):
    rows = tokens.shape[0]
    depth, width = wt.shape
    first, last, begun = start == 0, acts is not None, isinstance(acts, tuple)
    held = pl.BlockSpec(memory_space=pltpu.VMEM)
    anywhere = pl.BlockSpec(memory_space=pl.ANY)
    tile = pl.BlockSpec((rows, width), lambda k, at: (0, at[0]))
    if first and last:
        unit = depth // 4
        block = pl.BlockSpec((unit, width), lambda k, at: (k, 0))
        specs, args = [held, block] + [held] * 4, [tokens, wt, left, right, spread, rights]
        specs, args = specs + [anywhere], args + [after]
        aliases = {}
        if not begun:
            specs, args = specs + [anywhere], args + [acts]
            aliases = {len(args): 0}
        shape = acts if begun else acts.shape
        out_shape, out_specs = [jax.ShapeDtypeStruct(shape, jnp.bfloat16)], [tile]
        if keep:
            out_shape.append(jax.ShapeDtypeStruct((depth, width), jnp.bfloat16))
            out_specs.append(block)
        out_shape.append(MARK)
        out_specs.append(vmem())
        return call(
            functools.partial(full_kernel, scale, keep, begun),
            where, (4,), specs, args, out_specs, out_shape, aliases,
            [pltpu.VMEM((rows, width), jnp.float32)],
        )
    sums = jax.ShapeDtypeStruct((rows, width), jnp.float32)
    if first:
        return call(
            functools.partial(first_kernel, scale, start),
            where, (1,), [held] * 6 + [anywhere],
            [tokens, wt, left, right, spread, rights, after], held, sums,
        )
    if not last:
        return call(
            functools.partial(middle_kernel, start),
            where, (1,), [held] * 5 + [anywhere],
            [tokens, wt, left, right, before, after], held, sums, {5: 0},
        )
    part = rows // 4
    return call(
        functools.partial(last_kernel, start),
        where, (4,), [held] * 5 + [anywhere] * 2,
        [tokens, wt, left, right, before, after, acts],
        pl.BlockSpec((part, width), lambda k, at: (k, at[0])),
        jax.ShapeDtypeStruct(acts.shape, jnp.bfloat16), {7: 0},
        [pltpu.VMEM((depth, width), jnp.bfloat16)],
    )


def local(tokens, weight, old_left, old_right, selected, shaping, new_left, new_right):
    groups = lax.axis_size("pop")
    me = lax.axis_index("pop")
    spot = lax.axis_index("col")
    depth, width = weight.shape
    members, rank, slab = new_left.shape
    rows = tokens.shape[0]
    each = rows // members
    count = selected.shape[1]
    scale = noise_scale / math.sqrt(depth * rank)
    grain = depth // sum(PIECES)
    chips = groups // 2
    where = jnp.stack([me, spot]).astype(jnp.int32)

    plan = []
    hops = [chips // 2] + [hop for hop in range(1, chips) if hop != chips // 2]
    for hop in hops:
        at = 0
        for piece in PIECES if hop == hops[-1] else (sum(PIECES),):
            plan.append((hop, at * grain, piece * grain))
            at += piece

    def send(index, piece):
        turn = [(p, (p + 2 * plan[index][0]) % groups) for p in range(groups)]
        return lax.ppermute(piece, "pop", turn)

    factor = 1.0 / math.sqrt(depth * rank * count * groups)
    packed, left, right, mark = pick(
        factor, selected, shaping, old_left, old_right, weight, plan[0][2]
    )
    arrived = [send(0, packed)]
    piece, mark = cut(weight, *plan[1][1:], mark)
    arrived.append(send(1, piece))
    proj = project(tokens, new_left.reshape(-1, slab), rank, each, where, mark)
    tall = count * rank
    lefts, rights, arrived[0] = unpack(arrived[0], tall, slab, old_right.shape[2])
    left, right = jnp.concatenate([left, lefts], 0), jnp.concatenate([right, rights], 0)
    for bit in bits(chips, 2):
        left = jnp.concatenate([left, swap(left, "pop", bit)], 0)
        right = jnp.concatenate([right, swap(right, "pop", bit)], 0)
    pieces = [weight[start : start + size] for _, start, size in plan[2:]]
    piece, mark = gate(pieces[0], mark)
    arrived.append(send(2, piece))
    own = copy_of(weight, left)
    right = jnp.concatenate([right, swap(right, "pop", 1)], 0)
    left = left[None]
    for turns, bit in enumerate(bits(lax.axis_size("col"))):
        left = jnp.concatenate([left, swap(left, "col", bit)], 0)
        proj = proj + swap(proj, "col", bit)
        if turns == 0:
            arrived[1], mark = gate(arrived[1], left)
            piece, mark = gate(pieces[1], mark)
            arrived.append(send(3, piece))
            left, _ = gate(left, mark)
    arrived[2], mark = gate(arrived[2], left)
    piece, mark = gate(pieces[2], mark)
    arrived.append(send(4, piece))
    left, _ = gate(left, mark)
    own, mark = gate(own, right, proj)
    sibling = swap(own, "pop", 1)
    left = turn(jnp.concatenate([left, swap(left, "pop", 1)], 1), where)
    spread = spread_out(proj, members, rank, each)
    rights = new_right.reshape(members * rank, -1)

    def run(block, wt, start, before, acts, after, keep=False):
        return run_block(
            jnp.reshape(block, (1,)).astype(jnp.int32),
            tokens, wt, left, right, start, scale, spread, rights, acts, before, after, keep,
        )

    narrow = width % 128 != 0
    core = lax.rem(me, 2)

    def pair(own, other):
        return jnp.where(
            core == 0, jnp.concatenate([own, other], 1), jnp.concatenate([other, own], 1)
        )

    whole = (rows, width * groups)
    if narrow:
        acts, both, done = run(me // 2, pair(weight, sibling), 0, None, whole, where, keep=True)
        updated = lax.dynamic_slice_in_dim(both, core * width, width, 1)
    else:
        acts, updated, done = run(me, weight, 0, None, whole, where, keep=True)
    crossed = [None] * len(plan)

    def arrive(index, after):
        arrived[index], mark = gate(arrived[index], after)
        if index + 2 < len(plan):
            piece, mark = gate(pieces[index], mark)
            arrived.append(send(index + 2, piece))

    def cross(index, after):
        arrived[index], _ = gate(arrived[index], after)
        crossed[index] = swap(arrived[index], "pop", 1)

    cross(0, done)
    cross(1, done)
    if not narrow:
        acts, done = run(me ^ 1, sibling, 0, None, acts, done)
    cross(2, done)
    for index, (hop, start, size) in enumerate(plan):
        if index > 2:
            arrive(index, done)
            cross(index, done)
        part, other = arrived[index], crossed[index]
        if start == 0:
            sums = [None, None]
        ends = start + size == depth
        source = lax.rem(me - 2 * hop + 2 * groups, groups)
        tasks = ((source, part), (source ^ 1, other))
        if narrow:
            tasks = ((source // 2, pair(part, other)),)
        for side, (block, wt) in enumerate(tasks):
            got = run(block, wt, start, sums[side], acts if ends else None, done)
            if not ends:
                sums[side] = done = got
            elif start == 0:
                acts, done = got
            else:
                acts = got
    return updated, acts


def solution(mesh):
    placed = (
        P("pop", None),
        P(None, ("col", "pop")),
        P("pop", None, "col"),
        P("pop", None, "col"),
        P("pop", None),
        P("pop", None),
        P("pop", None, "col"),
        P("pop", None, "col"),
    )
    return jax.shard_map(
        local,
        mesh=mesh,
        in_specs=placed,
        out_specs=(P(None, ("col", "pop")), P("pop", "col")),
        check_vma=False,
    )
```

time: 220 us -> 159 us (0.72)
  blocking collectives: 83.1 us -> 0 us
  Pallas kernels: 0 us -> 56.4 us
  matrix products: 35.2 us -> 0 us
  starting transfers between devices: 0.08 us -> 21.2 us
  between operations: 14.1 us -> 1.11 us
  waiting for transfers between devices: 52.3 us -> 45.6 us
    pallas_call x0 -> x38, Pallas kernels: none -> 56.4 us  [the longest x14 36 us: call(): pl.pallas_call(kernel, grid_spec=pltpu.PrefetchScalarGridSpec(num_scalar_...]
    all_gather x2 -> x0, waiting for transfers between devices: 52.3 us -> none  [the longest x1 52.3 us: local(): lax.all_gather(updated, 'pop', axis=1, tiled=True)]
    ppermute x0 -> x21, waiting for transfers between devices: none -> 45.6 us  [the longest x6 24.5 us: send(): return lax.ppermute(piece, 'pop', turn)]
    psum x1 -> x0, blocking collectives: 39.6 us -> none  [local(): proj = lax.psum(partial_proj, 'col').astype(jnp.bfloat16)]
    dot_general x4 -> x0, matrix products: 35.2 us -> none  [the longest x1 24.2 us: local(): jnp.dot(tokens, lax.all_gather(updated, 'pop', axis=1, tiled=True), prefe...]
    all_gather x1 -> x0, blocking collectives: 34.5 us -> none  [local(): scaled_left = lax.all_gather(scaled_local, 'col', axis=2, tiled=True)]
    ppermute x0 -> x21, starting transfers between devices: none -> 21.2 us  [the longest x15 13.2 us: swap(): lax.ppermute(array, axis, [(i, i ^ bit) for i in range(lax.axis_size(axis...]
    unnamed x7 -> x70, local copies, waits for them, and re-layouts: 12.9 us -> 25.1 us
  transfers between devices with their start and end apart: 2 -> 21, of which waited for: 1 -> 10; matrix products, arithmetic and copies ran while one was open for 13% -> 6% of each run, Pallas kernels for 0% -> 30%
where the time goes in v1:
time: 159 us; the launch traced here: 158 us
  Pallas kernels  56.4 us (35%)
  waiting for transfers between devices  45.6 us (29%)
  local copies, waits for them, and re-layouts  32 us (20%)
  starting transfers between devices  21.2 us (13%)
  other arithmetic  1.87 us (1%)
    pallas_call x14, Pallas kernels, call(): pl.pallas_call(kernel, grid_spec=pltpu.PrefetchScalarGridSpec(num_scalar_...  36 us
    unnamed x70, local copies, waits for them, and re-layouts  25.1 us
    ppermute x6, waiting for transfers between devices, send(): return lax.ppermute(piece, 'pop', turn)  24.5 us
    ppermute x15, waiting for transfers between devices, swap(): lax.ppermute(array, axis, [(i, i ^ bit) for i in range(lax.axis_size(axis...  21.1 us
    ppermute x15, starting transfers between devices, swap(): lax.ppermute(array, axis, [(i, i ^ bit) for i in range(lax.axis_size(axis...  13.2 us
    ppermute x6, starting transfers between devices, send(): return lax.ppermute(piece, 'pop', turn)  7.97 us
    pallas_call x18, Pallas kernels, gate(): pl.pallas_call(functools.partial(gate_kernel, len(after) + 2), in_specs=[...  7.79 us
    pallas_call x1, Pallas kernels, copy_of(): pl.pallas_call(copy_kernel, grid=(4,), in_specs=[block, anywhere()], out_...  4.79 us
  transfers between devices with their start and end apart: 21, of which 10 were waited for; matrix products, arithmetic and copies ran while one was open for 6% of the time, Pallas kernels for 30%

profile of v1, /device:TPU:0, one launch (start us, length us, event | category | flops | bytes accessed | tf_op | source)
XLA Modules:
  0.0 158.2 jit_solution(9774178677713761474)
XLA Ops:
  0.6 3.4 %shard_map.95 = (bf16[416,512]{1,0:T(8,128)(2,1)}, bf16[32,512]{1,0:T(8,128)(2,1)}, bf16[32,2048]{1,0:T(8,128)(2,1)}, f32[8,128]{1,0:T(8,128)}) custom-call(s32[1,8]{1,0:T(1,128)} %picked.1, f32[1,8]{1,0:T(1,128)} %shaping.1, bf16[112,4,512]{2,1,0:T(4,128)(2,1)} %lefts.1, bf16[112,4,2048]{2,1,0:T(4,128)(2,1)} %rights.1, bf16[4096,512]{1,0:T(8,128)(2,1)} %wt.7), custom_call_target="tpu_custom_call" | custom-call | flops 1 | bytes 1 | tf_op jit(solution)/shard_map/pallas_call | solution.py:133
  4.1 3.0 %collective-permute-start = (bf16[416,512]{1,0:T(8,128)(2,1)}, bf16[416,512]{1,0:T(8,128)(2,1)S(1)}, u32[]{:S(2)}, u32[]{:S(2)}) collective-permute-start(bf16[416,512]{1,0:T(8,128)(2,1)} %get-tuple-element.37), channel_id=1, source_target_pairs={{0,16},{8,24},{16,0},{24,8},{1,17},{9,25},{17,1},{25,9},{2,18},{10... | collective-permute-start | bytes 1277960 | tf_op jit(solution)/shard_map/ppermute | solution.py:399
  7.1 1.7 %shard_map.96 = (bf16[256,512]{1,0:T(8,128)(2,1)}, f32[8,128]{1,0:T(8,128)}) custom-call(bf16[4096,512]{1,0:T(8,128)(2,1)} %wt.7, f32[8,128]{1,0:T(8,128)} %get-tuple-element.38.after), custom_call_target="tpu_custom_call" | custom-call | flops 1 | bytes 1 | tf_op jit(solution)/shard_map/pallas_call | solution.py:71
  9.0 8.2 %collective-permute-done = bf16[416,512]{1,0:T(8,128)(2,1)S(1)} collective-permute-done((bf16[416,512]{1,0:T(8,128)(2,1)}, bf16[416,512]{1,0:T(8,128)(2,1)S(1)}, u32[]{:S(2)}, u32[]{:S(2)}) %collective-permute-start) | collective-permute-done | bytes 426016 | tf_op jit(solution)/shard_map/ppermute | solution.py:399
  17.4 3.1 %copy-done = bf16[896,4096]{1,0:T(8,128)(2,1)S(1)} copy-done((bf16[896,4096]{1,0:T(8,128)(2,1)S(1)}, bf16[896,4096]{1,0:T(8,128)(2,1)}, u32[]{:S(2)}) %copy-start) | copy-done | bytes 7340056
  21.1 1.2 shard_map.105
  22.4 1.8 %collective-permute-start.8 = (f32[8,896]{1,0:T(8,128)S(1)}, f32[8,896]{1,0:T(8,128)S(1)}, u32[]{:S(2)}, u32[]{:S(2)}) collective-permute-start(f32[8,896]{1,0:T(8,128)S(1)} %shard_map.105), channel_id=1, source_target_pairs={{0,1},{1,0},{2,3},{3,2},{4,5},{5,4},{6,7},{7,6},{8,9},{9,8},{10,11... | collective-permute-start | bytes 86024 | tf_op jit(solution)/shard_map/ppermute | solution.py:26
  24.1 2.2 %collective-permute-done.8 = f32[8,896]{1,0:T(8,128)S(1)} collective-permute-done((f32[8,896]{1,0:T(8,128)S(1)}, f32[8,896]{1,0:T(8,128)S(1)}, u32[]{:S(2)}, u32[]{:S(2)}) %collective-permute-start.8) | collective-permute-done | bytes 28704 | tf_op jit(solution)/shard_map/ppermute | solution.py:26
  26.3 1.8 %collective-permute-start.9 = (f32[8,896]{1,0:T(8,128)S(1)}, f32[8,896]{1,0:T(8,128)S(1)}, u32[]{:S(2)}, u32[]{:S(2)}) collective-permute-start(f32[8,896]{1,0:T(8,128)S(1)} %add.20), channel_id=1, source_target_pairs={{0,2},{1,3},{2,0},{3,1},{4,6},{5,7},{6,4},{7,5},{8,10},{9,11},{10,... | collective-permute-start | bytes 86024 | tf_op jit(solution)/shard_map/ppermute | solution.py:26
  28.1 2.1 %collective-permute-done.9 = f32[8,896]{1,0:T(8,128)S(1)} collective-permute-done((f32[8,896]{1,0:T(8,128)S(1)}, f32[8,896]{1,0:T(8,128)S(1)}, u32[]{:S(2)}, u32[]{:S(2)}) %collective-permute-start.9) | collective-permute-done | bytes 28704 | tf_op jit(solution)/shard_map/ppermute | solution.py:26
  30.2 2.8 %collective-permute-start.10 = (f32[8,896]{1,0:T(8,128)S(1)}, f32[8,896]{1,0:T(8,128)S(1)}, u32[]{:S(2)}, u32[]{:S(2)}) collective-permute-start(f32[8,896]{1,0:T(8,128)S(1)} %add.21), channel_id=1, source_target_pairs={{0,4},{1,5},{2,6},{3,7},{4,0},{5,1},{6,2},{7,3},{8,12},{9,13},{10,... | collective-permute-start | bytes 86024 | tf_op jit(solution)/shard_map/ppermute | solution.py:26
  33.0 2.0 %collective-permute-done.10 = f32[8,896]{1,0:T(8,128)S(1)} collective-permute-done((f32[8,896]{1,0:T(8,128)S(1)}, f32[8,896]{1,0:T(8,128)S(1)}, u32[]{:S(2)}, u32[]{:S(2)}) %collective-permute-start.10) | collective-permute-done | bytes 28704 | tf_op jit(solution)/shard_map/ppermute | solution.py:26
  35.6 4.8 %shard_map.108.refs_0_ = bf16[4096,512]{1,0:T(8,128)(2,1)} custom-call(bf16[4096,512]{1,0:T(8,128)(2,1)} %wt.7, bf16[64,512]{1,0:T(8,128)(2,1)} %get-tuple-element.75.after), custom_call_target="tpu_custom_call" | custom-call | flops 1 | bytes 1 | tf_op jit(solution)/shard_map/pallas_call | solution.py:89
  41.6 1.7 %collective-permute-start.2 = (bf16[256,512]{1,0:T(8,128)(2,1)S(1)}, bf16[256,512]{1,0:T(8,128)(2,1)S(1)}, u32[]{:S(2)}, u32[]{:S(2)}) collective-permute-start(bf16[256,512]{1,0:T(8,128)(2,1)S(1)} %copy-done.29), channel_id=1, source_target_pairs={{0,16},{8,24},{16,0},{24,8},{1,17},{9,25},{17,1},{25,9},{2,18},{10... | collective-permute-start | bytes 786440 | tf_op jit(solution)/shard_map/ppermute | solution.py:399
  43.3 1.5 collective-permute-start.1
  46.0 1.6 %slice.31.refs_0_ = bf16[2048,512]{1,0:T(8,128)(2,1)} slice(bf16[4096,512]{1,0:T(8,128)(2,1)S(1)} %copy-done.10), slice={[1280:3328], [0:512]} | slice | bytes 4194304 | tf_op jit(solution)/shard_map/slice | solution.py:415
  47.6 3.1 %collective-permute-done.2.refs_0_ = bf16[256,512]{1,0:T(8,128)(2,1)S(1)} collective-permute-done((bf16[256,512]{1,0:T(8,128)(2,1)S(1)}, bf16[256,512]{1,0:T(8,128)(2,1)S(1)}, u32[]{:S(2)}, u32[]{:S(2)}) %collective-permute-start.2) | collective-permute-done | bytes 262176 | tf_op jit(solution)/shard_map/ppermute | solution.py:399
  50.7 1.7 %collective-permute-start.11 = (bf16[2048,512]{1,0:T(8,128)(2,1)}, bf16[2048,512]{1,0:T(8,128)(2,1)}, u32[]{:S(2)}, u32[]{:S(2)}) collective-permute-start(bf16[2048,512]{1,0:T(8,128)(2,1)} %get-tuple-element.50), channel_id=1, source_target_pairs={{0,16},{8,24},{16,0},{24,8},{1,17},{9,25},{17,1},{25,9},{2,18},{10... | collective-permute-start | bytes 6291464 | tf_op jit(solution)/shard_map/ppermute | solution.py:399
  53.1 1.6 collective-permute-start.3
  54.7 3.4 %collective-permute-done.3 = bf16[2,64,512]{2,1,0:T(8,128)(2,1)S(1)} collective-permute-done((bf16[2,64,512]{2,1,0:T(8,128)(2,1)S(1)}, bf16[2,64,512]{2,1,0:T(8,128)(2,1)S(1)}, u32[]{:S(2)}, u32[]{:S(2)}) %collective-permute-start.3) | collective-permute-done | bytes 131104 | tf_op jit(solution)/shard_map/ppermute | solution.py:26
  58.1 2.7 %collective-permute-start.4 = (bf16[4,64,512]{2,1,0:T(8,128)(2,1)S(1)}, bf16[4,64,512]{2,1,0:T(8,128)(2,1)S(1)}, u32[]{:S(2)}, u32[]{:S(2)}) collective-permute-start(bf16[4,64,512]{2,1,0:T(8,128)(2,1)S(1)} %pad_maximum_fusion.2), channel_id=1, source_target_pairs={{0,4},{1,5},{2,6},{3,7},{4,0},{5,1},{6,2},{7,3},{8,12},{9,13},{10,... | collective-permute-start | bytes 786440 | tf_op jit(solution)/shard_map/ppermute | solution.py:26
  60.8 9.6 %collective-permute-done.4 = bf16[4,64,512]{2,1,0:T(8,128)(2,1)S(1)} collective-permute-done((bf16[4,64,512]{2,1,0:T(8,128)(2,1)S(1)}, bf16[4,64,512]{2,1,0:T(8,128)(2,1)S(1)}, u32[]{:S(2)}, u32[]{:S(2)}) %collective-permute-start.4) | collective-permute-done | bytes 262176 | tf_op jit(solution)/shard_map/ppermute | solution.py:26
  71.1 1.9 %collective-permute-done.6 = bf16[8,64,512]{2,1,0:T(8,128)(2,1)S(1)} collective-permute-done((bf16[8,64,512]{2,1,0:T(8,128)(2,1)S(1)}, bf16[8,64,512]{2,1,0:T(8,128)(2,1)S(1)}, u32[]{:S(2)}, u32[]{:S(2)}) %collective-permute-start.6) | collective-permute-done | bytes 524320 | tf_op jit(solution)/shard_map/ppermute | solution.py:26
  73.0 1.0 pad_maximum_fusion.left
  74.0 4.2 %reshape.32.rights = bf16[448,2048]{1,0:T(8,128)(2,1)} reshape(bf16[112,4,2048]{2,1,0:T(4,128)(2,1)} %param.15) | data formatting | bytes 3670016 | tf_op jit(solution)/shard_map/reshape | solution.py:437
  79.3 1.2 copy-done.19
  80.5 1.3 shard_map.104.left
  81.9 1.0 copy-done.3
  82.8 3.1 %copy-done.1 = bf16[896,4096]{1,0:T(8,128)(2,1)S(1)} copy-done((bf16[896,4096]{1,0:T(8,128)(2,1)S(1)}, bf16[896,4096]{1,0:T(8,128)(2,1)}, u32[]{:S(2)}) %copy-start.1) | copy-done | bytes 7340056
  85.9 1.2 copy-done.4
  87.1 1.0 copy-done.7
  88.2 2.2 %copy-done.11 = bf16[4096,512]{1,0:T(8,128)(2,1)S(1)} copy-done((bf16[4096,512]{1,0:T(8,128)(2,1)S(1)}, bf16[4096,512]{1,0:T(8,128)(2,1)}, u32[]{:S(2)}) %copy-start.11) | copy-done | bytes 4194328
  90.4 1.5 copy-done.12
  91.9 1.2 copy-done.16
  93.1 7.7 %shard_map.107 = (bf16[896,2048]{1,0:T(8,128)(2,1)}, bf16[4096,512]{1,0:T(8,128)(2,1)}, f32[8,128]{1,0:T(8,128)S(1)}) custom-call(s32[1]{0:T(128)} %bitcast.where, bf16[896,4096]{1,0:T(8,128)(2,1)S(1)} %copy-done.1, bf16[4096,512]{1,0:T(8,128)(2,1)S(1)} %copy-done.11, bf16[4096,128]{1,0:T(8,128)(2,1)S(1)} %copy-done.4, bf16[128,2048]{1,0:T(8,128)(2,1)S(1)} %copy-done.7, ...), custom_call_target="tpu_custom_call" | custom-call | flops 1 | bytes 1 | tf_op jit(solution)/shard_map/pallas_call | solution.py:307
  100.8 8.6 %shard_map.110 = (bf16[896,2048]{1,0:T(8,128)(2,1)}, f32[8,128]{1,0:T(8,128)S(1)}) custom-call(s32[1]{0:T(128)} %bitcast.4.where, bf16[896,4096]{1,0:T(8,128)(2,1)S(1)} %bitcast.8, bf16[4096,512]{1,0:T(8,128)(2,1)} %collective-permute-done.12.wt, bf16[4096,128]{1,0:T(8,128)(2,1)S(1)} %copy-done.4, ...), custom_call_target="tpu_custom_call", output_to_operand_aliasing={{0}: (8, {})} | custom-call | flops 1 | bytes 1 | tf_op jit(solution)/shard_map/pallas_call | solution.py:307
  111.9 3.1 %copy-done.2 = bf16[896,4096]{1,0:T(8,128)(2,1)S(1)} copy-done((bf16[896,4096]{1,0:T(8,128)(2,1)S(1)}, bf16[896,4096]{1,0:T(8,128)(2,1)}, u32[]{:S(2)}) %copy-start.2) | copy-done | bytes 7340056
  114.9 1.5 copy-done.14
  116.4 1.2 copy-done.18
  119.8 1.2 slice-done.3
  122.3 2.2 %shard_map.118.after.before = f32[896,512]{1,0:T(8,128)S(1)} custom-call(s32[1]{0:T(128)} %bitcast.5.where, bf16[896,4096]{1,0:T(8,128)(2,1)S(1)} %bitcast.10, bf16[768,512]{1,0:T(8,128)(2,1)} %get-tuple-element.56.wt, bf16[4096,128]{1,0:T(8,128)(2,1)S(1)} %copy-done.5, bf16[128,2048]{1,0:T(8,128)(2,1)S(1)} %copy-done.9, ...), custom_call_target="tpu_custom_call", output_to_operand_aliasing={{}: (5, {})} | custom-call | flops 1 | bytes 1 | tf_op jit(solution)/shard_map/pallas_call | solution.py:307
  124.6 1.1 shard_map.119.refs_1_.after.before
  127.2 4.2 %shard_map.123.after.before = f32[896,512]{1,0:T(8,128)S(1)} custom-call(s32[1]{0:T(128)} %bitcast.5.where, bf16[896,4096]{1,0:T(8,128)(2,1)S(1)} %bitcast.10, bf16[2048,512]{1,0:T(8,128)(2,1)} %get-tuple-element.64.wt, bf16[4096,128]{1,0:T(8,128)(2,1)S(1)} %copy-done.5, bf16[128,2048]{1,0:T(8,128)(2,1)S(1)} %copy-done.9, ...), custom_call_target="tpu_custom_call", output_to_operand_aliasing={{}: (5, {})} | custom-call | flops 1 | bytes 1 | tf_op jit(solution)/shard_map/pallas_call | solution.py:307
  131.5 2.7 %shard_map.124.refs_1_.after.before = f32[896,512]{1,0:T(8,128)S(1)} custom-call(s32[1]{0:T(128)} %bitcast.3.where, bf16[896,4096]{1,0:T(8,128)(2,1)S(1)} %bitcast.10, bf16[2048,512]{1,0:T(8,128)(2,1)S(1)} %collective-permute-done.18.wt, bf16[4096,128]{1,0:T(8,128)(2,1)S(1)} %copy-done.5, ...), custom_call_target="tpu_custom_call", output_to_operand_aliasing={{}: (5, {})} | custom-call | flops 1 | bytes 1 | tf_op jit(solution)/shard_map/pallas_call | solution.py:307
  134.2 6.8 %collective-permute-done.17.refs_0_ = bf16[512,512]{1,0:T(8,128)(2,1)S(1)} collective-permute-done((bf16[512,512]{1,0:T(8,128)(2,1)S(1)}, bf16[512,512]{1,0:T(8,128)(2,1)S(1)}, u32[]{:S(2)}, u32[]{:S(2)}) %collective-permute-start.17) | collective-permute-done | bytes 524320 | tf_op jit(solution)/shard_map/ppermute | solution.py:399
  146.0 6.4 %collective-permute-done.16.refs_0_ = bf16[256,512]{1,0:T(8,128)(2,1)S(1)} collective-permute-done((bf16[256,512]{1,0:T(8,128)(2,1)S(1)}, bf16[256,512]{1,0:T(8,128)(2,1)S(1)}, u32[]{:S(2)}, u32[]{:S(2)}) %collective-permute-start.16) | collective-permute-done | bytes 262176 | tf_op jit(solution)/shard_map/ppermute | solution.py:399
  153.6 2.3 %shard_map.131.acts = bf16[896,2048]{1,0:T(8,128)(2,1)} custom-call(s32[1]{0:T(128)} %bitcast.5.where, bf16[896,4096]{1,0:T(8,128)(2,1)S(1)} %bitcast.10, bf16[256,512]{1,0:T(8,128)(2,1)S(1)} %get-tuple-element.68.wt, bf16[4096,128]{1,0:T(8,128)(2,1)S(1)} %copy-done.5, bf16[128,2048]{1,0:T(8,128)(2,1)S(1)} %copy-done.9, ...), custom_call_target="tpu_custom_call", output_to_operand_aliasing={{}: (7, {})} | custom-call | flops 1 | bytes 1 | tf_op jit(solution)/shard_map/pallas_call | solution.py:307
  155.9 2.3 %shard_map.132 = bf16[896,2048]{1,0:T(8,128)(2,1)} custom-call(s32[1]{0:T(128)} %bitcast.3.where, bf16[896,4096]{1,0:T(8,128)(2,1)S(1)} %bitcast.10, bf16[256,512]{1,0:T(8,128)(2,1)S(1)} %collective-permute-done.20.wt, bf16[4096,128]{1,0:T(8,128)(2,1)S(1)} %copy-done.5, bf16[128,2048]{1,0:T(8,128)(2,1)S(1)} %copy-done.9, ...), custom_call_target="tpu_custom_call", output_to_operand_aliasing={{}: (7, {})} | custom-call | flops 1 | bytes 1 | tf_op jit(solution)/shard_map/pallas_call | solution.py:307
  (123 shorter events, 20.1 us)
Async XLA Ops:
  4.1 13.1 %collective-permute-start = (bf16[416,512]{1,0:T(8,128)(2,1)}, bf16[416,512]{1,0:T(8,128)(2,1)S(1)}, u32[]{:S(2)}, u32[]{:S(2)}) collective-permute-start(bf16[416,512]{1,0:T(8,128)(2,1)} %get-tuple-element.37), channel_id=1, source_target_pairs={{0,16},{8,24},{16,0},{24,8},{1,17},{9,25},{17,1},{25,9},{2,18},{10... | collective-permute-start | bytes 1277960 | tf_op jit(solution)/shard_map/ppermute | solution.py:399
  7.1 1.7 %copy-start.25 = (bf16[112,4,512]{2,1,0:T(4,128)(2,1)S(1)}, bf16[112,4,512]{2,1,0:T(4,128)(2,1)}, u32[]{:S(2)}) copy-start(bf16[112,4,512]{2,1,0:T(4,128)(2,1)} %param.14) | copy-start | bytes 1376260
  7.1 10.0 %copy-start.24 = (bf16[32,2048]{1,0:T(8,128)(2,1)S(1)}, bf16[32,2048]{1,0:T(8,128)(2,1)}, u32[]{:S(2)}) copy-start(bf16[32,2048]{1,0:T(8,128)(2,1)} %get-tuple-element.48) | copy-start | bytes 393220
  17.1 5.2 %copy-start.26 = (bf16[416,512]{1,0:T(8,128)(2,1)}, bf16[416,512]{1,0:T(8,128)(2,1)S(1)}, u32[]{:S(2)}) copy-start(bf16[416,512]{1,0:T(8,128)(2,1)S(1)} %collective-permute-done) | copy-start | bytes 1277956
  17.2 23.2 %collective-permute-start.7 = (bf16[64,2048]{1,0:T(8,128)(2,1)S(1)}, bf16[64,2048]{1,0:T(8,128)(2,1)S(1)}, u32[]{:S(2)}, u32[]{:S(2)}) collective-permute-start(bf16[64,2048]{1,0:T(8,128)(2,1)S(1)} %maximum_maximum_fusion), channel_id=1, source_target_pairs={{0,8},{8,0},{16,24},{24,16},{1,9},{9,1},{17,25},{25,17},{2,10},{10... | collective-permute-start | bytes 786440 | tf_op jit(solution)/shard_map/ppermute | solution.py:26
  17.4 3.1 %copy-start = (bf16[896,4096]{1,0:T(8,128)(2,1)S(1)}, bf16[896,4096]{1,0:T(8,128)(2,1)}, u32[]{:S(2)}) copy-start(bf16[896,4096]{1,0:T(8,128)(2,1)} %tok.29) | copy-start | bytes 22020100
  21.1 13.8 %copy-start.28 = (bf16[32,512]{1,0:T(8,128)(2,1)S(1)}, bf16[32,512]{1,0:T(8,128)(2,1)}, u32[]{:S(2)}) copy-start(bf16[32,512]{1,0:T(8,128)(2,1)} %get-tuple-element.36) | copy-start | bytes 98308
  22.4 3.9 %collective-permute-start.8 = (f32[8,896]{1,0:T(8,128)S(1)}, f32[8,896]{1,0:T(8,128)S(1)}, u32[]{:S(2)}, u32[]{:S(2)}) collective-permute-start(f32[8,896]{1,0:T(8,128)S(1)} %shard_map.105), channel_id=1, source_target_pairs={{0,1},{1,0},{2,3},{3,2},{4,5},{5,4},{6,7},{7,6},{8,9},{9,8},{10,11... | collective-permute-start | bytes 86024 | tf_op jit(solution)/shard_map/ppermute | solution.py:26
  26.3 3.9 %collective-permute-start.9 = (f32[8,896]{1,0:T(8,128)S(1)}, f32[8,896]{1,0:T(8,128)S(1)}, u32[]{:S(2)}, u32[]{:S(2)}) collective-permute-start(f32[8,896]{1,0:T(8,128)S(1)} %add.20), channel_id=1, source_target_pairs={{0,2},{1,3},{2,0},{3,1},{4,6},{5,7},{6,4},{7,5},{8,10},{9,11},{10,... | collective-permute-start | bytes 86024 | tf_op jit(solution)/shard_map/ppermute | solution.py:26
  30.2 4.8 %collective-permute-start.10 = (f32[8,896]{1,0:T(8,128)S(1)}, f32[8,896]{1,0:T(8,128)S(1)}, u32[]{:S(2)}, u32[]{:S(2)}) collective-permute-start(f32[8,896]{1,0:T(8,128)S(1)} %add.21), channel_id=1, source_target_pairs={{0,4},{1,5},{2,6},{3,7},{4,0},{5,1},{6,2},{7,3},{8,12},{9,13},{10,... | collective-permute-start | bytes 86024 | tf_op jit(solution)/shard_map/ppermute | solution.py:26
  40.5 4.4 %copy-start.10 = (bf16[4096,512]{1,0:T(8,128)(2,1)S(1)}, bf16[4096,512]{1,0:T(8,128)(2,1)}, u32[]{:S(2)}) copy-start(bf16[4096,512]{1,0:T(8,128)(2,1)} %wt.7) | copy-start | bytes 12582916
  40.5 4.4 %copy-start.23 = (f32[8,128]{1,0:T(8,128)S(1)}, f32[8,128]{1,0:T(8,128)}, u32[]{:S(2)}) copy-start(f32[8,128]{1,0:T(8,128)} %get-tuple-element.43.refs_1_.after) | copy-start | bytes 12292
  41.2 59.5 %collective-permute-start.12 = (bf16[4096,512]{1,0:T(8,128)(2,1)}, bf16[4096,512]{1,0:T(8,128)(2,1)}, u32[]{:S(2)}, u32[]{:S(2)}) collective-permute-start(bf16[4096,512]{1,0:T(8,128)(2,1)} %get-tuple-element.52), channel_id=1, source_target_pairs={{0,8},{8,0},{16,24},{24,16},{1,9},{9,1},{17,25},{25,17},{2,10},{10... | collective-permute-start | bytes 12582920 | tf_op jit(solution)/shard_map/ppermute | solution.py:26
  41.6 9.1 %collective-permute-start.2 = (bf16[256,512]{1,0:T(8,128)(2,1)S(1)}, bf16[256,512]{1,0:T(8,128)(2,1)S(1)}, u32[]{:S(2)}, u32[]{:S(2)}) collective-permute-start(bf16[256,512]{1,0:T(8,128)(2,1)S(1)} %copy-done.29), channel_id=1, source_target_pairs={{0,16},{8,24},{16,0},{24,8},{1,17},{9,25},{17,1},{25,9},{2,18},{10... | collective-permute-start | bytes 786440 | tf_op jit(solution)/shard_map/ppermute | solution.py:399
  43.3 4.3 %collective-permute-start.1 = (bf16[1,64,512]{2,1,0:T(8,128)(2,1)S(1)}, bf16[1,64,512]{2,1,0:T(8,128)(2,1)S(1)}, u32[]{:S(2)}, u32[]{:S(2)}) collective-permute-start(bf16[1,64,512]{2,1,0:T(8,128)(2,1)S(1)} %get-tuple-element.76), channel_id=1, source_target_pairs={{0,1},{1,0},{2,3},{3,2},{4,5},{5,4},{6,7},{7,6},{8,9},{9,8},{10,11... | collective-permute-start | bytes 196616 | tf_op jit(solution)/shard_map/ppermute | solution.py:26
  45.5 24.9 %collective-permute-start.5 = (bf16[768,512]{1,0:T(8,128)(2,1)S(1)}, bf16[768,512]{1,0:T(8,128)(2,1)}, u32[]{:S(2)}, u32[]{:S(2)}) collective-permute-start(bf16[768,512]{1,0:T(8,128)(2,1)S(1)} %get-tuple-element.44), channel_id=1, source_target_pairs={{0,16},{8,24},{16,0},{24,8},{1,17},{9,25},{17,1},{25,9},{2,18},{10... | collective-permute-start | bytes 2359304 | tf_op jit(solution)/shard_map/ppermute | solution.py:399
  50.7 75.0 %collective-permute-start.11 = (bf16[2048,512]{1,0:T(8,128)(2,1)}, bf16[2048,512]{1,0:T(8,128)(2,1)}, u32[]{:S(2)}, u32[]{:S(2)}) collective-permute-start(bf16[2048,512]{1,0:T(8,128)(2,1)} %get-tuple-element.50), channel_id=1, source_target_pairs={{0,16},{8,24},{16,0},{24,8},{1,17},{9,25},{17,1},{25,9},{2,18},{10... | collective-permute-start | bytes 6291464 | tf_op jit(solution)/shard_map/ppermute | solution.py:399
  53.1 5.0 %collective-permute-start.3 = (bf16[2,64,512]{2,1,0:T(8,128)(2,1)S(1)}, bf16[2,64,512]{2,1,0:T(8,128)(2,1)S(1)}, u32[]{:S(2)}, u32[]{:S(2)}) collective-permute-start(bf16[2,64,512]{2,1,0:T(8,128)(2,1)S(1)} %get-tuple-element.42), channel_id=1, source_target_pairs={{0,2},{1,3},{2,0},{3,1},{4,6},{5,7},{6,4},{7,5},{8,10},{9,11},{10,... | collective-permute-start | bytes 393224 | tf_op jit(solution)/shard_map/ppermute | solution.py:26
  58.1 12.3 %collective-permute-start.4 = (bf16[4,64,512]{2,1,0:T(8,128)(2,1)S(1)}, bf16[4,64,512]{2,1,0:T(8,128)(2,1)S(1)}, u32[]{:S(2)}, u32[]{:S(2)}) collective-permute-start(bf16[4,64,512]{2,1,0:T(8,128)(2,1)S(1)} %pad_maximum_fusion.2), channel_id=1, source_target_pairs={{0,4},{1,5},{2,6},{3,7},{4,0},{5,1},{6,2},{7,3},{8,12},{9,13},{10,... | collective-permute-start | bytes 786440 | tf_op jit(solution)/shard_map/ppermute | solution.py:26
  70.4 2.6 %copy-start.20 = (bf16[512,512]{1,0:T(8,128)(2,1)}, bf16[512,512]{1,0:T(8,128)(2,1)S(1)}, u32[]{:S(2)}) copy-start(bf16[512,512]{1,0:T(8,128)(2,1)S(1)} %get-tuple-element.62) | copy-start | bytes 1572868
  71.1 1.9 %collective-permute-start.6 = (bf16[8,64,512]{2,1,0:T(8,128)(2,1)S(1)}, bf16[8,64,512]{2,1,0:T(8,128)(2,1)S(1)}, u32[]{:S(2)}, u32[]{:S(2)}) collective-permute-start(bf16[8,64,512]{2,1,0:T(8,128)(2,1)S(1)} %get-tuple-element.47), channel_id=1, source_target_pairs={{0,8},{8,0},{16,24},{24,16},{1,9},{9,1},{17,25},{25,17},{2,10},{10... | collective-permute-start | bytes 1572872 | tf_op jit(solution)/shard_map/ppermute | solution.py:26
  74.0 26.7 %slice-start = ((s8[7340032]{0:T(1024)(128)(4,1)}), s8[3145728]{0:T(1024)(128)(4,1)S(1)}, s32[]{:S(2)}) async-start(s8[7340032]{0:T(1024)(128)(4,1)} %bitcast.7), calls=%async_computation | async-start | bytes 6291456
  79.3 1.2 copy-start.19
  82.8 3.1 %copy-start.1 = (bf16[896,4096]{1,0:T(8,128)(2,1)S(1)}, bf16[896,4096]{1,0:T(8,128)(2,1)}, u32[]{:S(2)}) copy-start(bf16[896,4096]{1,0:T(8,128)(2,1)} %tok.29) | copy-start | bytes 22020100
  85.9 1.2 copy-start.4
  88.2 2.2 %copy-start.11 = (bf16[4096,512]{1,0:T(8,128)(2,1)S(1)}, bf16[4096,512]{1,0:T(8,128)(2,1)}, u32[]{:S(2)}) copy-start(bf16[4096,512]{1,0:T(8,128)(2,1)} %wt.7) | copy-start | bytes 12582916
  90.4 1.5 copy-start.12
  91.9 1.2 copy-start.16
  93.1 7.7 %slice-start.1 = ((s8[7340032]{0:T(1024)(128)(4,1)}), s8[4194304]{0:T(1024)(128)(4,1)S(1)}, s32[]{:S(2)}) async-start(s8[7340032]{0:T(1024)(128)(4,1)} %bitcast.7), calls=%async_computation.1 | async-start | bytes 8388608
  93.1 7.7 %copy-start.8 = (bf16[128,2048]{1,0:T(8,128)(2,1)S(1)}, bf16[128,2048]{1,0:T(8,128)(2,1)}, u32[]{:S(2)}) copy-start(bf16[128,2048]{1,0:T(8,128)(2,1)} %copy-done.6) | copy-start | bytes 1572868
  93.1 7.7 %copy-start.13 = (bf16[448,2048]{1,0:T(8,128)(2,1)S(1)}, bf16[448,2048]{1,0:T(8,128)(2,1)}, u32[]{:S(2)}) copy-start(bf16[448,2048]{1,0:T(8,128)(2,1)} %reshape.32.rights) | copy-start | bytes 5505028
  93.1 7.7 %copy-start.17 = (bf16[896,448]{1,0:T(8,128)(2,1)S(1)}, bf16[896,448]{1,0:T(8,128)(2,1)}, u32[]{:S(2)}) copy-start(bf16[896,448]{1,0:T(8,128)(2,1)} %copy-done.15) | copy-start | bytes 2408452
  100.8 9.4 %copy-start.27 = (bf16[416,512]{1,0:T(8,128)(2,1)S(1)}, bf16[416,512]{1,0:T(8,128)(2,1)}, u32[]{:S(2)}) copy-start(bf16[416,512]{1,0:T(8,128)(2,1)} %copy-done.26) | copy-start | bytes 1277956
  109.4 2.5 %copy-start.5 = (bf16[4096,128]{1,0:T(8,128)(2,1)S(1)}, bf16[4096,128]{1,0:T(8,128)(2,1)}, u32[]{:S(2)}) copy-start(bf16[4096,128]{1,0:T(8,128)(2,1)} %copy-done.3) | copy-start | bytes 3145732
  109.4 2.5 %copy-start.9 = (bf16[128,2048]{1,0:T(8,128)(2,1)S(1)}, bf16[128,2048]{1,0:T(8,128)(2,1)}, u32[]{:S(2)}) copy-start(bf16[128,2048]{1,0:T(8,128)(2,1)} %copy-done.6) | copy-start | bytes 1572868
  110.0 14.6 %collective-permute-start.13 = (bf16[768,512]{1,0:T(8,128)(2,1)}, bf16[768,512]{1,0:T(8,128)(2,1)S(1)}, u32[]{:S(2)}, u32[]{:S(2)}) collective-permute-start(bf16[768,512]{1,0:T(8,128)(2,1)} %get-tuple-element.56.wt), channel_id=1, source_target_pairs={{0,8},{8,0},{16,24},{24,16},{1,9},{9,1},{17,25},{25,17},{2,10},{10... | collective-permute-start | bytes 2359304 | tf_op jit(solution)/shard_map/ppermute | solution.py:26
  110.7 7.8 %collective-permute-start.15 = (bf16[256,512]{1,0:T(8,128)(2,1)S(1)}, bf16[256,512]{1,0:T(8,128)(2,1)S(1)}, u32[]{:S(2)}, u32[]{:S(2)}) collective-permute-start(bf16[256,512]{1,0:T(8,128)(2,1)S(1)} %get-tuple-element.59.wt), channel_id=1, source_target_pairs={{0,8},{8,0},{16,24},{24,16},{1,9},{9,1},{17,25},{25,17},{2,10},{10... | collective-permute-start | bytes 786440 | tf_op jit(solution)/shard_map/ppermute | solution.py:26
  111.7 10.0 %collective-permute-start.14 = (bf16[256,512]{1,0:T(8,128)(2,1)S(1)}, bf16[256,512]{1,0:T(8,128)(2,1)S(1)}, u32[]{:S(2)}, u32[]{:S(2)}) collective-permute-start(bf16[256,512]{1,0:T(8,128)(2,1)S(1)} %get-tuple-element.58.wt), channel_id=1, source_target_pairs={{0,8},{8,0},{16,24},{24,16},{1,9},{9,1},{17,25},{25,17},{2,10},{10... | collective-permute-start | bytes 786440 | tf_op jit(solution)/shard_map/ppermute | solution.py:26
  111.9 3.1 %copy-start.2 = (bf16[896,4096]{1,0:T(8,128)(2,1)S(1)}, bf16[896,4096]{1,0:T(8,128)(2,1)}, u32[]{:S(2)}) copy-start(bf16[896,4096]{1,0:T(8,128)(2,1)} %tok.29) | copy-start | bytes 22020100
  114.9 1.5 copy-start.14
  116.4 1.2 copy-start.18
  117.6 2.2 %slice-start.2 = ((s8[7340032]{0:T(1024)(128)(4,1)}), s8[4194304]{0:T(1024)(128)(4,1)S(1)}, s32[]{:S(2)}) async-start(s8[7340032]{0:T(1024)(128)(4,1)} %bitcast.9), calls=%async_computation.2 | async-start | bytes 8388608
  118.6 2.4 %slice-start.3 = ((s8[7340032]{0:T(1024)(128)(4,1)}), s8[3145728]{0:T(1024)(128)(4,1)S(1)}, s32[]{:S(2)}) async-start(s8[7340032]{0:T(1024)(128)(4,1)} %bitcast.9), calls=%async_computation.3 | async-start | bytes 6291456
  126.3 5.1 %collective-permute-start.18 = (bf16[2048,512]{1,0:T(8,128)(2,1)}, bf16[2048,512]{1,0:T(8,128)(2,1)S(1)}, u32[]{:S(2)}, u32[]{:S(2)}) collective-permute-start(bf16[2048,512]{1,0:T(8,128)(2,1)} %get-tuple-element.64.wt), channel_id=1, source_target_pairs={{0,8},{8,0},{16,24},{24,16},{1,9},{9,1},{17,25},{25,17},{2,10},{10... | collective-permute-start | bytes 6291464 | tf_op jit(solution)/shard_map/ppermute | solution.py:26
  126.8 14.2 %collective-permute-start.17 = (bf16[512,512]{1,0:T(8,128)(2,1)S(1)}, bf16[512,512]{1,0:T(8,128)(2,1)S(1)}, u32[]{:S(2)}, u32[]{:S(2)}) collective-permute-start(bf16[512,512]{1,0:T(8,128)(2,1)S(1)} %copy-done.21), channel_id=1, source_target_pairs={{0,16},{8,24},{16,0},{24,8},{1,17},{9,25},{17,1},{25,9},{2,18},{10... | collective-permute-start | bytes 1572872 | tf_op jit(solution)/shard_map/ppermute | solution.py:399
  142.1 3.0 %collective-permute-start.19 = (bf16[512,512]{1,0:T(8,128)(2,1)S(1)}, bf16[512,512]{1,0:T(8,128)(2,1)S(1)}, u32[]{:S(2)}, u32[]{:S(2)}) collective-permute-start(bf16[512,512]{1,0:T(8,128)(2,1)S(1)} %get-tuple-element.66.wt), channel_id=1, source_target_pairs={{0,8},{8,0},{16,24},{24,16},{1,9},{9,1},{17,25},{25,17},{2,10},{10... | collective-permute-start | bytes 1572872 | tf_op jit(solution)/shard_map/ppermute | solution.py:26
  143.7 8.7 %collective-permute-start.16 = (bf16[256,512]{1,0:T(8,128)(2,1)S(1)}, bf16[256,512]{1,0:T(8,128)(2,1)S(1)}, u32[]{:S(2)}, u32[]{:S(2)}) collective-permute-start(bf16[256,512]{1,0:T(8,128)(2,1)S(1)} %get-tuple-element.61), channel_id=1, source_target_pairs={{0,16},{8,24},{16,0},{24,8},{1,17},{9,25},{17,1},{25,9},{2,18},{10... | collective-permute-start | bytes 786440 | tf_op jit(solution)/shard_map/ppermute | solution.py:399
  153.6 2.3 %collective-permute-start.20 = (bf16[256,512]{1,0:T(8,128)(2,1)S(1)}, bf16[256,512]{1,0:T(8,128)(2,1)S(1)}, u32[]{:S(2)}, u32[]{:S(2)}) collective-permute-start(bf16[256,512]{1,0:T(8,128)(2,1)S(1)} %get-tuple-element.68.wt), channel_id=1, source_target_pairs={{0,8},{8,0},{16,24},{24,16},{1,9},{9,1},{17,25},{25,17},{2,10},{10... | collective-permute-start | bytes 786440 | tf_op jit(solution)/shard_map/ppermute | solution.py:26
  (7 other events, 6.6 us)

commit v2 on v1

v2 whole, which is shorter than its diff:
```python
import functools
import math

import jax
import jax.numpy as jnp
from jax import lax
from jax.experimental import pallas as pl
from jax.experimental.pallas import tpu as pltpu
from jax.sharding import PartitionSpec as P

noise_scale = 0.5
PIECES = (1, 4, 9, 2)
LIMIT = 20 * 2**20
WIDE = 58 * 2**20


def params(limit=LIMIT):
    return pltpu.CompilerParams(dimension_semantics=("arbitrary",), vmem_limit_bytes=limit)


def cost():
    return pl.CostEstimate(flops=1, bytes_accessed=1, transcendentals=0)


def swap(array, axis, bit):
    return lax.ppermute(array, axis, [(i, i ^ bit) for i in range(lax.axis_size(axis))])


def bits(size, least=1):
    bit = least
    while bit < size:
        yield bit
        bit *= 2


MARK = jax.ShapeDtypeStruct((8, 128), jnp.float32)


def vmem():
    return pl.BlockSpec(memory_space=pltpu.VMEM)


def anywhere():
    return pl.BlockSpec(memory_space=pl.ANY)


def gate_kernel(mark_at, *refs):
    refs[mark_at][...] = jnp.zeros(MARK.shape, MARK.dtype)


def gate(array, *after):
    return pl.pallas_call(
        functools.partial(gate_kernel, len(after) + 2),
        in_specs=[anywhere()] * (1 + len(after)),
        out_specs=[anywhere(), vmem()],
        out_shape=[jax.ShapeDtypeStruct(array.shape, array.dtype), MARK],
        input_output_aliases={0: 0},
        compiler_params=pltpu.CompilerParams(vmem_limit_bytes=2**20),
        cost_estimate=cost(),
    )(array, *after)


def cut_kernel(start, wt, after, out, mark, sem):
    copy = pltpu.make_async_copy(wt.at[pl.ds(start, out.shape[0])], out, sem)
    copy.start()
    copy.wait()
    mark[...] = jnp.zeros(MARK.shape, MARK.dtype)


def cut(weight, start, depth, after):
    return pl.pallas_call(
        functools.partial(cut_kernel, start),
        in_specs=[anywhere()] * 2,
        out_specs=[vmem()] * 2,
        out_shape=[jax.ShapeDtypeStruct((depth, weight.shape[1]), weight.dtype), MARK],
        scratch_shapes=[pltpu.SemaphoreType.DMA],
        compiler_params=pltpu.CompilerParams(vmem_limit_bytes=WIDE - 2 * depth * weight.shape[1]),
        cost_estimate=cost(),
    )(weight, after)


def pick_kernel(
    factor, picked, shaping, lefts, rights, after, packed, left, right, mark, some_left, some_right, sems
):
    chosen, width = picked.shape[1], packed.shape[1]
    tall = chosen * lefts.shape[1]
    copies = []
    for slot in range(chosen):
        member = picked[0, slot]
        for source, kept in ((lefts, some_left), (rights, some_right)):
            sem = sems.at[len(copies)]
            copies.append(pltpu.make_async_copy(source.at[member], kept.at[slot], sem))
    for copy in copies:
        copy.start()
    for copy in copies:
        copy.wait()
    scaled, plain = [], []
    for slot in range(chosen):
        scale = shaping[0, slot] * factor
        scaled.append(some_left[slot].astype(jnp.float32) * scale)
        plain.append(some_right[slot].astype(jnp.float32))
    scaled = jnp.concatenate(scaled, 0).astype(jnp.bfloat16)
    plain = jnp.concatenate(plain, 0).astype(jnp.bfloat16)
    left[...] = scaled
    right[...] = plain
    at = 0
    for whole in (scaled, plain):
        for block in range(whole.shape[1] // width):
            packed[at : at + tall, :] = whole[:, block * width : (block + 1) * width]
            at += tall
    mark[...] = jnp.zeros(MARK.shape, MARK.dtype)


def pick(factor, selected, shaping, old_left, old_right, width, after):
    chosen, rank = selected.shape[1], old_left.shape[1]
    tall = chosen * rank
    slab, wide, kind = old_left.shape[2], old_right.shape[2], old_left.dtype
    return pl.pallas_call(
        functools.partial(pick_kernel, factor),
        in_specs=[pl.BlockSpec(memory_space=pltpu.SMEM)] * 2 + [anywhere()] * 3,
        out_specs=[vmem()] * 4,
        out_shape=[
            jax.ShapeDtypeStruct((tall * (slab + wide) // width, width), kind),
            jax.ShapeDtypeStruct((tall, slab), kind),
            jax.ShapeDtypeStruct((tall, wide), kind),
            MARK,
        ],
        scratch_shapes=[
            pltpu.VMEM((chosen, rank, slab), kind),
            pltpu.VMEM((chosen, rank, wide), kind),
            pltpu.SemaphoreType.DMA((2 * chosen,)),
        ],
        compiler_params=pltpu.CompilerParams(vmem_limit_bytes=WIDE),
        cost_estimate=cost(),
    )(selected, shaping, old_left, old_right, after)


def unpack(packed, tall, slab, wide):
    width = packed.shape[1]
    blocks = [slab // width, wide // width]
    got, at = [], 0
    for count in blocks:
        got.append(
            jnp.concatenate([packed[at + tall * i : at + tall * (i + 1)] for i in range(count)], 1)
        )
        at += tall * count
    return got


def mine(shape, rank, each):
    row = lax.broadcasted_iota(jnp.int32, shape, 0)
    token = lax.broadcasted_iota(jnp.int32, shape, 1)
    return lax.div(row, rank) == lax.div(token, each)


def proj_kernel(rank, each, where, left, tok, after, out):
    full = lax.dot_general(
        left[...], tok[...], (((1,), (1,)), ((), ())), preferred_element_type=jnp.float32
    )
    full = jnp.where(mine(full.shape, rank, each), full, 0.0)
    out[...] = full.reshape(-1, *out.shape).sum(0)


def project(tokens, lefts, rank, each, where, after):
    rows, slab = tokens.shape[0], lefts.shape[1]
    return pl.pallas_call(
        functools.partial(proj_kernel, rank, each),
        grid_spec=pltpu.PrefetchScalarGridSpec(
            num_scalar_prefetch=1,
            grid=(1,),
            in_specs=[
                pl.BlockSpec(lefts.shape, lambda k, at: (0, 0)),
                pl.BlockSpec((rows, slab), lambda k, at: (0, at[1])),
                pl.BlockSpec(memory_space=pl.ANY),
            ],
            out_specs=pl.BlockSpec((2 * rank, rows), lambda k, at: (0, 0)),
        ),
        out_shape=jax.ShapeDtypeStruct((2 * rank, rows), jnp.float32),
        compiler_params=params(WIDE),
        cost_estimate=cost(),
    )(where, lefts, tokens, after)


def turn_kernel(where, left, out):
    out[...] = left[...].T


def turn(left, where):
    blocks, sels, slab = left.shape
    return pl.pallas_call(
        turn_kernel,
        grid_spec=pltpu.PrefetchScalarGridSpec(
            num_scalar_prefetch=1,
            grid=(blocks,),
            in_specs=[pl.BlockSpec((None, sels, slab), lambda k, at: (k ^ at[1], 0, 0))],
            out_specs=pl.BlockSpec((slab, sels), lambda k, at: (k, 0)),
        ),
        out_shape=jax.ShapeDtypeStruct((blocks * slab, sels), left.dtype),
        compiler_params=params(),
        cost_estimate=cost(),
    )(where, left)


def spread_kernel(rank, each, proj, out):
    narrow = proj[...].astype(jnp.bfloat16).astype(jnp.float32)
    full = jnp.tile(narrow, (out.shape[1] // narrow.shape[0], 1))
    out[...] = jnp.where(mine(full.shape, rank, each), full, 0.0).T.astype(jnp.bfloat16)


def spread_out(proj, members, rank, each):
    return pl.pallas_call(
        functools.partial(spread_kernel, rank, each),
        in_specs=[pl.BlockSpec(memory_space=pltpu.VMEM)],
        out_specs=pl.BlockSpec(memory_space=pltpu.VMEM),
        out_shape=jax.ShapeDtypeStruct((proj.shape[1], members * rank), jnp.bfloat16),
        compiler_params=pltpu.CompilerParams(vmem_limit_bytes=LIMIT),
        cost_estimate=cost(),
    )(proj)


def columns(ref, at, width):
    return ref[:, pl.ds(pl.multiple_of(at * width, width), width)]


def refresh(wt, left, right):
    delta = jnp.dot(left, right, preferred_element_type=jnp.float32)
    return (wt.astype(jnp.float32) + delta).astype(jnp.bfloat16)


def finish(total):
    return (jnp.maximum(total, 0.0) ** 2).astype(jnp.bfloat16)


def begin(scale, spread, rights):
    return scale * jnp.dot(spread, rights, preferred_element_type=jnp.float32)


def full_kernel(scale, keep, begun, where, tok, wt, left, right, spread, rights, *refs):
    out, mark, held = refs[1 if begun else 2], refs[-2], refs[-1]
    step = pl.program_id(0)

    @pl.when(step == 0)
    def _():
        mark[...] = jnp.zeros(MARK.shape, MARK.dtype)
        held[...] = begin(scale, spread[...], rights[...])

    fresh = refresh(wt[...], left[...], right[...])
    if keep:
        refs[-3][...] = fresh
    held[...] += jnp.dot(tok[...], fresh, preferred_element_type=jnp.float32)

    @pl.when(step == pl.num_programs(0) - 1)
    def _():
        out[...] = finish(held[...])


def product(start, where, tok, wt, left, right):
    unit, width = wt.shape
    fresh = refresh(wt[...], left[start : start + unit, :], columns(right, where[0], width))

    def rows(at, size):
        some = tok[at : at + size, start : start + unit]
        return jnp.dot(some, fresh, preferred_element_type=jnp.float32)

    return rows


def sum_kernel(scale, start, where, tok, wt, left, right, *refs):
    out = refs[-1]
    if start == 0:
        before = begin(scale, refs[0][...], columns(refs[1], where[0], wt.shape[1]))
    else:
        before = refs[0][...]
    out[...] = before + product(start, where, tok, wt, left, right)(0, tok.shape[0])


def last_kernel(start, where, tok, wt, left, right, before, acts, out, kept, sems):
    width = wt.shape[1]
    got = product(start, where, tok, wt, left, right)
    part = kept.shape[0] // 2
    place = pl.ds(pl.multiple_of(where[0] * width, width), width)
    copies = []
    for half in range(2):
        rows = pl.ds(half * part, part)
        kept[rows, :] = finish(before[rows, :] + got(half * part, part))
        copies.append(pltpu.make_async_copy(kept.at[rows], out.at[rows, place], sems.at[half]))
        copies[-1].start()
    for copy in copies:
        copy.wait()


def call(
    kernel, where, grid, specs, args, out_specs, out_shape, aliases=None, scratch=(), limit=LIMIT
):
    return pl.pallas_call(
        kernel,
        grid_spec=pltpu.PrefetchScalarGridSpec(
            num_scalar_prefetch=1,
            grid=grid,
            in_specs=specs,
            out_specs=out_specs,
            scratch_shapes=list(scratch),
        ),
        out_shape=out_shape,
        input_output_aliases=aliases or {},
        compiler_params=params(limit),
        cost_estimate=cost(),
    )(where, *args)


def run_block(where, tokens, wt, left, right, start, scale, spread, rights, acts, before, after, keep):
    rows = tokens.shape[0]
    depth, width = wt.shape
    first, last, begun = start == 0, acts is not None, isinstance(acts, tuple)
    tile = pl.BlockSpec((rows, width), lambda k, at: (0, at[0]))
    if first and last:
        unit = depth // 4
        block = pl.BlockSpec((unit, width), lambda k, at: (k, 0))
        specs = [
            pl.BlockSpec((rows, unit), lambda k, at: (0, k)),
            block,
            pl.BlockSpec((unit, left.shape[1]), lambda k, at: (k, 0)),
            pl.BlockSpec((right.shape[0], width), lambda k, at: (0, at[0])),
            pl.BlockSpec(spread.shape, lambda k, at: (0, 0)),
            pl.BlockSpec((rights.shape[0], width), lambda k, at: (0, at[0])),
            anywhere(),
        ]
        args = [tokens, wt, left, right, spread, rights, after]
        aliases = {}
        if not begun:
            specs, args = specs + [anywhere()], args + [acts]
            aliases = {len(args): 0}
        shape = acts if begun else acts.shape
        out_shape, out_specs = [jax.ShapeDtypeStruct(shape, jnp.bfloat16)], [tile]
        if keep:
            out_shape.append(jax.ShapeDtypeStruct((depth, width), jnp.bfloat16))
            out_specs.append(block)
        out_shape.append(MARK)
        out_specs.append(vmem())
        return call(
            functools.partial(full_kernel, scale, keep, begun),
            where, (4,), specs, args, out_specs, out_shape, aliases,
            [pltpu.VMEM((rows, width), jnp.float32)], WIDE,
        )
    if not last:
        extra = [spread, rights] if first else [before]
        return call(
            functools.partial(sum_kernel, scale, start),
            where, (1,), [vmem()] * (4 + len(extra)) + [anywhere()],
            [tokens, wt, left, right, *extra, after], vmem(),
            jax.ShapeDtypeStruct((rows, width), jnp.float32), {} if first else {5: 0},
        )
    return call(
        functools.partial(last_kernel, start),
        where, (1,), [vmem()] * 5 + [anywhere()],
        [tokens, wt, left, right, before, acts], anywhere(),
        jax.ShapeDtypeStruct(acts.shape, jnp.bfloat16), {6: 0},
        [pltpu.VMEM((rows, width), jnp.bfloat16), pltpu.SemaphoreType.DMA((2,))],
    )


def local(tokens, weight, old_left, old_right, selected, shaping, new_left, new_right):
    groups = lax.axis_size("pop")
    me = lax.axis_index("pop")
    spot = lax.axis_index("col")
    depth, width = weight.shape
    members, rank, slab = new_left.shape
    rows = tokens.shape[0]
    each = rows // members
    count = selected.shape[1]
    scale = noise_scale / math.sqrt(depth * rank)
    grain = depth // sum(PIECES)
    chips = groups // 2
    where = jnp.stack([me, spot]).astype(jnp.int32)

    plan = []
    hops = [chips // 2] + [hop for hop in range(1, chips) if hop != chips // 2]
    for hop in hops:
        at = 0
        for piece in PIECES if hop == hops[-1] else (sum(PIECES),):
            plan.append((hop, at * grain, piece * grain))
            at += piece

    def send(index, piece):
        turn = [(p, (p + 2 * plan[index][0]) % groups) for p in range(groups)]
        return lax.ppermute(piece, "pop", turn)

    factor = 1.0 / math.sqrt(depth * rank * count * groups)
    piece, mark = cut(weight, *plan[0][1:], selected)
    arrived = [send(0, piece)]
    packed, left, right, mark = pick(
        factor, selected, shaping, old_left, old_right, width, mark
    )
    packed = send(0, packed)
    piece, mark = cut(weight, *plan[1][1:], mark)
    arrived.append(send(1, piece))
    tall = count * rank
    lefts, rights = unpack(packed, tall, slab, old_right.shape[2])
    left, right = jnp.concatenate([left, lefts], 0), jnp.concatenate([right, rights], 0)
    for bit in bits(chips, 2):
        left = jnp.concatenate([left, swap(left, "pop", bit)], 0)
        right = jnp.concatenate([right, swap(right, "pop", bit)], 0)
    left, mark = gate(left[None], mark)
    sibling = swap(weight, "pop", 1)
    rights = new_right.reshape(members * rank, -1)
    proj = project(tokens, new_left.reshape(-1, slab), rank, each, where, mark)
    piece, mark = cut(weight, *plan[2][1:], mark)
    spare, ready = cut(weight, *plan[3][1:], mark)
    for turns, bit in enumerate(bits(lax.axis_size("col"))):
        left = jnp.concatenate([left, swap(left, "col", bit)], 0)
        if turns == 0:
            arrived[0], mark = gate(arrived[0], left)
            piece, mark = gate(piece, mark)
            arrived.append(send(2, piece))
            right, _ = gate(right, mark)
            right = jnp.concatenate([right, swap(right, "pop", 1)], 0)
            sibling, mark = gate(sibling, mark)
            left, mark = gate(left, mark, proj, ready)
        elif bit * 2 < lax.axis_size("col"):
            left, _ = gate(left, proj)
        else:
            arrived[1], mark = gate(arrived[1], left, proj)
            spare, mark = gate(spare, mark)
            arrived.append(send(3, spare))
            left, _ = gate(left, mark, rights)
        proj = proj + swap(proj, "col", bit)
    left = turn(jnp.concatenate([left, swap(left, "pop", 1)], 1), where)
    spread = spread_out(proj, members, rank, each)

    def run(block, wt, start, before, acts, after, keep=False):
        return run_block(
            jnp.reshape(block, (1,)).astype(jnp.int32),
            tokens, wt, left, right, start, scale, spread, rights, acts, before, after, keep,
        )

    narrow = width % 128 != 0
    core = lax.rem(me, 2)

    def pair(own, other):
        return jnp.where(
            core == 0, jnp.concatenate([own, other], 1), jnp.concatenate([other, own], 1)
        )

    whole = (rows, width * groups)
    if narrow:
        acts, both, done = run(me // 2, pair(weight, sibling), 0, None, whole, where, keep=True)
        updated = lax.dynamic_slice_in_dim(both, core * width, width, 1)
    else:
        acts, updated, done = run(me, weight, 0, None, whole, where, keep=True)
    if not narrow:
        acts, done = run(me ^ 1, sibling, 0, None, acts, done)
    many = [index for index, part in enumerate(plan) if part[0] == hops[-1]][:-2]
    for index, (hop, start, size) in enumerate(plan):
        part = arrived[index]
        if index > 1:
            part, mark = gate(part, done)
            arrived[index] = part
            if index + 2 < len(plan):
                piece, _ = cut(weight, *plan[index + 2][1:], mark)
                arrived.append(send(index + 2, piece))
        if index in many:
            if index != many[-1]:
                continue
            part = jnp.concatenate([arrived[i] for i in many[:-1]] + [part], 0)
            start, size = 0, part.shape[0]
        other = swap(part, "pop", 1)
        if start == 0:
            sums = [None, None]
        ends = start + size == depth
        source = lax.rem(me - 2 * hop + 2 * groups, groups)
        tasks = ((source, part), (source ^ 1, other))
        if narrow:
            tasks = ((source // 2, pair(part, other)),)
        for side, (block, wt) in enumerate(tasks):
            got = run(block, wt, start, sums[side], acts if ends else None, done)
            if not ends:
                sums[side] = done = got
            elif start == 0:
                acts, done = got
            else:
                acts = got
    return updated, acts


def solution(mesh):
    placed = (
        P("pop", None),
        P(None, ("col", "pop")),
        P("pop", None, "col"),
        P("pop", None, "col"),
        P("pop", None),
        P("pop", None),
        P("pop", None, "col"),
        P("pop", None, "col"),
    )
    return jax.shard_map(
        local,
        mesh=mesh,
        in_specs=placed,
        out_specs=(P(None, ("col", "pop")), P("pop", "col")),
        check_vma=False,
    )
```

time: 159 us -> 119 us (0.75)
  waiting for transfers between devices: 45.6 us -> 24 us
  local copies, waits for them, and re-layouts: 32 us -> 16.6 us
  starting transfers between devices: 21.2 us -> 15.5 us
  Pallas kernels: 56.4 us -> 59.3 us
    ppermute x6 -> x5, waiting for transfers between devices: 24.5 us -> 6.86 us  [send(): return lax.ppermute(piece, 'pop', turn)]
    unnamed x70 -> x54, local copies, waits for them, and re-layouts: 25.1 us -> 11 us
    pallas_call x1 -> x4, Pallas kernels: 1.72 us -> 8.8 us  [cut(): pl.pallas_call(functools.partial(cut_kernel, start), in_specs=[anywhere()...]
    pallas_call x1 -> x0, Pallas kernels: 4.79 us -> none  [copy_of(): pl.pallas_call(copy_kernel, grid=(4,), in_specs=[block, anywhere()], out_...]
    ppermute x15 -> x12, starting transfers between devices: 13.2 us -> 8.75 us  [swap(): lax.ppermute(array, axis, [(i, i ^ bit) for i in range(lax.axis_size(axis...]
    pallas_call x18 -> x12, Pallas kernels: 7.79 us -> 3.62 us  [gate(): pl.pallas_call(functools.partial(gate_kernel, len(after) + 2), in_specs=[...]
    ppermute x15 -> x12, waiting for transfers between devices: 21.1 us -> 17.1 us  [swap(): lax.ppermute(array, axis, [(i, i ^ bit) for i in range(lax.axis_size(axis...]
    pallas_call x14 -> x8, Pallas kernels: 36 us -> 39.6 us  [call(): pl.pallas_call(kernel, grid_spec=pltpu.PrefetchScalarGridSpec(num_scalar_...]
  transfers between devices with their start and end apart: 21 -> 17, of which waited for: 10 -> 8; matrix products, arithmetic and copies ran while one was open for 6% -> 7% of each run, Pallas kernels for 30% -> 48%
where the time goes in v2:
time: 119 us; the launch traced here: 118 us
  Pallas kernels  59.3 us (50%)
  waiting for transfers between devices  24 us (20%)
  local copies, waits for them, and re-layouts  16.6 us (14%)
  starting transfers between devices  15.5 us (13%)
  other arithmetic  1.82 us (2%)
  between operations  1.22 us (1%)
    pallas_call x8, Pallas kernels, call(): pl.pallas_call(kernel, grid_spec=pltpu.PrefetchScalarGridSpec(num_scalar_...  39.6 us
    ppermute x12, waiting for transfers between devices, swap(): lax.ppermute(array, axis, [(i, i ^ bit) for i in range(lax.axis_size(axis...  17.1 us
    unnamed x54, local copies, waits for them, and re-layouts  11 us
    pallas_call x4, Pallas kernels, cut(): pl.pallas_call(functools.partial(cut_kernel, start), in_specs=[anywhere()...  8.8 us
    ppermute x12, starting transfers between devices, swap(): lax.ppermute(array, axis, [(i, i ^ bit) for i in range(lax.axis_size(axis...  8.75 us
    ppermute x5, waiting for transfers between devices, send(): return lax.ppermute(piece, 'pop', turn)  6.86 us
    ppermute x5, starting transfers between devices, send(): return lax.ppermute(piece, 'pop', turn)  6.71 us
    pallas_call x12, Pallas kernels, gate(): pl.pallas_call(functools.partial(gate_kernel, len(after) + 2), in_specs=[...  3.62 us
  transfers between devices with their start and end apart: 17, of which 8 were waited for; matrix products, arithmetic and copies ran while one was open for 7% of the time, Pallas kernels for 48%

profile of v2, /device:TPU:0, one launch (start us, length us, event | category | flops | bytes accessed | tf_op | source)
XLA Modules:
  0.0 118.4 jit_solution(13569005783841667894)
XLA Ops:
  1.1 1.7 %shard_map.95 = (bf16[256,512]{1,0:T(8,128)(2,1)}, f32[8,128]{1,0:T(8,128)}) custom-call(bf16[4096,512]{1,0:T(8,128)(2,1)} %wt.9, s32[1,8]{1,0:T(1,128)} %picked.1), custom_call_target="tpu_custom_call" | custom-call | flops 1 | bytes 1 | tf_op jit(solution)/shard_map/pallas_call | solution.py:71
  2.8 2.6 %shard_map.96 = (bf16[160,512]{1,0:T(8,128)(2,1)}, bf16[32,512]{1,0:T(8,128)(2,1)}, bf16[32,2048]{1,0:T(8,128)(2,1)}, f32[8,128]{1,0:T(8,128)}) custom-call(s32[1,8]{1,0:T(1,128)} %picked.1, f32[1,8]{1,0:T(1,128)} %shaping.1, bf16[112,4,512]{2,1,0:T(4,128)(2,1)} %lefts.1, bf16[112,4,2048]{2,1,0:T(4,128)(2,1)} %rights.1, f32[8,128]{1,0:T(8,128)} %get-tuple-element.37.after), custom_call_target="tpu_custom_call" | custom-call | flops 1 | bytes 1 | tf_op jit(solution)/shard_map/pallas_call | solution.py:118
  5.4 2.6 %collective-permute-start = (bf16[160,512]{1,0:T(8,128)(2,1)}, bf16[160,512]{1,0:T(8,128)(2,1)S(1)}, u32[]{:S(2)}, u32[]{:S(2)}) collective-permute-start(bf16[160,512]{1,0:T(8,128)(2,1)} %get-tuple-element.39), channel_id=1, source_target_pairs={{0,16},{8,24},{16,0},{24,8},{1,17},{9,25},{17,1},{25,9},{2,18},{10... | collective-permute-start | bytes 491528 | tf_op jit(solution)/shard_map/ppermute | solution.py:386
  8.1 2.2 %shard_map.97 = (bf16[1024,512]{1,0:T(8,128)(2,1)}, f32[8,128]{1,0:T(8,128)}) custom-call(bf16[4096,512]{1,0:T(8,128)(2,1)} %wt.9, f32[8,128]{1,0:T(8,128)} %get-tuple-element.40.after), custom_call_target="tpu_custom_call" | custom-call | flops 1 | bytes 1 | tf_op jit(solution)/shard_map/pallas_call | solution.py:71
  10.3 2.0 %collective-permute-start.7 = (bf16[1024,512]{1,0:T(8,128)(2,1)}, bf16[1024,512]{1,0:T(8,128)(2,1)S(1)}, u32[]{:S(2)}, u32[]{:S(2)}) collective-permute-start(bf16[1024,512]{1,0:T(8,128)(2,1)} %get-tuple-element.54), channel_id=1, source_target_pairs={{0,16},{8,24},{16,0},{24,8},{1,17},{9,25},{17,1},{25,9},{2,18},{10... | collective-permute-start | bytes 3145736 | tf_op jit(solution)/shard_map/ppermute | solution.py:386
  12.4 0.9 collective-permute-done
  13.3 0.6 fusion
  13.9 0.7 copy-done.18
  14.6 0.6 copy-done.15
  15.2 1.9 %collective-permute-start.1 = (bf16[1,64,512]{2,1,0:T(8,128)(2,1)S(1)}, bf16[1,64,512]{2,1,0:T(8,128)(2,1)S(1)}, u32[]{:S(2)}, u32[]{:S(2)}) collective-permute-start(bf16[1,64,512]{2,1,0:T(8,128)(2,1)S(1)} %get-tuple-element.42), channel_id=1, source_target_pairs={{0,1},{1,0},{2,3},{3,2},{4,5},{5,4},{6,7},{7,6},{8,9},{9,8},{10,11... | collective-permute-start | bytes 196616 | tf_op jit(solution)/shard_map/ppermute | solution.py:26
  17.1 3.1 %shard_map.99 = (bf16[2304,512]{1,0:T(8,128)(2,1)}, f32[8,128]{1,0:T(8,128)}) custom-call(bf16[4096,512]{1,0:T(8,128)(2,1)} %wt.9, f32[8,128]{1,0:T(8,128)} %copy-done.15), custom_call_target="tpu_custom_call" | custom-call | flops 1 | bytes 1 | tf_op jit(solution)/shard_map/pallas_call | solution.py:71
  20.3 1.7 %copy-done.9 = bf16[2304,512]{1,0:T(8,128)(2,1)S(1)} copy-done((bf16[2304,512]{1,0:T(8,128)(2,1)S(1)}, bf16[2304,512]{1,0:T(8,128)(2,1)}, u32[]{:S(2)}) %copy-start.9) | copy-done | bytes 2359320
  22.0 1.5 %copy-done.10 = bf16[2304,512]{1,0:T(8,128)(2,1)} copy-done((bf16[2304,512]{1,0:T(8,128)(2,1)}, bf16[2304,512]{1,0:T(8,128)(2,1)S(1)}, u32[]{:S(2)}) %copy-start.10) | copy-done | bytes 2359320
  23.5 1.5 %collective-permute-start.13 = (bf16[2304,512]{1,0:T(8,128)(2,1)}, bf16[2304,512]{1,0:T(8,128)(2,1)}, u32[]{:S(2)}, u32[]{:S(2)}) collective-permute-start(bf16[2304,512]{1,0:T(8,128)(2,1)} %copy-done.10), channel_id=1, source_target_pairs={{0,16},{8,24},{16,0},{24,8},{1,17},{9,25},{17,1},{25,9},{2,18},{10... | collective-permute-start | bytes 7077896 | tf_op jit(solution)/shard_map/ppermute | solution.py:386
  25.0 0.9 reshape.27.left
  25.9 0.6 pad_add_fusion.where.refs_0_
  26.5 1.8 %shard_map.104 = (bf16[512,512]{1,0:T(8,128)(2,1)}, f32[8,128]{1,0:T(8,128)}) custom-call(bf16[4096,512]{1,0:T(8,128)(2,1)} %wt.9, f32[8,128]{1,0:T(8,128)} %get-tuple-element.49.after), custom_call_target="tpu_custom_call" | custom-call | flops 1 | bytes 1 | tf_op jit(solution)/shard_map/pallas_call | solution.py:71
  28.4 3.3 %shard_map.103.refs_2_ = f32[8,896]{1,0:T(8,128)} custom-call(s32[2]{0:T(128)} %pad_add_fusion.where.refs_0_, bf16[448,512]{1,0:T(8,128)(2,1)} %reshape.27.left, bf16[896,4096]{1,0:T(8,128)(2,1)} %tok.17, f32[8,128]{1,0:T(8,128)} %copy-done.15), custom_call_target="tpu_custom_call" | custom-call | flops 1 | bytes 1 | tf_op jit(solution)/shard_map/pallas_call | solution.py:166
  31.6 0.7 copy-done.14
  32.4 0.6 shard_map.105
  33.0 1.6 %collective-permute-start.4 = (bf16[2,64,512]{2,1,0:T(8,128)(2,1)S(1)}, bf16[2,64,512]{2,1,0:T(8,128)(2,1)S(1)}, u32[]{:S(2)}, u32[]{:S(2)}) collective-permute-start(bf16[2,64,512]{2,1,0:T(8,128)(2,1)S(1)} %get-tuple-element.51), channel_id=1, source_target_pairs={{0,2},{1,3},{2,0},{3,1},{4,6},{5,7},{6,4},{7,5},{8,10},{9,11},{10,... | collective-permute-start | bytes 393224 | tf_op jit(solution)/shard_map/ppermute | solution.py:26
  34.5 1.1 collective-permute-start.5
  35.6 2.8 %collective-permute-done.5 = f32[8,896]{1,0:T(8,128)S(1)} collective-permute-done((f32[8,896]{1,0:T(8,128)S(1)}, f32[8,896]{1,0:T(8,128)S(1)}, u32[]{:S(2)}, u32[]{:S(2)}) %collective-permute-start.5) | collective-permute-done | bytes 28704 | tf_op jit(solution)/shard_map/ppermute | solution.py:26
  38.9 0.6 shard_map.106
  39.5 2.6 %collective-permute-start.6 = (bf16[4,64,512]{2,1,0:T(8,128)(2,1)S(1)}, bf16[4,64,512]{2,1,0:T(8,128)(2,1)S(1)}, u32[]{:S(2)}, u32[]{:S(2)}) collective-permute-start(bf16[4,64,512]{2,1,0:T(8,128)(2,1)S(1)} %get-tuple-element.52), channel_id=1, source_target_pairs={{0,4},{1,5},{2,6},{3,7},{4,0},{5,1},{6,2},{7,3},{8,12},{9,13},{10,... | collective-permute-start | bytes 786440 | tf_op jit(solution)/shard_map/ppermute | solution.py:26
  42.3 0.7 constant_dynamic-update-slice_fusion.7
  43.1 8.5 %collective-permute-done.6 = bf16[4,64,512]{2,1,0:T(8,128)(2,1)S(1)} collective-permute-done((bf16[4,64,512]{2,1,0:T(8,128)(2,1)S(1)}, bf16[4,64,512]{2,1,0:T(8,128)(2,1)S(1)}, u32[]{:S(2)}, u32[]{:S(2)}) %collective-permute-start.6) | collective-permute-done | bytes 262176 | tf_op jit(solution)/shard_map/ppermute | solution.py:26
  51.6 1.0 constant_dynamic-update-slice_fusion.6.wt
  52.7 3.0 %reshape.28.refs_2_.rights.refs_1_ = bf16[448,2048]{1,0:T(8,128)(2,1)S(1)} reshape(bf16[112,4,2048]{2,1,0:T(4,128)(2,1)} %param.15) | data formatting | bytes 3670016 | tf_op jit(solution)/shard_map/reshape | solution.py:405
  55.7 0.6 shard_map.109
  56.8 5.0 %collective-permute-done.11 = f32[8,896]{1,0:T(8,128)S(1)} collective-permute-done((f32[8,896]{1,0:T(8,128)S(1)}, f32[8,896]{1,0:T(8,128)S(1)}, u32[]{:S(2)}, u32[]{:S(2)}) %collective-permute-start.11) | collective-permute-done | bytes 28704 | tf_op jit(solution)/shard_map/ppermute | solution.py:26
  61.9 0.6 shard_map.111
  62.6 1.1 pad_maximum_fusion.left
  64.2 1.3 %shard_map.110.left = bf16[4096,128]{1,0:T(8,128)(2,1)S(1)} custom-call(s32[2]{0:T(128)S(1)} %copy-done.16, bf16[8,128,512]{2,1,0:T(8,128)(2,1)S(1)} %pad_maximum_fusion.left), custom_call_target="tpu_custom_call" | custom-call | flops 1 | bytes 1 | tf_op jit(solution)/shard_map/pallas_call | solution.py:190
  65.5 0.9 copy-done.1
  66.5 11.2 %shard_map.113 = (bf16[896,2048]{1,0:T(8,128)(2,1)}, bf16[4096,512]{1,0:T(8,128)(2,1)}, f32[8,128]{1,0:T(8,128)}) custom-call(s32[1]{0:T(128)} %bitcast.where, bf16[896,4096]{1,0:T(8,128)(2,1)} %tok.17, bf16[4096,512]{1,0:T(8,128)(2,1)} %wt.9, bf16[4096,128]{1,0:T(8,128)(2,1)} %copy-done.1, bf16[128,2048]{1,0:T(8,128)(2,1)} %copy-done.5, ...), custom_call_target="tpu_custom_call" | custom-call | flops 1 | bytes 1 | tf_op jit(solution)/shard_map/pallas_call | solution.py:295
  77.7 10.6 %shard_map.114 = (bf16[896,2048]{1,0:T(8,128)(2,1)}, f32[8,128]{1,0:T(8,128)}) custom-call(s32[1]{0:T(128)} %bitcast.5.where, bf16[896,4096]{1,0:T(8,128)(2,1)} %tok.17, bf16[4096,512]{1,0:T(8,128)(2,1)} %get-tuple-element.65.wt, bf16[4096,128]{1,0:T(8,128)(2,1)} %copy-done.1, bf16[128,2048]{1,0:T(8,128)(2,1)} %copy-done.5, ...), custom_call_target="tpu_custom_call", output_to_operand_aliasing={{0}: (8, {})} | custom-call | flops 1 | bytes 1 | tf_op jit(solution)/shard_map/pallas_call | solution.py:295
  88.4 3.1 %copy-done = bf16[896,4096]{1,0:T(8,128)(2,1)S(1)} copy-done((bf16[896,4096]{1,0:T(8,128)(2,1)S(1)}, bf16[896,4096]{1,0:T(8,128)(2,1)}, u32[]{:S(2)}) %copy-start) | copy-done | bytes 7340056
  91.5 0.7 copy-done.17
  92.1 3.5 %shard_map.115.refs_2_.refs_0_ = f32[896,512]{1,0:T(8,128)S(1)} custom-call(s32[1]{0:T(128)} %bitcast.4.where, bf16[896,4096]{1,0:T(8,128)(2,1)S(1)} %copy-done, bf16[1280,512]{1,0:T(8,128)(2,1)} %constant_dynamic-update-slice_fusion.6.wt, bf16[4096,128]{1,0:T(8,128)(2,1)S(1)} %copy-done.2, bf16[128,2048]{1,0:T(8,128)(2,1)S(1)} %copy-done.6, ...), custom_call_target="tpu_custom_call" | custom-call | flops 1 | bytes 1 | tf_op jit(solution)/shard_map/pallas_call | solution.py:295
  95.6 3.5 %shard_map.116.refs_1_.refs_0_ = f32[896,512]{1,0:T(8,128)S(1)} custom-call(s32[1]{0:T(128)} %bitcast.3.where, bf16[896,4096]{1,0:T(8,128)(2,1)S(1)} %copy-done, bf16[1280,512]{1,0:T(8,128)(2,1)} %collective-permute-done.14.wt, bf16[4096,128]{1,0:T(8,128)(2,1)S(1)} %copy-done.2, bf16[128,2048]{1,0:T(8,128)(2,1)S(1)} %copy-done.6, ...), custom_call_target="tpu_custom_call" | custom-call | flops 1 | bytes 1 | tf_op jit(solution)/shard_map/pallas_call | solution.py:295
  99.1 0.6 shard_map.117
  100.7 4.6 %shard_map.118.refs_1_.before = f32[896,512]{1,0:T(8,128)S(1)} custom-call(s32[1]{0:T(128)} %bitcast.4.where, bf16[896,4096]{1,0:T(8,128)(2,1)S(1)} %copy-done, bf16[2304,512]{1,0:T(8,128)(2,1)} %get-tuple-element.69.wt, bf16[4096,128]{1,0:T(8,128)(2,1)S(1)} %copy-done.2, bf16[128,2048]{1,0:T(8,128)(2,1)S(1)} %copy-done.6, ...), custom_call_target="tpu_custom_call", output_to_operand_aliasing={{}: (5, {})} | custom-call | flops 1 | bytes 1 | tf_op jit(solution)/shard_map/pallas_call | solution.py:295
  105.3 3.0 %shard_map.119.refs_1_.before = f32[896,512]{1,0:T(8,128)S(1)} custom-call(s32[1]{0:T(128)} %bitcast.3.where, bf16[896,4096]{1,0:T(8,128)(2,1)S(1)} %copy-done, bf16[2304,512]{1,0:T(8,128)(2,1)S(1)} %collective-permute-done.15.wt, bf16[4096,128]{1,0:T(8,128)(2,1)S(1)} %copy-done.2, bf16[128,2048]{1,0:T(8,128)(2,1)S(1)} %copy-done.6, ...), custom_call_target="tpu_custom_call", output_to_operand_aliasing={{}: (5, {})} | custom-call | flops 1 | bytes 1 | tf_op jit(solution)/shard_map/pallas_call | solution.py:295
  108.2 5.9 %collective-permute-done.12.refs_0_ = bf16[512,512]{1,0:T(8,128)(2,1)S(1)} collective-permute-done((bf16[512,512]{1,0:T(8,128)(2,1)S(1)}, bf16[512,512]{1,0:T(8,128)(2,1)S(1)}, u32[]{:S(2)}, u32[]{:S(2)}) %collective-permute-start.12) | collective-permute-done | bytes 524320 | tf_op jit(solution)/shard_map/ppermute | solution.py:386
  114.1 0.6 shard_map.120
  114.7 1.6 %shard_map.121.acts = bf16[896,2048]{1,0:T(8,128)(2,1)} custom-call(s32[1]{0:T(128)} %bitcast.4.where, bf16[896,4096]{1,0:T(8,128)(2,1)S(1)} %copy-done, bf16[512,512]{1,0:T(8,128)(2,1)S(1)} %get-tuple-element.70.wt, bf16[4096,128]{1,0:T(8,128)(2,1)S(1)} %copy-done.2, bf16[128,2048]{1,0:T(8,128)(2,1)S(1)} %copy-done.6, ...), custom_call_target="tpu_custom_call", output_to_operand_aliasing={{}: (6, {})} | custom-call | flops 1 | bytes 1 | tf_op jit(solution)/shard_map/pallas_call | solution.py:295
  116.7 1.6 %shard_map.122 = bf16[896,2048]{1,0:T(8,128)(2,1)} custom-call(s32[1]{0:T(128)} %bitcast.3.where, bf16[896,4096]{1,0:T(8,128)(2,1)S(1)} %copy-done, bf16[512,512]{1,0:T(8,128)(2,1)S(1)} %collective-permute-done.16.wt, bf16[4096,128]{1,0:T(8,128)(2,1)S(1)} %copy-done.2, bf16[128,2048]{1,0:T(8,128)(2,1)S(1)} %copy-done.6, ...), custom_call_target="tpu_custom_call", output_to_operand_aliasing={{}: (6, {})} | custom-call | flops 1 | bytes 1 | tf_op jit(solution)/shard_map/pallas_call | solution.py:295
  (83 shorter events, 3.7 us)
Async XLA Ops:
  0.6 31.0 %collective-permute-start.2 = (bf16[4096,512]{1,0:T(8,128)(2,1)}, bf16[4096,512]{1,0:T(8,128)(2,1)}, u32[]{:S(2)}, u32[]{:S(2)}) collective-permute-start(bf16[4096,512]{1,0:T(8,128)(2,1)} %wt.9), channel_id=1, source_target_pairs={{0,8},{8,0},{16,24},{24,16},{1,9},{9,1},{17,25},{25,17},{2,10},{10... | collective-permute-start | bytes 12582920 | tf_op jit(solution)/shard_map/ppermute | solution.py:26
  2.8 5.2 %copy-start.24 = (bf16[256,512]{1,0:T(8,128)(2,1)S(1)}, bf16[256,512]{1,0:T(8,128)(2,1)}, u32[]{:S(2)}) copy-start(bf16[256,512]{1,0:T(8,128)(2,1)} %get-tuple-element.45) | copy-start | bytes 786436
  5.4 7.9 %collective-permute-start = (bf16[160,512]{1,0:T(8,128)(2,1)}, bf16[160,512]{1,0:T(8,128)(2,1)S(1)}, u32[]{:S(2)}, u32[]{:S(2)}) collective-permute-start(bf16[160,512]{1,0:T(8,128)(2,1)} %get-tuple-element.39), channel_id=1, source_target_pairs={{0,16},{8,24},{16,0},{24,8},{1,17},{9,25},{17,1},{25,9},{2,18},{10... | collective-permute-start | bytes 491528 | tf_op jit(solution)/shard_map/ppermute | solution.py:386
  8.0 12.2 %collective-permute-start.3 = (bf16[256,512]{1,0:T(8,128)(2,1)S(1)}, bf16[256,512]{1,0:T(8,128)(2,1)S(1)}, u32[]{:S(2)}, u32[]{:S(2)}) collective-permute-start(bf16[256,512]{1,0:T(8,128)(2,1)S(1)} %copy-done.24), channel_id=1, source_target_pairs={{0,16},{8,24},{16,0},{24,8},{1,17},{9,25},{17,1},{25,9},{2,18},{10... | collective-permute-start | bytes 786440 | tf_op jit(solution)/shard_map/ppermute | solution.py:386
  8.1 5.8 %copy-start.23 = (bf16[32,512]{1,0:T(8,128)(2,1)S(1)}, bf16[32,512]{1,0:T(8,128)(2,1)}, u32[]{:S(2)}) copy-start(bf16[32,512]{1,0:T(8,128)(2,1)} %get-tuple-element.38) | copy-start | bytes 98308
  10.3 41.2 %collective-permute-start.7 = (bf16[1024,512]{1,0:T(8,128)(2,1)}, bf16[1024,512]{1,0:T(8,128)(2,1)S(1)}, u32[]{:S(2)}, u32[]{:S(2)}) collective-permute-start(bf16[1024,512]{1,0:T(8,128)(2,1)} %get-tuple-element.54), channel_id=1, source_target_pairs={{0,16},{8,24},{16,0},{24,8},{1,17},{9,25},{17,1},{25,9},{2,18},{10... | collective-permute-start | bytes 3145736 | tf_op jit(solution)/shard_map/ppermute | solution.py:386
  13.9 0.7 copy-start.18
  14.6 0.6 copy-start.15
  15.2 5.0 %collective-permute-start.1 = (bf16[1,64,512]{2,1,0:T(8,128)(2,1)S(1)}, bf16[1,64,512]{2,1,0:T(8,128)(2,1)S(1)}, u32[]{:S(2)}, u32[]{:S(2)}) collective-permute-start(bf16[1,64,512]{2,1,0:T(8,128)(2,1)S(1)} %get-tuple-element.42), channel_id=1, source_target_pairs={{0,1},{1,0},{2,3},{3,2},{4,5},{5,4},{6,7},{7,6},{8,9},{9,8},{10,11... | collective-permute-start | bytes 196616 | tf_op jit(solution)/shard_map/ppermute | solution.py:26
  20.2 4.8 %copy-start.20 = (bf16[112,4,512]{2,1,0:T(4,128)(2,1)S(1)}, bf16[112,4,512]{2,1,0:T(4,128)(2,1)}, u32[]{:S(2)}) copy-start(bf16[112,4,512]{2,1,0:T(4,128)(2,1)} %param.14) | copy-start | bytes 1376260
  20.3 1.7 %copy-start.9 = (bf16[2304,512]{1,0:T(8,128)(2,1)S(1)}, bf16[2304,512]{1,0:T(8,128)(2,1)}, u32[]{:S(2)}) copy-start(bf16[2304,512]{1,0:T(8,128)(2,1)} %get-tuple-element.44.refs_0_) | copy-start | bytes 7077892
  22.0 1.5 %copy-start.10 = (bf16[2304,512]{1,0:T(8,128)(2,1)}, bf16[2304,512]{1,0:T(8,128)(2,1)S(1)}, u32[]{:S(2)}) copy-start(bf16[2304,512]{1,0:T(8,128)(2,1)S(1)} %get-tuple-element.62) | copy-start | bytes 7077892
  23.5 75.7 %collective-permute-start.13 = (bf16[2304,512]{1,0:T(8,128)(2,1)}, bf16[2304,512]{1,0:T(8,128)(2,1)}, u32[]{:S(2)}, u32[]{:S(2)}) collective-permute-start(bf16[2304,512]{1,0:T(8,128)(2,1)} %copy-done.10), channel_id=1, source_target_pairs={{0,16},{8,24},{16,0},{24,8},{1,17},{9,25},{17,1},{25,9},{2,18},{10... | collective-permute-start | bytes 7077896 | tf_op jit(solution)/shard_map/ppermute | solution.py:386
  31.6 0.7 copy-start.14
  31.6 0.7 copy-start.19
  33.0 5.9 %collective-permute-start.4 = (bf16[2,64,512]{2,1,0:T(8,128)(2,1)S(1)}, bf16[2,64,512]{2,1,0:T(8,128)(2,1)S(1)}, u32[]{:S(2)}, u32[]{:S(2)}) collective-permute-start(bf16[2,64,512]{2,1,0:T(8,128)(2,1)S(1)} %get-tuple-element.51), channel_id=1, source_target_pairs={{0,2},{1,3},{2,0},{3,1},{4,6},{5,7},{6,4},{7,5},{8,10},{9,11},{10,... | collective-permute-start | bytes 393224 | tf_op jit(solution)/shard_map/ppermute | solution.py:26
  34.5 3.9 %collective-permute-start.5 = (f32[8,896]{1,0:T(8,128)S(1)}, f32[8,896]{1,0:T(8,128)S(1)}, u32[]{:S(2)}, u32[]{:S(2)}) collective-permute-start(f32[8,896]{1,0:T(8,128)S(1)} %copy-done.14), channel_id=1, source_target_pairs={{0,1},{1,0},{2,3},{3,2},{4,5},{5,4},{6,7},{7,6},{8,9},{9,8},{10,11... | collective-permute-start | bytes 86024 | tf_op jit(solution)/shard_map/ppermute | solution.py:26
  38.4 3.9 %collective-permute-start.8 = (f32[8,896]{1,0:T(8,128)S(1)}, f32[8,896]{1,0:T(8,128)S(1)}, u32[]{:S(2)}, u32[]{:S(2)}) collective-permute-start(f32[8,896]{1,0:T(8,128)S(1)} %add.17.refs_1_), channel_id=1, source_target_pairs={{0,2},{1,3},{2,0},{3,1},{4,6},{5,7},{6,4},{7,5},{8,10},{9,11},{10,... | collective-permute-start | bytes 86024 | tf_op jit(solution)/shard_map/ppermute | solution.py:26
  39.5 12.1 %collective-permute-start.6 = (bf16[4,64,512]{2,1,0:T(8,128)(2,1)S(1)}, bf16[4,64,512]{2,1,0:T(8,128)(2,1)S(1)}, u32[]{:S(2)}, u32[]{:S(2)}) collective-permute-start(bf16[4,64,512]{2,1,0:T(8,128)(2,1)S(1)} %get-tuple-element.52), channel_id=1, source_target_pairs={{0,4},{1,5},{2,6},{3,7},{4,0},{5,1},{6,2},{7,3},{8,12},{9,13},{10,... | collective-permute-start | bytes 786440 | tf_op jit(solution)/shard_map/ppermute | solution.py:26
  52.6 3.0 %copy-start.11 = (bf16[512,512]{1,0:T(8,128)(2,1)S(1)}, bf16[512,512]{1,0:T(8,128)(2,1)}, u32[]{:S(2)}) copy-start(bf16[512,512]{1,0:T(8,128)(2,1)} %get-tuple-element.53.refs_0_) | copy-start | bytes 1572868
  52.7 43.0 %collective-permute-start.14 = (bf16[1280,512]{1,0:T(8,128)(2,1)}, bf16[1280,512]{1,0:T(8,128)(2,1)}, u32[]{:S(2)}, u32[]{:S(2)}) collective-permute-start(bf16[1280,512]{1,0:T(8,128)(2,1)} %constant_dynamic-update-slice_fusion.6.wt), channel_id=1, source_target_pairs={{0,8},{8,0},{16,24},{24,16},{1,9},{9,1},{17,25},{25,17},{2,10},{10... | collective-permute-start | bytes 3932168 | tf_op jit(solution)/shard_map/ppermute | solution.py:26
  55.6 6.3 %copy-start.3 = (bf16[448,2048]{1,0:T(8,128)(2,1)}, bf16[448,2048]{1,0:T(8,128)(2,1)S(1)}, u32[]{:S(2)}) copy-start(bf16[448,2048]{1,0:T(8,128)(2,1)S(1)} %reshape.28.refs_2_.rights.refs_1_) | copy-start | bytes 5505028
  55.7 1.1 copy-start.21
  55.7 1.1 copy-start.22
  55.7 6.9 %copy-start.12 = (bf16[512,512]{1,0:T(8,128)(2,1)}, bf16[512,512]{1,0:T(8,128)(2,1)S(1)}, u32[]{:S(2)}) copy-start(bf16[512,512]{1,0:T(8,128)(2,1)S(1)} %get-tuple-element.61) | copy-start | bytes 1572868
  56.3 6.3 %collective-permute-start.9 = (bf16[8,64,512]{2,1,0:T(8,128)(2,1)S(1)}, bf16[8,64,512]{2,1,0:T(8,128)(2,1)}, u32[]{:S(2)}, u32[]{:S(2)}) collective-permute-start(bf16[8,64,512]{2,1,0:T(8,128)(2,1)S(1)} %get-tuple-element.57), channel_id=1, source_target_pairs={{0,8},{8,0},{16,24},{24,16},{1,9},{9,1},{17,25},{25,17},{2,10},{10... | collective-permute-start | bytes 1572872 | tf_op jit(solution)/shard_map/ppermute | solution.py:26
  56.8 5.0 %collective-permute-start.11 = (f32[8,896]{1,0:T(8,128)S(1)}, f32[8,896]{1,0:T(8,128)S(1)}, u32[]{:S(2)}, u32[]{:S(2)}) collective-permute-start(f32[8,896]{1,0:T(8,128)S(1)} %add.18.refs_2_), channel_id=1, source_target_pairs={{0,4},{1,5},{2,6},{3,7},{4,0},{5,1},{6,2},{7,3},{8,12},{9,13},{10,... | collective-permute-start | bytes 86024 | tf_op jit(solution)/shard_map/ppermute | solution.py:26
  61.8 2.4 %copy-start.16 = (s32[2]{0:T(128)S(1)}, s32[2]{0:T(128)}, u32[]{:S(2)}) copy-start(s32[2]{0:T(128)} %pad_add_fusion.where.refs_0_) | copy-start | bytes 28
  61.9 2.2 %copy-start.7 = (bf16[896,448]{1,0:T(8,128)(2,1)}, bf16[896,448]{1,0:T(8,128)(2,1)S(1)}, u32[]{:S(2)}) copy-start(bf16[896,448]{1,0:T(8,128)(2,1)S(1)} %shard_map.112.spread.refs_0_) | copy-start | bytes 2408452
  62.6 1.5 %collective-permute-start.10 = (bf16[64,2048]{1,0:T(8,128)(2,1)S(1)}, bf16[64,2048]{1,0:T(8,128)(2,1)S(1)}, u32[]{:S(2)}, u32[]{:S(2)}) collective-permute-start(bf16[64,2048]{1,0:T(8,128)(2,1)S(1)} %get-tuple-element.59), channel_id=1, source_target_pairs={{0,8},{8,0},{16,24},{24,16},{1,9},{9,1},{17,25},{25,17},{2,10},{10... | collective-permute-start | bytes 786440 | tf_op jit(solution)/shard_map/ppermute | solution.py:26
  64.2 2.3 %copy-start.5 = (bf16[128,2048]{1,0:T(8,128)(2,1)}, bf16[128,2048]{1,0:T(8,128)(2,1)S(1)}, u32[]{:S(2)}) copy-start(bf16[128,2048]{1,0:T(8,128)(2,1)S(1)} %constant_dynamic-update-slice_fusion.4.right) | copy-start | bytes 1572868
  65.5 1.0 copy-start.1
  77.7 10.6 %copy-start.2 = (bf16[4096,128]{1,0:T(8,128)(2,1)S(1)}, bf16[4096,128]{1,0:T(8,128)(2,1)}, u32[]{:S(2)}) copy-start(bf16[4096,128]{1,0:T(8,128)(2,1)} %copy-done.1) | copy-start | bytes 3145732
  77.7 10.6 %copy-start.4 = (bf16[448,2048]{1,0:T(8,128)(2,1)S(1)}, bf16[448,2048]{1,0:T(8,128)(2,1)}, u32[]{:S(2)}) copy-start(bf16[448,2048]{1,0:T(8,128)(2,1)} %copy-done.3) | copy-start | bytes 5505028
  77.7 10.6 %copy-start.6 = (bf16[128,2048]{1,0:T(8,128)(2,1)S(1)}, bf16[128,2048]{1,0:T(8,128)(2,1)}, u32[]{:S(2)}) copy-start(bf16[128,2048]{1,0:T(8,128)(2,1)} %copy-done.5) | copy-start | bytes 1572868
  77.7 10.6 %copy-start.8 = (bf16[896,448]{1,0:T(8,128)(2,1)S(1)}, bf16[896,448]{1,0:T(8,128)(2,1)}, u32[]{:S(2)}) copy-start(bf16[896,448]{1,0:T(8,128)(2,1)} %copy-done.7) | copy-start | bytes 2408452
  88.3 3.1 %copy-start = (bf16[896,4096]{1,0:T(8,128)(2,1)S(1)}, bf16[896,4096]{1,0:T(8,128)(2,1)}, u32[]{:S(2)}) copy-start(bf16[896,4096]{1,0:T(8,128)(2,1)} %tok.17) | copy-start | bytes 22020100
  91.5 0.7 copy-start.17
  99.1 1.0 copy-start.13
  99.7 5.5 %collective-permute-start.15 = (bf16[2304,512]{1,0:T(8,128)(2,1)}, bf16[2304,512]{1,0:T(8,128)(2,1)S(1)}, u32[]{:S(2)}, u32[]{:S(2)}) collective-permute-start(bf16[2304,512]{1,0:T(8,128)(2,1)} %get-tuple-element.69.wt), channel_id=1, source_target_pairs={{0,8},{8,0},{16,24},{24,16},{1,9},{9,1},{17,25},{25,17},{2,10},{10... | collective-permute-start | bytes 7077896 | tf_op jit(solution)/shard_map/ppermute | solution.py:26
  100.2 14.0 %collective-permute-start.12 = (bf16[512,512]{1,0:T(8,128)(2,1)S(1)}, bf16[512,512]{1,0:T(8,128)(2,1)S(1)}, u32[]{:S(2)}, u32[]{:S(2)}) collective-permute-start(bf16[512,512]{1,0:T(8,128)(2,1)S(1)} %copy-done.13), channel_id=1, source_target_pairs={{0,16},{8,24},{16,0},{24,8},{1,17},{9,25},{17,1},{25,9},{2,18},{10... | collective-permute-start | bytes 1572872 | tf_op jit(solution)/shard_map/ppermute | solution.py:386
  114.7 1.9 %collective-permute-start.16 = (bf16[512,512]{1,0:T(8,128)(2,1)S(1)}, bf16[512,512]{1,0:T(8,128)(2,1)S(1)}, u32[]{:S(2)}, u32[]{:S(2)}) collective-permute-start(bf16[512,512]{1,0:T(8,128)(2,1)S(1)} %get-tuple-element.70.wt), channel_id=1, source_target_pairs={{0,8},{8,0},{16,24},{24,16},{1,9},{9,1},{17,25},{25,17},{2,10},{10... | collective-permute-start | bytes 1572872 | tf_op jit(solution)/shard_map/ppermute | solution.py:26

commit v3 on v2

--- a/solution.py
+++ b/solution.py
@@ -9,7 +9,7 @@
 from jax.sharding import PartitionSpec as P
 
 noise_scale = 0.5
-PIECES = (1, 4, 9, 2)
+PIECES = (5, 9, 2)
 LIMIT = 20 * 2**20
 WIDE = 58 * 2**20
 
@@ -18,8 +18,8 @@
     return pltpu.CompilerParams(dimension_semantics=("arbitrary",), vmem_limit_bytes=limit)
 
 
-def cost():
-    return pl.CostEstimate(flops=1, bytes_accessed=1, transcendentals=0)
+def cost(flops=1, moved=1):
+    return pl.CostEstimate(flops=flops, bytes_accessed=moved, transcendentals=0)
 
 
 def swap(array, axis, bit):
@@ -48,16 +48,21 @@
     refs[mark_at][...] = jnp.zeros(MARK.shape, MARK.dtype)
 
 
-def gate(array, *after):
-    return pl.pallas_call(
-        functools.partial(gate_kernel, len(after) + 2),
-        in_specs=[anywhere()] * (1 + len(after)),
-        out_specs=[anywhere(), vmem()],
-        out_shape=[jax.ShapeDtypeStruct(array.shape, array.dtype), MARK],
-        input_output_aliases={0: 0},
+def gate_all(arrays, *after):
+    count = len(arrays)
+    return pl.pallas_call(
+        functools.partial(gate_kernel, 2 * count + len(after)),
+        in_specs=[anywhere()] * (count + len(after)),
+        out_specs=[anywhere()] * count + [vmem()],
+        out_shape=[jax.ShapeDtypeStruct(array.shape, array.dtype) for array in arrays] + [MARK],
+        input_output_aliases={index: index for index in range(count)},
         compiler_params=pltpu.CompilerParams(vmem_limit_bytes=2**20),
         cost_estimate=cost(),
-    )(array, *after)
+    )(*arrays, *after)
+
+
+def gate(array, *after):
+    return gate_all([array], *after)
 
 
 def cut_kernel(start, wt, after, out, mark, sem):
@@ -75,7 +80,7 @@
         out_shape=[jax.ShapeDtypeStruct((depth, weight.shape[1]), weight.dtype), MARK],
         scratch_shapes=[pltpu.SemaphoreType.DMA],
         compiler_params=pltpu.CompilerParams(vmem_limit_bytes=WIDE - 2 * depth * weight.shape[1]),
-        cost_estimate=cost(),
+        cost_estimate=cost(1, 8 * depth * weight.shape[1]),
     )(weight, after)
 
 
@@ -177,8 +182,17 @@
         ),
         out_shape=jax.ShapeDtypeStruct((2 * rank, rows), jnp.float32),
         compiler_params=params(WIDE),
-        cost_estimate=cost(),
+        cost_estimate=cost(2 * rows * slab * lefts.shape[0], 8 * rows * slab),
     )(where, lefts, tokens, after)
+
+
+def flipped(index, size):
+    got = index * 0
+    bit = 1
+    while bit < size:
+        got = got * 2 + ((index // bit) & 1)
+        bit *= 2
+    return got
 
 
 def turn_kernel(where, left, out):
@@ -192,7 +206,7 @@
         grid_spec=pltpu.PrefetchScalarGridSpec(
             num_scalar_prefetch=1,
             grid=(blocks,),
-            in_specs=[pl.BlockSpec((None, sels, slab), lambda k, at: (k ^ at[1], 0, 0))],
+            in_specs=[pl.BlockSpec((None, sels, slab), lambda k, at: (flipped(k ^ at[1], blocks), 0, 0))],
             out_specs=pl.BlockSpec((slab, sels), lambda k, at: (k, 0)),
         ),
         out_shape=jax.ShapeDtypeStruct((blocks * slab, sels), left.dtype),
@@ -386,44 +400,37 @@
         return lax.ppermute(piece, "pop", turn)
 
     factor = 1.0 / math.sqrt(depth * rank * count * groups)
-    piece, mark = cut(weight, *plan[0][1:], selected)
-    arrived = [send(0, piece)]
     packed, left, right, mark = pick(
-        factor, selected, shaping, old_left, old_right, width, mark
+        factor, selected, shaping, old_left, old_right, width, selected
     )
     packed = send(0, packed)
-    piece, mark = cut(weight, *plan[1][1:], mark)
-    arrived.append(send(1, piece))
+    piece, mark = cut(weight, *plan[0][1:], mark)
+    arrived = [send(0, piece)]
     tall = count * rank
+    sibling, mark = gate(swap(weight, "pop", 1), mark)
     lefts, rights = unpack(packed, tall, slab, old_right.shape[2])
     left, right = jnp.concatenate([left, lefts], 0), jnp.concatenate([right, rights], 0)
     for bit in bits(chips, 2):
         left = jnp.concatenate([left, swap(left, "pop", bit)], 0)
         right = jnp.concatenate([right, swap(right, "pop", bit)], 0)
     left, mark = gate(left[None], mark)
-    sibling = swap(weight, "pop", 1)
     rights = new_right.reshape(members * rank, -1)
     proj = project(tokens, new_left.reshape(-1, slab), rank, each, where, mark)
-    piece, mark = cut(weight, *plan[2][1:], mark)
-    spare, ready = cut(weight, *plan[3][1:], mark)
-    for turns, bit in enumerate(bits(lax.axis_size("col"))):
+    piece, early = cut(weight, *plan[1][1:], mark)
+    arrived.append(send(1, piece))
+    turns = list(bits(lax.axis_size("col")))[::-1]
+    for turn_at, bit in enumerate(turns):
         left = jnp.concatenate([left, swap(left, "col", bit)], 0)
-        if turns == 0:
-            arrived[0], mark = gate(arrived[0], left)
-            piece, mark = gate(piece, mark)
-            arrived.append(send(2, piece))
-            right, _ = gate(right, mark)
+        partial = proj
+        proj = proj + swap(proj, "col", bit)
+        if turn_at == 0:
+            left, right, mark = gate_all([left, right], early, partial)
             right = jnp.concatenate([right, swap(right, "pop", 1)], 0)
-            sibling, mark = gate(sibling, mark)
-            left, mark = gate(left, mark, proj, ready)
-        elif bit * 2 < lax.axis_size("col"):
-            left, _ = gate(left, proj)
-        else:
-            arrived[1], mark = gate(arrived[1], left, proj)
-            spare, mark = gate(spare, mark)
-            arrived.append(send(3, spare))
-            left, _ = gate(left, mark, rights)
-        proj = proj + swap(proj, "col", bit)
+            spare, ready = cut(weight, *plan[2][1:], mark)
+        elif turn_at < len(turns) - 1:
+            left, mark = gate(left, partial)
+    left, arrived[0], spare, mark = gate_all([left, arrived[0], spare], partial, rights, ready)
+    arrived.append(send(2, spare))
     left = turn(jnp.concatenate([left, swap(left, "pop", 1)], 1), where)
     spread = spread_out(proj, members, rank, each)
 
@@ -452,7 +459,7 @@
     many = [index for index, part in enumerate(plan) if part[0] == hops[-1]][:-2]
     for index, (hop, start, size) in enumerate(plan):
         part = arrived[index]
-        if index > 1:
+        if index > 0:
             part, mark = gate(part, done)
             arrived[index] = part
             if index + 2 < len(plan):

time: 119 us -> 111 us (0.933)
  waiting for transfers between devices: 24 us -> 17.1 us
  Pallas kernels: 59.3 us -> 55.6 us
  other arithmetic: 1.82 us -> 5.45 us
  local copies, waits for them, and re-layouts: 16.6 us -> 13.8 us
    ppermute x12, waiting for transfers between devices: 17.1 us -> 6.68 us  [swap(): lax.ppermute(array, axis, [(i, i ^ bit) for i in range(lax.axis_size(axis...]
    ppermute x5 -> x4, waiting for transfers between devices: 6.86 us -> 10.4 us  [send(): return lax.ppermute(piece, 'pop', turn)]
    concatenate x1 -> x3, other arithmetic: 0.03 us -> 2.61 us  [local(): left = jnp.concatenate([left, swap(left, 'col', bit)], 0)]
    ppermute x12, starting transfers between devices: 8.75 us -> 10.4 us  [swap(): lax.ppermute(array, axis, [(i, i ^ bit) for i in range(lax.axis_size(axis...]
    pallas_call x8, Pallas kernels: 39.6 us -> 38.3 us  [call(): pl.pallas_call(kernel, grid_spec=pltpu.PrefetchScalarGridSpec(num_scalar_...]
    pallas_call x12 -> x7, Pallas kernels: 3.62 us -> 2.38 us  [gate_all(): pl.pallas_call(functools.partial(gate_kernel, 2 * count + len(after)), in...]
    pallas_call x4 -> x3, Pallas kernels: 8.8 us -> 7.66 us  [cut(): pl.pallas_call(functools.partial(cut_kernel, start), in_specs=[anywhere()...]
    unnamed x54 -> x47, local copies, waits for them, and re-layouts: 11 us -> 9.97 us
  transfers between devices with their start and end apart: 17 -> 16, of which waited for: 8 -> 7; matrix products, arithmetic and copies ran while one was open for 7% -> 8% of each run, Pallas kernels for 48% -> 48%
where the time goes in v3:
time: 111 us; the launch traced here: 110 us
  Pallas kernels  55.6 us (50%)
  waiting for transfers between devices  17.1 us (15%)
  starting transfers between devices  16.6 us (15%)
  local copies, waits for them, and re-layouts  13.8 us (12%)
  other arithmetic  5.45 us (5%)
  between operations  1.14 us (1%)
    pallas_call x8, Pallas kernels, call(): pl.pallas_call(kernel, grid_spec=pltpu.PrefetchScalarGridSpec(num_scalar_...  38.3 us
    ppermute x12, starting transfers between devices, swap(): lax.ppermute(array, axis, [(i, i ^ bit) for i in range(lax.axis_size(axis...  10.4 us
    ppermute x4, waiting for transfers between devices, send(): return lax.ppermute(piece, 'pop', turn)  10.4 us
    unnamed x47, local copies, waits for them, and re-layouts  9.97 us
    pallas_call x3, Pallas kernels, cut(): pl.pallas_call(functools.partial(cut_kernel, start), in_specs=[anywhere()...  7.66 us
    ppermute x12, waiting for transfers between devices, swap(): lax.ppermute(array, axis, [(i, i ^ bit) for i in range(lax.axis_size(axis...  6.68 us
    ppermute x4, starting transfers between devices, send(): return lax.ppermute(piece, 'pop', turn)  6.22 us
    pallas_call x1, Pallas kernels, project(): pl.pallas_call(functools.partial(proj_kernel, rank, each), grid_spec=pltp...  3.27 us
  transfers between devices with their start and end apart: 16, of which 7 were waited for; matrix products, arithmetic and copies ran while one was open for 8% of the time, Pallas kernels for 48%

profile of v3, /device:TPU:0, one launch (start us, length us, event | category | flops | bytes accessed | tf_op | source)
XLA Modules:
  0.0 109.7 jit_solution(7355929395308330890)
XLA Ops:
  1.1 2.4 %shard_map.95 = (bf16[160,512]{1,0:T(8,128)(2,1)}, bf16[32,512]{1,0:T(8,128)(2,1)}, bf16[32,2048]{1,0:T(8,128)(2,1)}, f32[8,128]{1,0:T(8,128)}) custom-call(s32[1,8]{1,0:T(1,128)} %after.1, f32[1,8]{1,0:T(1,128)} %shaping.1, bf16[112,4,512]{2,1,0:T(4,128)(2,1)} %lefts.1, bf16[112,4,2048]{2,1,0:T(4,128)(2,1)} %rights.1, s32[1,8]{1,0:T(1,128)} %after.1), custom_call_target="tpu_custom_call" | custom-call | flops 1 | bytes 1 | tf_op jit(solution)/shard_map/pallas_call | solution.py:123
  3.6 2.6 %collective-permute-start = (bf16[160,512]{1,0:T(8,128)(2,1)}, bf16[160,512]{1,0:T(8,128)(2,1)S(1)}, u32[]{:S(2)}, u32[]{:S(2)}) collective-permute-start(bf16[160,512]{1,0:T(8,128)(2,1)} %get-tuple-element.31), channel_id=1, source_target_pairs={{0,16},{8,24},{16,0},{24,8},{1,17},{9,25},{17,1},{25,9},{2,18},{10... | collective-permute-start | bytes 491528 | tf_op jit(solution)/shard_map/ppermute | solution.py:400
  6.2 2.4 %shard_map.96 = (bf16[1280,512]{1,0:T(8,128)(2,1)}, f32[8,128]{1,0:T(8,128)}) custom-call(bf16[4096,512]{1,0:T(8,128)(2,1)} %wt.7, f32[8,128]{1,0:T(8,128)} %get-tuple-element.32.after), custom_call_target="tpu_custom_call" | custom-call | flops 1 | bytes 5242880 | tf_op jit(solution)/shard_map/pallas_call | solution.py:76
  8.7 2.6 %collective-permute-done = bf16[160,512]{1,0:T(8,128)(2,1)S(1)} collective-permute-done((bf16[160,512]{1,0:T(8,128)(2,1)}, bf16[160,512]{1,0:T(8,128)(2,1)S(1)}, u32[]{:S(2)}, u32[]{:S(2)}) %collective-permute-start) | collective-permute-done | bytes 163872 | tf_op jit(solution)/shard_map/ppermute | solution.py:400
  11.3 0.7 copy-done.16
  12.0 0.6 copy-done.13
  12.6 3.2 %shard_map.99 = (bf16[2304,512]{1,0:T(8,128)(2,1)}, f32[8,128]{1,0:T(8,128)}) custom-call(bf16[4096,512]{1,0:T(8,128)(2,1)} %wt.7, f32[8,128]{1,0:T(8,128)} %copy-done.13), custom_call_target="tpu_custom_call" | custom-call | flops 1 | bytes 9437184 | tf_op jit(solution)/shard_map/pallas_call | solution.py:76
  15.8 2.2 %collective-permute-start.12 = (bf16[2304,512]{1,0:T(8,128)(2,1)}, bf16[2304,512]{1,0:T(8,128)(2,1)}, u32[]{:S(2)}, u32[]{:S(2)}) collective-permute-start(bf16[2304,512]{1,0:T(8,128)(2,1)} %get-tuple-element.49), channel_id=1, source_target_pairs={{0,16},{8,24},{16,0},{24,8},{1,17},{9,25},{17,1},{25,9},{2,18},{10... | collective-permute-start | bytes 7077896 | tf_op jit(solution)/shard_map/ppermute | solution.py:400
  18.0 0.6 pad_add_fusion.where.refs_0_
  18.6 0.9 reshape.27.left
  19.5 2.6 %collective-permute-start.2 = (bf16[1,64,512]{2,1,0:T(8,128)(2,1)S(1)}, bf16[1,64,512]{2,1,0:T(8,128)(2,1)S(1)}, u32[]{:S(2)}, u32[]{:S(2)}) collective-permute-start(bf16[1,64,512]{2,1,0:T(8,128)(2,1)S(1)} %get-tuple-element.35), channel_id=1, source_target_pairs={{0,4},{1,5},{2,6},{3,7},{4,0},{5,1},{6,2},{7,3},{8,12},{9,13},{10,... | collective-permute-start | bytes 196616 | tf_op jit(solution)/shard_map/ppermute | solution.py:26
  22.1 3.3 %shard_map.100.refs_3_ = f32[8,896]{1,0:T(8,128)} custom-call(s32[2]{0:T(128)} %pad_add_fusion.where.refs_0_, bf16[448,512]{1,0:T(8,128)(2,1)} %reshape.27.left, bf16[896,4096]{1,0:T(8,128)(2,1)} %tok.17, f32[8,128]{1,0:T(8,128)} %copy-done.13), custom_call_target="tpu_custom_call" | custom-call | flops 411041792 | bytes 3670016 | tf_op jit(solution)/shard_map/pallas_call | solution.py:171
  25.4 0.7 copy-done.12
  26.2 0.6 copy-done.15
  26.8 1.6 %collective-permute-start.3 = (bf16[2,64,512]{2,1,0:T(8,128)(2,1)S(1)}, bf16[2,64,512]{2,1,0:T(8,128)(2,1)S(1)}, u32[]{:S(2)}, u32[]{:S(2)}) collective-permute-start(bf16[2,64,512]{2,1,0:T(8,128)(2,1)S(1)} %get-tuple-element.39), channel_id=1, source_target_pairs={{0,2},{1,3},{2,0},{3,1},{4,6},{5,7},{6,4},{7,5},{8,10},{9,11},{10,... | collective-permute-start | bytes 393224 | tf_op jit(solution)/shard_map/ppermute | solution.py:26
  28.4 2.4 %collective-permute-start.4 = (f32[8,896]{1,0:T(8,128)}, f32[8,896]{1,0:T(8,128)S(1)}, u32[]{:S(2)}, u32[]{:S(2)}) collective-permute-start(f32[8,896]{1,0:T(8,128)} %shard_map.100.refs_3_), channel_id=1, source_target_pairs={{0,4},{1,5},{2,6},{3,7},{4,0},{5,1},{6,2},{7,3},{8,12},{9,13},{10,... | collective-permute-start | bytes 86024 | tf_op jit(solution)/shard_map/ppermute | solution.py:26
  30.8 2.8 %collective-permute-done.4 = f32[8,896]{1,0:T(8,128)S(1)} collective-permute-done((f32[8,896]{1,0:T(8,128)}, f32[8,896]{1,0:T(8,128)S(1)}, u32[]{:S(2)}, u32[]{:S(2)}) %collective-permute-start.4) | collective-permute-done | bytes 28704 | tf_op jit(solution)/shard_map/ppermute | solution.py:26
  33.6 0.8 add.17.refs_1_
  34.4 0.7 pad_maximum_fusion.2.refs_0_
  35.1 0.6 shard_map.102
  35.7 1.5 %collective-permute-start.5 = (bf16[4,64,512]{2,1,0:T(8,128)(2,1)}, bf16[4,64,512]{2,1,0:T(8,128)(2,1)}, u32[]{:S(2)}, u32[]{:S(2)}) collective-permute-start(bf16[4,64,512]{2,1,0:T(8,128)(2,1)} %get-tuple-element.40), channel_id=1, source_target_pairs={{0,1},{1,0},{2,3},{3,2},{4,5},{5,4},{6,7},{7,6},{8,9},{9,8},{10,11... | collective-permute-start | bytes 786440 | tf_op jit(solution)/shard_map/ppermute | solution.py:26
  37.7 2.9 %reshape.28.refs_4_.rights.refs_1_ = bf16[448,2048]{1,0:T(8,128)(2,1)S(1)} reshape(bf16[112,4,2048]{2,1,0:T(4,128)(2,1)} %param.15) | data formatting | bytes 3670016 | tf_op jit(solution)/shard_map/reshape | solution.py:417
  41.1 2.0 %shard_map.103 = (bf16[512,512]{1,0:T(8,128)(2,1)}, f32[8,128]{1,0:T(8,128)}) custom-call(bf16[4096,512]{1,0:T(8,128)(2,1)} %wt.7, f32[8,128]{1,0:T(8,128)} %copy-done.15), custom_call_target="tpu_custom_call" | custom-call | flops 1 | bytes 2097152 | tf_op jit(solution)/shard_map/pallas_call | solution.py:76
  43.2 1.9 %pad_maximum_fusion.1.refs_0_ = bf16[8,64,512]{2,1,0:T(8,128)(2,1)} fusion(bf16[4,64,512]{2,1,0:T(8,128)(2,1)} %collective-permute-done.5, bf16[4,64,512]{2,1,0:T(8,128)(2,1)} %get-tuple-element.40), kind=kLoop, calls=%fused_computation.1 | loop fusion | flops 262144 | bytes 1048576 | tf_op jit(solution)/shard_map/concatenate | solution.py:423
  45.0 1.0 copy-done.9
  46.1 0.7 copy-done.19
  46.8 0.6 shard_map.104
  47.4 0.8 copy-done.10
  48.7 0.7 collective-permute-start.10
  49.4 3.1 %collective-permute-done.10 = f32[8,896]{1,0:T(8,128)S(1)} collective-permute-done((f32[8,896]{1,0:T(8,128)S(1)}, f32[8,896]{1,0:T(8,128)S(1)}, u32[]{:S(2)}, u32[]{:S(2)}) %collective-permute-start.10) | collective-permute-done | bytes 28704 | tf_op jit(solution)/shard_map/ppermute | solution.py:26
  52.7 1.5 %pad_maximum_fusion.left = bf16[8,128,512]{2,1,0:T(8,128)(2,1)S(1)} fusion(bf16[8,64,512]{2,1,0:T(8,128)(2,1)S(1)} %collective-permute-done.8, bf16[8,64,512]{2,1,0:T(8,128)(2,1)} %get-tuple-element.45), kind=kLoop, calls=%fused_computation | loop fusion | flops 2097152 | bytes 2097152 | tf_op jit(solution)/shard_map/concatenate | solution.py:434
  54.2 1.4 %shard_map.105.left = bf16[4096,128]{1,0:T(8,128)(2,1)S(1)} custom-call(s32[2]{0:T(128)S(1)} %copy-done.14, bf16[8,128,512]{2,1,0:T(8,128)(2,1)S(1)} %pad_maximum_fusion.left), custom_call_target="tpu_custom_call" | custom-call | flops 1 | bytes 1 | tf_op jit(solution)/shard_map/pallas_call | solution.py:204
  55.7 1.0 copy-done.1
  56.7 11.3 %shard_map.107 = (bf16[896,2048]{1,0:T(8,128)(2,1)}, bf16[4096,512]{1,0:T(8,128)(2,1)}, f32[8,128]{1,0:T(8,128)}) custom-call(s32[1]{0:T(128)} %bitcast.where, bf16[896,4096]{1,0:T(8,128)(2,1)} %tok.17, bf16[4096,512]{1,0:T(8,128)(2,1)} %wt.7, bf16[4096,128]{1,0:T(8,128)(2,1)} %copy-done.1, bf16[128,2048]{1,0:T(8,128)(2,1)} %copy-done.5, ...), custom_call_target="tpu_custom_call" | custom-call | flops 1 | bytes 1 | tf_op jit(solution)/shard_map/pallas_call | solution.py:309
  68.0 10.6 %shard_map.108 = (bf16[896,2048]{1,0:T(8,128)(2,1)}, f32[8,128]{1,0:T(8,128)}) custom-call(s32[1]{0:T(128)} %bitcast.5.where, bf16[896,4096]{1,0:T(8,128)(2,1)} %tok.17, bf16[4096,512]{1,0:T(8,128)(2,1)} %get-tuple-element.51.wt, bf16[4096,128]{1,0:T(8,128)(2,1)} %copy-done.1, bf16[128,2048]{1,0:T(8,128)(2,1)} %copy-done.5, ...), custom_call_target="tpu_custom_call", output_to_operand_aliasing={{0}: (8, {})} | custom-call | flops 1 | bytes 1 | tf_op jit(solution)/shard_map/pallas_call | solution.py:309
  78.6 3.1 %copy-done = bf16[896,4096]{1,0:T(8,128)(2,1)S(1)} copy-done((bf16[896,4096]{1,0:T(8,128)(2,1)S(1)}, bf16[896,4096]{1,0:T(8,128)(2,1)}, u32[]{:S(2)}) %copy-start) | copy-done | bytes 7340056
  81.7 0.7 copy-done.17
  82.4 2.2 %shard_map.109.refs_2_.refs_0_ = f32[896,512]{1,0:T(8,128)S(1)} custom-call(s32[1]{0:T(128)} %bitcast.4.where, bf16[896,4096]{1,0:T(8,128)(2,1)S(1)} %copy-done, bf16[1280,512]{1,0:T(8,128)(2,1)S(1)} %get-tuple-element.50.wt, bf16[4096,128]{1,0:T(8,128)(2,1)S(1)} %copy-done.2, bf16[128,2048]{1,0:T(8,128)(2,1)S(1)} %copy-done.6, ...), custom_call_target="tpu_custom_call" | custom-call | flops 1 | bytes 1 | tf_op jit(solution)/shard_map/pallas_call | solution.py:309
  84.6 3.5 %shard_map.110.refs_1_.refs_0_ = f32[896,512]{1,0:T(8,128)S(1)} custom-call(s32[1]{0:T(128)} %bitcast.3.where, bf16[896,4096]{1,0:T(8,128)(2,1)S(1)} %copy-done, bf16[1280,512]{1,0:T(8,128)(2,1)} %collective-permute-done.13.wt, bf16[4096,128]{1,0:T(8,128)(2,1)S(1)} %copy-done.2, bf16[128,2048]{1,0:T(8,128)(2,1)S(1)} %copy-done.6, ...), custom_call_target="tpu_custom_call" | custom-call | flops 1 | bytes 1 | tf_op jit(solution)/shard_map/pallas_call | solution.py:309
  88.1 2.4 %collective-permute-done.12.refs_0_ = bf16[2304,512]{1,0:T(8,128)(2,1)} collective-permute-done((bf16[2304,512]{1,0:T(8,128)(2,1)}, bf16[2304,512]{1,0:T(8,128)(2,1)}, u32[]{:S(2)}, u32[]{:S(2)}) %collective-permute-start.12) | collective-permute-done | bytes 2359328 | tf_op jit(solution)/shard_map/ppermute | solution.py:400
  90.4 0.6 shard_map.111
  91.0 1.3 %collective-permute-start.11 = (bf16[512,512]{1,0:T(8,128)(2,1)S(1)}, bf16[512,512]{1,0:T(8,128)(2,1)S(1)}, u32[]{:S(2)}, u32[]{:S(2)}) collective-permute-start(bf16[512,512]{1,0:T(8,128)(2,1)S(1)} %copy-done.11), channel_id=1, source_target_pairs={{0,16},{8,24},{16,0},{24,8},{1,17},{9,25},{17,1},{25,9},{2,18},{10... | collective-permute-start | bytes 1572872 | tf_op jit(solution)/shard_map/ppermute | solution.py:400
  92.4 4.6 %shard_map.112.refs_1_.before = f32[896,512]{1,0:T(8,128)S(1)} custom-call(s32[1]{0:T(128)} %bitcast.4.where, bf16[896,4096]{1,0:T(8,128)(2,1)S(1)} %copy-done, bf16[2304,512]{1,0:T(8,128)(2,1)} %get-tuple-element.55.wt, bf16[4096,128]{1,0:T(8,128)(2,1)S(1)} %copy-done.2, bf16[128,2048]{1,0:T(8,128)(2,1)S(1)} %copy-done.6, ...), custom_call_target="tpu_custom_call", output_to_operand_aliasing={{}: (5, {})} | custom-call | flops 1 | bytes 1 | tf_op jit(solution)/shard_map/pallas_call | solution.py:309
  97.0 2.9 %shard_map.113.refs_1_.before = f32[896,512]{1,0:T(8,128)S(1)} custom-call(s32[1]{0:T(128)} %bitcast.3.where, bf16[896,4096]{1,0:T(8,128)(2,1)S(1)} %copy-done, bf16[2304,512]{1,0:T(8,128)(2,1)S(1)} %collective-permute-done.14.wt, bf16[4096,128]{1,0:T(8,128)(2,1)S(1)} %copy-done.2, bf16[128,2048]{1,0:T(8,128)(2,1)S(1)} %copy-done.6, ...), custom_call_target="tpu_custom_call", output_to_operand_aliasing={{}: (5, {})} | custom-call | flops 1 | bytes 1 | tf_op jit(solution)/shard_map/pallas_call | solution.py:309
  99.9 5.4 %collective-permute-done.11.refs_0_ = bf16[512,512]{1,0:T(8,128)(2,1)S(1)} collective-permute-done((bf16[512,512]{1,0:T(8,128)(2,1)S(1)}, bf16[512,512]{1,0:T(8,128)(2,1)S(1)}, u32[]{:S(2)}, u32[]{:S(2)}) %collective-permute-start.11) | collective-permute-done | bytes 524320 | tf_op jit(solution)/shard_map/ppermute | solution.py:400
  105.4 0.6 shard_map.114
  106.0 1.6 %shard_map.115.acts = bf16[896,2048]{1,0:T(8,128)(2,1)} custom-call(s32[1]{0:T(128)} %bitcast.4.where, bf16[896,4096]{1,0:T(8,128)(2,1)S(1)} %copy-done, bf16[512,512]{1,0:T(8,128)(2,1)S(1)} %get-tuple-element.56.wt, bf16[4096,128]{1,0:T(8,128)(2,1)S(1)} %copy-done.2, bf16[128,2048]{1,0:T(8,128)(2,1)S(1)} %copy-done.6, ...), custom_call_target="tpu_custom_call", output_to_operand_aliasing={{}: (6, {})} | custom-call | flops 1 | bytes 1 | tf_op jit(solution)/shard_map/pallas_call | solution.py:309
  107.9 1.6 %shard_map.116 = bf16[896,2048]{1,0:T(8,128)(2,1)} custom-call(s32[1]{0:T(128)} %bitcast.3.where, bf16[896,4096]{1,0:T(8,128)(2,1)S(1)} %copy-done, bf16[512,512]{1,0:T(8,128)(2,1)S(1)} %collective-permute-done.15.wt, bf16[4096,128]{1,0:T(8,128)(2,1)S(1)} %copy-done.2, bf16[128,2048]{1,0:T(8,128)(2,1)S(1)} %copy-done.6, ...), custom_call_target="tpu_custom_call", output_to_operand_aliasing={{}: (6, {})} | custom-call | flops 1 | bytes 1 | tf_op jit(solution)/shard_map/pallas_call | solution.py:309
  (67 shorter events, 2.7 us)
Async XLA Ops:
  0.6 10.7 %collective-permute-start.1 = (bf16[4096,512]{1,0:T(8,128)(2,1)}, bf16[4096,512]{1,0:T(8,128)(2,1)}, u32[]{:S(2)}, u32[]{:S(2)}) collective-permute-start(bf16[4096,512]{1,0:T(8,128)(2,1)} %wt.7), channel_id=1, source_target_pairs={{0,8},{8,0},{16,24},{24,16},{1,9},{9,1},{17,25},{25,17},{2,10},{10... | collective-permute-start | bytes 12582920 | tf_op jit(solution)/shard_map/ppermute | solution.py:26
  3.6 7.7 %collective-permute-start = (bf16[160,512]{1,0:T(8,128)(2,1)}, bf16[160,512]{1,0:T(8,128)(2,1)S(1)}, u32[]{:S(2)}, u32[]{:S(2)}) collective-permute-start(bf16[160,512]{1,0:T(8,128)(2,1)} %get-tuple-element.31), channel_id=1, source_target_pairs={{0,16},{8,24},{16,0},{24,8},{1,17},{9,25},{17,1},{25,9},{2,18},{10... | collective-permute-start | bytes 491528 | tf_op jit(solution)/shard_map/ppermute | solution.py:400
  6.2 5.1 %copy-start.22 = (bf16[32,512]{1,0:T(8,128)(2,1)S(1)}, bf16[32,512]{1,0:T(8,128)(2,1)}, u32[]{:S(2)}) copy-start(bf16[32,512]{1,0:T(8,128)(2,1)} %get-tuple-element.30) | copy-start | bytes 98308
  8.6 36.4 %collective-permute-start.6 = (bf16[1280,512]{1,0:T(8,128)(2,1)}, bf16[1280,512]{1,0:T(8,128)(2,1)S(1)}, u32[]{:S(2)}, u32[]{:S(2)}) collective-permute-start(bf16[1280,512]{1,0:T(8,128)(2,1)} %get-tuple-element.41), channel_id=1, source_target_pairs={{0,16},{8,24},{16,0},{24,8},{1,17},{9,25},{17,1},{25,9},{2,18},{10... | collective-permute-start | bytes 3932168 | tf_op jit(solution)/shard_map/ppermute | solution.py:400
  11.3 0.7 copy-start.16
  12.0 0.6 copy-start.13
  12.6 6.0 %copy-start.20 = (bf16[112,4,512]{2,1,0:T(4,128)(2,1)S(1)}, bf16[112,4,512]{2,1,0:T(4,128)(2,1)}, u32[]{:S(2)}) copy-start(bf16[112,4,512]{2,1,0:T(4,128)(2,1)} %param.14) | copy-start | bytes 1376260
  12.6 9.5 %copy-start.21 = (bf16[32,2048]{1,0:T(8,128)(2,1)S(1)}, bf16[32,2048]{1,0:T(8,128)(2,1)}, u32[]{:S(2)}) copy-start(bf16[32,2048]{1,0:T(8,128)(2,1)} %get-tuple-element.36) | copy-start | bytes 393220
  15.8 74.6 %collective-permute-start.12 = (bf16[2304,512]{1,0:T(8,128)(2,1)}, bf16[2304,512]{1,0:T(8,128)(2,1)}, u32[]{:S(2)}, u32[]{:S(2)}) collective-permute-start(bf16[2304,512]{1,0:T(8,128)(2,1)} %get-tuple-element.49), channel_id=1, source_target_pairs={{0,16},{8,24},{16,0},{24,8},{1,17},{9,25},{17,1},{25,9},{2,18},{10... | collective-permute-start | bytes 7077896 | tf_op jit(solution)/shard_map/ppermute | solution.py:400
  19.5 5.9 %collective-permute-start.2 = (bf16[1,64,512]{2,1,0:T(8,128)(2,1)S(1)}, bf16[1,64,512]{2,1,0:T(8,128)(2,1)S(1)}, u32[]{:S(2)}, u32[]{:S(2)}) collective-permute-start(bf16[1,64,512]{2,1,0:T(8,128)(2,1)S(1)} %get-tuple-element.35), channel_id=1, source_target_pairs={{0,4},{1,5},{2,6},{3,7},{4,0},{5,1},{6,2},{7,3},{8,12},{9,13},{10,... | collective-permute-start | bytes 196616 | tf_op jit(solution)/shard_map/ppermute | solution.py:26
  22.1 3.3 %copy-start.18 = (f32[8,128]{1,0:T(8,128)S(1)}, f32[8,128]{1,0:T(8,128)}, u32[]{:S(2)}) copy-start(f32[8,128]{1,0:T(8,128)} %get-tuple-element.38.refs_2_) | copy-start | bytes 12292
  25.4 0.7 copy-start.12
  26.2 0.6 copy-start.15
  26.8 7.6 %collective-permute-start.3 = (bf16[2,64,512]{2,1,0:T(8,128)(2,1)S(1)}, bf16[2,64,512]{2,1,0:T(8,128)(2,1)S(1)}, u32[]{:S(2)}, u32[]{:S(2)}) collective-permute-start(bf16[2,64,512]{2,1,0:T(8,128)(2,1)S(1)} %get-tuple-element.39), channel_id=1, source_target_pairs={{0,2},{1,3},{2,0},{3,1},{4,6},{5,7},{6,4},{7,5},{8,10},{9,11},{10,... | collective-permute-start | bytes 393224 | tf_op jit(solution)/shard_map/ppermute | solution.py:26
  28.4 5.3 %collective-permute-start.4 = (f32[8,896]{1,0:T(8,128)}, f32[8,896]{1,0:T(8,128)S(1)}, u32[]{:S(2)}, u32[]{:S(2)}) collective-permute-start(f32[8,896]{1,0:T(8,128)} %shard_map.100.refs_3_), channel_id=1, source_target_pairs={{0,4},{1,5},{2,6},{3,7},{4,0},{5,1},{6,2},{7,3},{8,12},{9,13},{10,... | collective-permute-start | bytes 86024 | tf_op jit(solution)/shard_map/ppermute | solution.py:26
  35.7 7.4 %collective-permute-start.5 = (bf16[4,64,512]{2,1,0:T(8,128)(2,1)}, bf16[4,64,512]{2,1,0:T(8,128)(2,1)}, u32[]{:S(2)}, u32[]{:S(2)}) collective-permute-start(bf16[4,64,512]{2,1,0:T(8,128)(2,1)} %get-tuple-element.40), channel_id=1, source_target_pairs={{0,1},{1,0},{2,3},{3,2},{4,5},{5,4},{6,7},{7,6},{8,9},{9,8},{10,11... | collective-permute-start | bytes 786440 | tf_op jit(solution)/shard_map/ppermute | solution.py:26
  37.2 3.9 %collective-permute-start.7 = (f32[8,896]{1,0:T(8,128)S(1)}, f32[8,896]{1,0:T(8,128)S(1)}, u32[]{:S(2)}, u32[]{:S(2)}) collective-permute-start(f32[8,896]{1,0:T(8,128)S(1)} %add.17.refs_1_), channel_id=1, source_target_pairs={{0,2},{1,3},{2,0},{3,1},{4,6},{5,7},{6,4},{7,5},{8,10},{9,11},{10,... | collective-permute-start | bytes 86024 | tf_op jit(solution)/shard_map/ppermute | solution.py:26
  40.7 4.4 %copy-start.3 = (bf16[448,2048]{1,0:T(8,128)(2,1)}, bf16[448,2048]{1,0:T(8,128)(2,1)S(1)}, u32[]{:S(2)}) copy-start(bf16[448,2048]{1,0:T(8,128)(2,1)S(1)} %reshape.28.refs_4_.rights.refs_1_) | copy-start | bytes 5505028
  45.0 1.0 copy-start.9
  46.1 0.7 copy-start.19
  47.4 0.8 copy-start.10
  48.1 36.4 %collective-permute-start.13 = (bf16[1280,512]{1,0:T(8,128)(2,1)S(1)}, bf16[1280,512]{1,0:T(8,128)(2,1)}, u32[]{:S(2)}, u32[]{:S(2)}) collective-permute-start(bf16[1280,512]{1,0:T(8,128)(2,1)S(1)} %get-tuple-element.50.wt), channel_id=1, source_target_pairs={{0,8},{8,0},{16,24},{24,16},{1,9},{9,1},{17,25},{25,17},{2,10},{10... | collective-permute-start | bytes 3932168 | tf_op jit(solution)/shard_map/ppermute | solution.py:26
  48.1 4.6 %collective-permute-start.8 = (bf16[8,64,512]{2,1,0:T(8,128)(2,1)}, bf16[8,64,512]{2,1,0:T(8,128)(2,1)S(1)}, u32[]{:S(2)}, u32[]{:S(2)}) collective-permute-start(bf16[8,64,512]{2,1,0:T(8,128)(2,1)} %get-tuple-element.45), channel_id=1, source_target_pairs={{0,8},{8,0},{16,24},{24,16},{1,9},{9,1},{17,25},{25,17},{2,10},{10... | collective-permute-start | bytes 1572872 | tf_op jit(solution)/shard_map/ppermute | solution.py:26
  48.7 3.9 %collective-permute-start.10 = (f32[8,896]{1,0:T(8,128)S(1)}, f32[8,896]{1,0:T(8,128)S(1)}, u32[]{:S(2)}, u32[]{:S(2)}) collective-permute-start(f32[8,896]{1,0:T(8,128)S(1)} %add.18.refs_3_), channel_id=1, source_target_pairs={{0,1},{1,0},{2,3},{3,2},{4,5},{5,4},{6,7},{7,6},{8,9},{9,8},{10,11... | collective-permute-start | bytes 86024 | tf_op jit(solution)/shard_map/ppermute | solution.py:26
  49.4 4.8 %copy-start.14 = (s32[2]{0:T(128)S(1)}, s32[2]{0:T(128)}, u32[]{:S(2)}) copy-start(s32[2]{0:T(128)} %pad_add_fusion.where.refs_0_) | copy-start | bytes 28
  49.4 4.8 %collective-permute-start.9 = (bf16[64,2048]{1,0:T(8,128)(2,1)S(1)}, bf16[64,2048]{1,0:T(8,128)(2,1)S(1)}, u32[]{:S(2)}, u32[]{:S(2)}) collective-permute-start(bf16[64,2048]{1,0:T(8,128)(2,1)S(1)} %get-tuple-element.46), channel_id=1, source_target_pairs={{0,8},{8,0},{16,24},{24,16},{1,9},{9,1},{17,25},{25,17},{2,10},{10... | collective-permute-start | bytes 786440 | tf_op jit(solution)/shard_map/ppermute | solution.py:26
  52.7 1.5 %copy-start.7 = (bf16[896,448]{1,0:T(8,128)(2,1)}, bf16[896,448]{1,0:T(8,128)(2,1)S(1)}, u32[]{:S(2)}) copy-start(bf16[896,448]{1,0:T(8,128)(2,1)S(1)} %shard_map.106.spread.refs_0_) | copy-start | bytes 2408452
  54.2 2.4 %copy-start.5 = (bf16[128,2048]{1,0:T(8,128)(2,1)}, bf16[128,2048]{1,0:T(8,128)(2,1)S(1)}, u32[]{:S(2)}) copy-start(bf16[128,2048]{1,0:T(8,128)(2,1)S(1)} %constant_dynamic-update-slice_fusion.right) | copy-start | bytes 1572868
  55.7 1.0 copy-start.1
  67.9 10.6 %copy-start.2 = (bf16[4096,128]{1,0:T(8,128)(2,1)S(1)}, bf16[4096,128]{1,0:T(8,128)(2,1)}, u32[]{:S(2)}) copy-start(bf16[4096,128]{1,0:T(8,128)(2,1)} %copy-done.1) | copy-start | bytes 3145732
  68.0 10.6 %copy-start.4 = (bf16[448,2048]{1,0:T(8,128)(2,1)S(1)}, bf16[448,2048]{1,0:T(8,128)(2,1)}, u32[]{:S(2)}) copy-start(bf16[448,2048]{1,0:T(8,128)(2,1)} %copy-done.3) | copy-start | bytes 5505028
  68.0 10.6 %copy-start.6 = (bf16[128,2048]{1,0:T(8,128)(2,1)S(1)}, bf16[128,2048]{1,0:T(8,128)(2,1)}, u32[]{:S(2)}) copy-start(bf16[128,2048]{1,0:T(8,128)(2,1)} %copy-done.5) | copy-start | bytes 1572868
  68.0 10.6 %copy-start.8 = (bf16[896,448]{1,0:T(8,128)(2,1)S(1)}, bf16[896,448]{1,0:T(8,128)(2,1)}, u32[]{:S(2)}) copy-start(bf16[896,448]{1,0:T(8,128)(2,1)} %copy-done.7) | copy-start | bytes 2408452
  78.6 3.1 %copy-start = (bf16[896,4096]{1,0:T(8,128)(2,1)S(1)}, bf16[896,4096]{1,0:T(8,128)(2,1)}, u32[]{:S(2)}) copy-start(bf16[896,4096]{1,0:T(8,128)(2,1)} %tok.17) | copy-start | bytes 22020100
  81.7 0.7 copy-start.17
  88.1 3.0 %copy-start.11 = (bf16[512,512]{1,0:T(8,128)(2,1)S(1)}, bf16[512,512]{1,0:T(8,128)(2,1)}, u32[]{:S(2)}) copy-start(bf16[512,512]{1,0:T(8,128)(2,1)} %copy-done.10) | copy-start | bytes 1572868
  91.0 5.9 %collective-permute-start.14 = (bf16[2304,512]{1,0:T(8,128)(2,1)}, bf16[2304,512]{1,0:T(8,128)(2,1)S(1)}, u32[]{:S(2)}, u32[]{:S(2)}) collective-permute-start(bf16[2304,512]{1,0:T(8,128)(2,1)} %get-tuple-element.55.wt), channel_id=1, source_target_pairs={{0,8},{8,0},{16,24},{24,16},{1,9},{9,1},{17,25},{25,17},{2,10},{10... | collective-permute-start | bytes 7077896 | tf_op jit(solution)/shard_map/ppermute | solution.py:26
  91.0 14.3 %collective-permute-start.11 = (bf16[512,512]{1,0:T(8,128)(2,1)S(1)}, bf16[512,512]{1,0:T(8,128)(2,1)S(1)}, u32[]{:S(2)}, u32[]{:S(2)}) collective-permute-start(bf16[512,512]{1,0:T(8,128)(2,1)S(1)} %copy-done.11), channel_id=1, source_target_pairs={{0,16},{8,24},{16,0},{24,8},{1,17},{9,25},{17,1},{25,9},{2,18},{10... | collective-permute-start | bytes 1572872 | tf_op jit(solution)/shard_map/ppermute | solution.py:400
  106.0 1.9 %collective-permute-start.15 = (bf16[512,512]{1,0:T(8,128)(2,1)S(1)}, bf16[512,512]{1,0:T(8,128)(2,1)S(1)}, u32[]{:S(2)}, u32[]{:S(2)}) collective-permute-start(bf16[512,512]{1,0:T(8,128)(2,1)S(1)} %get-tuple-element.56.wt), channel_id=1, source_target_pairs={{0,8},{8,0},{16,24},{24,16},{1,9},{9,1},{17,25},{25,17},{2,10},{10... | collective-permute-start | bytes 1572872 | tf_op jit(solution)/shard_map/ppermute | solution.py:26

commit v4 on v3

--- a/solution.py
+++ b/solution.py
@@ -9,7 +9,7 @@
 from jax.sharding import PartitionSpec as P
 
 noise_scale = 0.5
-PIECES = (5, 9, 2)
+PIECES = (1, 5, 9, 1)
 LIMIT = 20 * 2**20
 WIDE = 58 * 2**20
 
@@ -400,14 +400,17 @@
         return lax.ppermute(piece, "pop", turn)
 
     factor = 1.0 / math.sqrt(depth * rank * count * groups)
+    arrived = [send(0, weight[: plan[0][2]])]
     packed, left, right, mark = pick(
         factor, selected, shaping, old_left, old_right, width, selected
     )
     packed = send(0, packed)
-    piece, mark = cut(weight, *plan[0][1:], mark)
-    arrived = [send(0, piece)]
+    piece, mark = cut(weight, *plan[1][1:], mark)
+    arrived.append(send(1, piece))
     tall = count * rank
     sibling, mark = gate(swap(weight, "pop", 1), mark)
+    arrived[0], mark = gate(arrived[0], mark)
+    packed, mark = gate(packed, mark)
     lefts, rights = unpack(packed, tall, slab, old_right.shape[2])
     left, right = jnp.concatenate([left, lefts], 0), jnp.concatenate([right, rights], 0)
     for bit in bits(chips, 2):
@@ -416,21 +419,21 @@
     left, mark = gate(left[None], mark)
     rights = new_right.reshape(members * rank, -1)
     proj = project(tokens, new_left.reshape(-1, slab), rank, each, where, mark)
-    piece, early = cut(weight, *plan[1][1:], mark)
-    arrived.append(send(1, piece))
     turns = list(bits(lax.axis_size("col")))[::-1]
     for turn_at, bit in enumerate(turns):
         left = jnp.concatenate([left, swap(left, "col", bit)], 0)
         partial = proj
         proj = proj + swap(proj, "col", bit)
         if turn_at == 0:
-            left, right, mark = gate_all([left, right], early, partial)
+            left, right, mark = gate_all([left, right], partial)
             right = jnp.concatenate([right, swap(right, "pop", 1)], 0)
-            spare, ready = cut(weight, *plan[2][1:], mark)
-        elif turn_at < len(turns) - 1:
-            left, mark = gate(left, partial)
-    left, arrived[0], spare, mark = gate_all([left, arrived[0], spare], partial, rights, ready)
-    arrived.append(send(2, spare))
+            piece, early = cut(weight, *plan[2][1:], mark)
+            arrived.append(send(2, piece))
+        elif turn_at == 1:
+            left, mark = gate(left, partial, early, rights)
+            spare, ready = cut(weight, *plan[3][1:], mark)
+    left, arrived[1], spare, mark = gate_all([left, arrived[1], spare], partial, ready)
+    arrived.append(send(3, spare))
     left = turn(jnp.concatenate([left, swap(left, "pop", 1)], 1), where)
     spread = spread_out(proj, members, rank, each)
 
@@ -459,7 +462,7 @@
     many = [index for index, part in enumerate(plan) if part[0] == hops[-1]][:-2]
     for index, (hop, start, size) in enumerate(plan):
         part = arrived[index]
-        if index > 0:
+        if index > 1:
             part, mark = gate(part, done)
             arrived[index] = part
             if index + 2 < len(plan):

time: 111 us -> 108 us (0.973)
  waiting for transfers between devices: 17.1 us -> 11.5 us
  local copies, waits for them, and re-layouts: 13.8 us -> 16.7 us
  other arithmetic: 5.45 us -> 2.66 us
  starting transfers between devices: 16.6 us -> 19.3 us
    ppermute x4 -> x5, waiting for transfers between devices: 10.4 us -> 5.81 us  [send(): return lax.ppermute(piece, 'pop', turn)]
    ppermute x4 -> x5, starting transfers between devices: 6.22 us -> 8.07 us  [send(): return lax.ppermute(piece, 'pop', turn)]
    pallas_call x8, Pallas kernels: 38.3 us -> 40 us  [call(): pl.pallas_call(kernel, grid_spec=pltpu.PrefetchScalarGridSpec(num_scalar_...]
    concatenate x3, other arithmetic: 2.61 us -> 0.99 us  [local(): left = jnp.concatenate([left, swap(left, 'col', bit)], 0)]
    concatenate x1, other arithmetic: 1.46 us -> 0.07 us  [local(): left = turn(jnp.concatenate([left, swap(left, 'pop', 1)], 1), where)]
    concatenate x0 -> x1, local copies, waits for them, and re-layouts: none -> 1.15 us  [local(): part = jnp.concatenate([arrived[i] for i in many[:-1]] + [part], 0)]
    unnamed x47 -> x54, local copies, waits for them, and re-layouts: 9.97 us -> 10.7 us
    pallas_call x7 -> x9, Pallas kernels: 2.38 us -> 1.78 us  [gate_all(): pl.pallas_call(functools.partial(gate_kernel, 2 * count + len(after)), in...]
  transfers between devices with their start and end apart: 16 -> 17, of which waited for: 7 -> 4; matrix products, arithmetic and copies ran while one was open for 8% -> 9% of each run, Pallas kernels for 48% -> 50%
where the time goes in v4:
time: 108 us
  Pallas kernels  56.3 us (52%)
  starting transfers between devices  19.3 us (18%)
  local copies, waits for them, and re-layouts  16.7 us (15%)
  waiting for transfers between devices  11.5 us (11%)
  other arithmetic  2.66 us (2%)
  between operations  1.25 us (1%)
    pallas_call x8, Pallas kernels, call(): pl.pallas_call(kernel, grid_spec=pltpu.PrefetchScalarGridSpec(num_scalar_...  40 us
    ppermute x12, starting transfers between devices, swap(): lax.ppermute(array, axis, [(i, i ^ bit) for i in range(lax.axis_size(axis...  11.2 us
    unnamed x54, local copies, waits for them, and re-layouts  10.7 us
    ppermute x5, starting transfers between devices, send(): return lax.ppermute(piece, 'pop', turn)  8.07 us
    pallas_call x3, Pallas kernels, cut(): pl.pallas_call(functools.partial(cut_kernel, start), in_specs=[anywhere()...  7.28 us
    ppermute x5, waiting for transfers between devices, send(): return lax.ppermute(piece, 'pop', turn)  5.81 us
    ppermute x12, waiting for transfers between devices, swap(): lax.ppermute(array, axis, [(i, i ^ bit) for i in range(lax.axis_size(axis...  5.71 us
    pallas_call x1, Pallas kernels, project(): pl.pallas_call(functools.partial(proj_kernel, rank, each), grid_spec=pltp...  3.26 us
  transfers between devices with their start and end apart: 17, of which 4 were waited for; matrix products, arithmetic and copies ran while one was open for 9% of the time, Pallas kernels for 50%

profile of v4, /device:TPU:0, one launch (start us, length us, event | category | flops | bytes accessed | tf_op | source)
XLA Modules:
  0.0 107.7 jit_solution(410951057423403637)
XLA Ops:
  1.1 1.0 slice.18
  2.1 2.6 %collective-permute-start.1 = (bf16[256,512]{1,0:T(8,128)(2,1)S(1)}, bf16[256,512]{1,0:T(8,128)(2,1)S(1)}, u32[]{:S(2)}, u32[]{:S(2)}) collective-permute-start(bf16[256,512]{1,0:T(8,128)(2,1)S(1)} %slice.18), channel_id=1, source_target_pairs={{0,16},{8,24},{16,0},{24,8},{1,17},{9,25},{17,1},{25,9},{2,18},{10... | collective-permute-start | bytes 786440 | tf_op jit(solution)/shard_map/ppermute | solution.py:400
  4.7 2.4 %shard_map.95 = (bf16[160,512]{1,0:T(8,128)(2,1)}, bf16[32,512]{1,0:T(8,128)(2,1)}, bf16[32,2048]{1,0:T(8,128)(2,1)}, f32[8,128]{1,0:T(8,128)}) custom-call(s32[1,8]{1,0:T(1,128)} %after.1, f32[1,8]{1,0:T(1,128)} %shaping.1, bf16[112,4,512]{2,1,0:T(4,128)(2,1)} %lefts.1, bf16[112,4,2048]{2,1,0:T(4,128)(2,1)} %rights.1, s32[1,8]{1,0:T(1,128)} %after.1), custom_call_target="tpu_custom_call" | custom-call | flops 1 | bytes 1 | tf_op jit(solution)/shard_map/pallas_call | solution.py:123
  7.3 2.4 %shard_map.96 = (bf16[1280,512]{1,0:T(8,128)(2,1)}, f32[8,128]{1,0:T(8,128)}) custom-call(bf16[4096,512]{1,0:T(8,128)(2,1)} %wt.7, f32[8,128]{1,0:T(8,128)} %get-tuple-element.37.after), custom_call_target="tpu_custom_call" | custom-call | flops 1 | bytes 5242880 | tf_op jit(solution)/shard_map/pallas_call | solution.py:76
  9.7 2.1 %collective-permute-start.7 = (bf16[1280,512]{1,0:T(8,128)(2,1)}, bf16[1280,512]{1,0:T(8,128)(2,1)S(1)}, u32[]{:S(2)}, u32[]{:S(2)}) collective-permute-start(bf16[1280,512]{1,0:T(8,128)(2,1)} %get-tuple-element.50), channel_id=1, source_target_pairs={{0,16},{8,24},{16,0},{24,8},{1,17},{9,25},{17,1},{25,9},{2,18},{10... | collective-permute-start | bytes 3932168 | tf_op jit(solution)/shard_map/ppermute | solution.py:400
  11.8 0.9 reshape.27.left
  12.7 0.6 pad_add_fusion.where.refs_0_
  13.3 0.7 copy-done.16
  14.0 1.4 %collective-permute-done.refs_0_ = bf16[160,512]{1,0:T(8,128)(2,1)S(1)} collective-permute-done((bf16[160,512]{1,0:T(8,128)(2,1)}, bf16[160,512]{1,0:T(8,128)(2,1)S(1)}, u32[]{:S(2)}, u32[]{:S(2)}) %collective-permute-start) | collective-permute-done | bytes 163872 | tf_op jit(solution)/shard_map/ppermute | solution.py:400
  15.4 3.1 %collective-permute-start.3 = (bf16[1,64,512]{2,1,0:T(8,128)(2,1)S(1)}, bf16[1,64,512]{2,1,0:T(8,128)(2,1)S(1)}, u32[]{:S(2)}, u32[]{:S(2)}) collective-permute-start(bf16[1,64,512]{2,1,0:T(8,128)(2,1)S(1)} %get-tuple-element.43), channel_id=1, source_target_pairs={{0,4},{1,5},{2,6},{3,7},{4,0},{5,1},{6,2},{7,3},{8,12},{9,13},{10,... | collective-permute-start | bytes 196616 | tf_op jit(solution)/shard_map/ppermute | solution.py:26
  18.6 3.3 %shard_map.101.refs_2_ = f32[8,896]{1,0:T(8,128)} custom-call(s32[2]{0:T(128)} %pad_add_fusion.where.refs_0_, bf16[448,512]{1,0:T(8,128)(2,1)} %reshape.27.left, bf16[896,4096]{1,0:T(8,128)(2,1)} %tok.17, f32[8,128]{1,0:T(8,128)} %copy-done.20), custom_call_target="tpu_custom_call" | custom-call | flops 411041792 | bytes 3670016 | tf_op jit(solution)/shard_map/pallas_call | solution.py:171
  21.9 0.7 copy-done.14
  22.6 0.6 copy-done.21
  23.2 1.6 %collective-permute-start.4 = (bf16[2,64,512]{2,1,0:T(8,128)(2,1)S(1)}, bf16[2,64,512]{2,1,0:T(8,128)(2,1)}, u32[]{:S(2)}, u32[]{:S(2)}) collective-permute-start(bf16[2,64,512]{2,1,0:T(8,128)(2,1)S(1)} %get-tuple-element.46), channel_id=1, source_target_pairs={{0,2},{1,3},{2,0},{3,1},{4,6},{5,7},{6,4},{7,5},{8,10},{9,11},{10,... | collective-permute-start | bytes 393224 | tf_op jit(solution)/shard_map/ppermute | solution.py:26
  24.8 2.5 %collective-permute-start.5 = (f32[8,896]{1,0:T(8,128)}, f32[8,896]{1,0:T(8,128)}, u32[]{:S(2)}, u32[]{:S(2)}) collective-permute-start(f32[8,896]{1,0:T(8,128)} %shard_map.101.refs_2_), channel_id=1, source_target_pairs={{0,4},{1,5},{2,6},{3,7},{4,0},{5,1},{6,2},{7,3},{8,12},{9,13},{10,... | collective-permute-start | bytes 86024 | tf_op jit(solution)/shard_map/ppermute | solution.py:26
  27.2 3.2 %shard_map.103 = (bf16[2304,512]{1,0:T(8,128)(2,1)}, f32[8,128]{1,0:T(8,128)}) custom-call(bf16[4096,512]{1,0:T(8,128)(2,1)} %wt.7, f32[8,128]{1,0:T(8,128)} %copy-done.21), custom_call_target="tpu_custom_call" | custom-call | flops 1 | bytes 9437184 | tf_op jit(solution)/shard_map/pallas_call | solution.py:76
  30.4 1.6 %collective-permute-start.13 = (bf16[2304,512]{1,0:T(8,128)(2,1)}, bf16[2304,512]{1,0:T(8,128)(2,1)}, u32[]{:S(2)}, u32[]{:S(2)}) collective-permute-start(bf16[2304,512]{1,0:T(8,128)(2,1)} %get-tuple-element.58), channel_id=1, source_target_pairs={{0,16},{8,24},{16,0},{24,8},{1,17},{9,25},{17,1},{25,9},{2,18},{10... | collective-permute-start | bytes 7077896 | tf_op jit(solution)/shard_map/ppermute | solution.py:400
  32.0 2.9 %reshape.28.refs_3_.rights.refs_1_ = bf16[448,2048]{1,0:T(8,128)(2,1)S(1)} reshape(bf16[112,4,2048]{2,1,0:T(4,128)(2,1)} %param.15) | data formatting | bytes 3670016 | tf_op jit(solution)/shard_map/reshape | solution.py:420
  35.0 1.0 add.17.refs_1_
  35.9 0.9 pad_maximum_fusion.2.refs_0_
  36.9 1.6 %collective-permute-start.6 = (bf16[4,64,512]{2,1,0:T(8,128)(2,1)S(1)}, bf16[4,64,512]{2,1,0:T(8,128)(2,1)S(1)}, u32[]{:S(2)}, u32[]{:S(2)}) collective-permute-start(bf16[4,64,512]{2,1,0:T(8,128)(2,1)S(1)} %get-tuple-element.49), channel_id=1, source_target_pairs={{0,1},{1,0},{2,3},{3,2},{4,5},{5,4},{6,7},{7,6},{8,9},{9,8},{10,11... | collective-permute-start | bytes 786440 | tf_op jit(solution)/shard_map/ppermute | solution.py:26
  38.4 0.7 constant_dynamic-update-slice_fusion.3
  39.2 3.1 %collective-permute-done.8 = f32[8,896]{1,0:T(8,128)S(1)} collective-permute-done((f32[8,896]{1,0:T(8,128)S(1)}, f32[8,896]{1,0:T(8,128)S(1)}, u32[]{:S(2)}, u32[]{:S(2)}) %collective-permute-start.8) | collective-permute-done | bytes 28704 | tf_op jit(solution)/shard_map/ppermute | solution.py:26
  42.3 1.7 %shard_map.105 = (bf16[256,512]{1,0:T(8,128)(2,1)}, f32[8,128]{1,0:T(8,128)}) custom-call(bf16[4096,512]{1,0:T(8,128)(2,1)} %wt.7, f32[8,128]{1,0:T(8,128)} %copy-done.17), custom_call_target="tpu_custom_call" | custom-call | flops 1 | bytes 1048576 | tf_op jit(solution)/shard_map/pallas_call | solution.py:76
  44.1 0.9 copy-done.11
  45.0 0.7 copy-done.19
  45.7 0.6 shard_map.106
  46.3 0.7 copy-done.12
  47.0 1.1 %constant_dynamic-update-slice_fusion.2.wt = bf16[1536,512]{1,0:T(8,128)(2,1)} fusion(bf16[1536,512]{1,0:T(8,128)(2,1)} %constant_dynamic-update-slice_fusion.3, bf16[1280,512]{1,0:T(8,128)(2,1)S(1)} %get-tuple-element.60), kind=kLoop, calls=%fused_computation.8 | loop fusion | bytes 2621440 | tf_op jit(solution)/shard_map/concatenate | solution.py:474
  48.7 1.3 %collective-permute-start.11 = (f32[8,896]{1,0:T(8,128)S(1)}, f32[8,896]{1,0:T(8,128)S(1)}, u32[]{:S(2)}, u32[]{:S(2)}) collective-permute-start(f32[8,896]{1,0:T(8,128)S(1)} %add.18.refs_3_), channel_id=1, source_target_pairs={{0,1},{1,0},{2,3},{3,2},{4,5},{5,4},{6,7},{7,6},{8,9},{9,8},{10,11... | collective-permute-start | bytes 86024 | tf_op jit(solution)/shard_map/ppermute | solution.py:26
  50.0 2.6 %collective-permute-done.11 = f32[8,896]{1,0:T(8,128)S(1)} collective-permute-done((f32[8,896]{1,0:T(8,128)S(1)}, f32[8,896]{1,0:T(8,128)S(1)}, u32[]{:S(2)}, u32[]{:S(2)}) %collective-permute-start.11) | collective-permute-done | bytes 28704 | tf_op jit(solution)/shard_map/ppermute | solution.py:26
  52.8 0.8 copy-done.7
  53.7 1.4 %shard_map.107.left = bf16[4096,128]{1,0:T(8,128)(2,1)S(1)} custom-call(s32[2]{0:T(128)S(1)} %copy-done.15, bf16[8,128,512]{2,1,0:T(8,128)(2,1)S(1)} %pad_maximum_fusion.left), custom_call_target="tpu_custom_call" | custom-call | flops 1 | bytes 1 | tf_op jit(solution)/shard_map/pallas_call | solution.py:204
  55.1 1.0 copy-done.1
  56.1 11.2 %shard_map.109 = (bf16[896,2048]{1,0:T(8,128)(2,1)}, bf16[4096,512]{1,0:T(8,128)(2,1)}, f32[8,128]{1,0:T(8,128)}) custom-call(s32[1]{0:T(128)} %bitcast.where, bf16[896,4096]{1,0:T(8,128)(2,1)} %tok.17, bf16[4096,512]{1,0:T(8,128)(2,1)} %wt.7, bf16[4096,128]{1,0:T(8,128)(2,1)} %copy-done.1, bf16[128,2048]{1,0:T(8,128)(2,1)} %copy-done.5, ...), custom_call_target="tpu_custom_call" | custom-call | flops 1 | bytes 1 | tf_op jit(solution)/shard_map/pallas_call | solution.py:309
  67.4 10.6 %shard_map.110 = (bf16[896,2048]{1,0:T(8,128)(2,1)}, f32[8,128]{1,0:T(8,128)}) custom-call(s32[1]{0:T(128)} %bitcast.5.where, bf16[896,4096]{1,0:T(8,128)(2,1)} %tok.17, bf16[4096,512]{1,0:T(8,128)(2,1)} %get-tuple-element.61.wt, bf16[4096,128]{1,0:T(8,128)(2,1)} %copy-done.1, bf16[128,2048]{1,0:T(8,128)(2,1)} %copy-done.5, ...), custom_call_target="tpu_custom_call", output_to_operand_aliasing={{0}: (8, {})} | custom-call | flops 1 | bytes 1 | tf_op jit(solution)/shard_map/pallas_call | solution.py:309
  78.0 3.1 %copy-done = bf16[896,4096]{1,0:T(8,128)(2,1)S(1)} copy-done((bf16[896,4096]{1,0:T(8,128)(2,1)S(1)}, bf16[896,4096]{1,0:T(8,128)(2,1)}, u32[]{:S(2)}) %copy-start) | copy-done | bytes 7340056
  81.1 0.7 copy-done.22
  81.8 3.9 %shard_map.111.refs_2_.refs_0_ = f32[896,512]{1,0:T(8,128)S(1)} custom-call(s32[1]{0:T(128)} %bitcast.4.where, bf16[896,4096]{1,0:T(8,128)(2,1)S(1)} %copy-done, bf16[1536,512]{1,0:T(8,128)(2,1)} %constant_dynamic-update-slice_fusion.2.wt, bf16[4096,128]{1,0:T(8,128)(2,1)S(1)} %copy-done.2, bf16[128,2048]{1,0:T(8,128)(2,1)S(1)} %copy-done.6, ...), custom_call_target="tpu_custom_call" | custom-call | flops 1 | bytes 1 | tf_op jit(solution)/shard_map/pallas_call | solution.py:309
  85.7 3.9 %shard_map.112.refs_1_.refs_0_ = f32[896,512]{1,0:T(8,128)S(1)} custom-call(s32[1]{0:T(128)} %bitcast.3.where, bf16[896,4096]{1,0:T(8,128)(2,1)S(1)} %copy-done, bf16[1536,512]{1,0:T(8,128)(2,1)} %collective-permute-done.14.wt, bf16[4096,128]{1,0:T(8,128)(2,1)S(1)} %copy-done.2, bf16[128,2048]{1,0:T(8,128)(2,1)S(1)} %copy-done.6, ...), custom_call_target="tpu_custom_call" | custom-call | flops 1 | bytes 1 | tf_op jit(solution)/shard_map/pallas_call | solution.py:309
  89.6 4.4 %collective-permute-done.13.refs_0_ = bf16[2304,512]{1,0:T(8,128)(2,1)} collective-permute-done((bf16[2304,512]{1,0:T(8,128)(2,1)}, bf16[2304,512]{1,0:T(8,128)(2,1)}, u32[]{:S(2)}, u32[]{:S(2)}) %collective-permute-start.13) | collective-permute-done | bytes 2359328 | tf_op jit(solution)/shard_map/ppermute | solution.py:400
  93.9 0.6 shard_map.113
  94.5 1.7 %collective-permute-start.12 = (bf16[256,512]{1,0:T(8,128)(2,1)S(1)}, bf16[256,512]{1,0:T(8,128)(2,1)S(1)}, u32[]{:S(2)}, u32[]{:S(2)}) collective-permute-start(bf16[256,512]{1,0:T(8,128)(2,1)S(1)} %copy-done.13), channel_id=1, source_target_pairs={{0,16},{8,24},{16,0},{24,8},{1,17},{9,25},{17,1},{25,9},{2,18},{10... | collective-permute-start | bytes 786440 | tf_op jit(solution)/shard_map/ppermute | solution.py:400
  96.3 4.6 %shard_map.114.refs_1_.before = f32[896,512]{1,0:T(8,128)S(1)} custom-call(s32[1]{0:T(128)} %bitcast.4.where, bf16[896,4096]{1,0:T(8,128)(2,1)S(1)} %copy-done, bf16[2304,512]{1,0:T(8,128)(2,1)} %get-tuple-element.65.wt, bf16[4096,128]{1,0:T(8,128)(2,1)S(1)} %copy-done.2, bf16[128,2048]{1,0:T(8,128)(2,1)S(1)} %copy-done.6, ...), custom_call_target="tpu_custom_call", output_to_operand_aliasing={{}: (5, {})} | custom-call | flops 1 | bytes 1 | tf_op jit(solution)/shard_map/pallas_call | solution.py:309
  100.9 3.0 %shard_map.115.refs_1_.before = f32[896,512]{1,0:T(8,128)S(1)} custom-call(s32[1]{0:T(128)} %bitcast.3.where, bf16[896,4096]{1,0:T(8,128)(2,1)S(1)} %copy-done, bf16[2304,512]{1,0:T(8,128)(2,1)S(1)} %collective-permute-done.15.wt, bf16[4096,128]{1,0:T(8,128)(2,1)S(1)} %copy-done.2, bf16[128,2048]{1,0:T(8,128)(2,1)S(1)} %copy-done.6, ...), custom_call_target="tpu_custom_call", output_to_operand_aliasing={{}: (5, {})} | custom-call | flops 1 | bytes 1 | tf_op jit(solution)/shard_map/pallas_call | solution.py:309
  103.9 0.6 shard_map.116
  104.7 1.4 %shard_map.117.acts = bf16[896,2048]{1,0:T(8,128)(2,1)} custom-call(s32[1]{0:T(128)} %bitcast.4.where, bf16[896,4096]{1,0:T(8,128)(2,1)S(1)} %copy-done, bf16[256,512]{1,0:T(8,128)(2,1)S(1)} %get-tuple-element.66.wt, bf16[4096,128]{1,0:T(8,128)(2,1)S(1)} %copy-done.2, bf16[128,2048]{1,0:T(8,128)(2,1)S(1)} %copy-done.6, ...), custom_call_target="tpu_custom_call", output_to_operand_aliasing={{}: (6, {})} | custom-call | flops 1 | bytes 1 | tf_op jit(solution)/shard_map/pallas_call | solution.py:309
  106.1 1.4 %shard_map.118 = bf16[896,2048]{1,0:T(8,128)(2,1)} custom-call(s32[1]{0:T(128)} %bitcast.3.where, bf16[896,4096]{1,0:T(8,128)(2,1)S(1)} %copy-done, bf16[256,512]{1,0:T(8,128)(2,1)S(1)} %collective-permute-done.16.wt, bf16[4096,128]{1,0:T(8,128)(2,1)S(1)} %copy-done.2, bf16[128,2048]{1,0:T(8,128)(2,1)S(1)} %copy-done.6, ...), custom_call_target="tpu_custom_call", output_to_operand_aliasing={{}: (6, {})} | custom-call | flops 1 | bytes 1 | tf_op jit(solution)/shard_map/pallas_call | solution.py:309
  (80 shorter events, 1.8 us)
Async XLA Ops:
  0.6 12.6 %collective-permute-start.2 = (bf16[4096,512]{1,0:T(8,128)(2,1)}, bf16[4096,512]{1,0:T(8,128)(2,1)}, u32[]{:S(2)}, u32[]{:S(2)}) collective-permute-start(bf16[4096,512]{1,0:T(8,128)(2,1)} %wt.7), channel_id=1, source_target_pairs={{0,8},{8,0},{16,24},{24,16},{1,9},{9,1},{17,25},{25,17},{2,10},{10... | collective-permute-start | bytes 12582920 | tf_op jit(solution)/shard_map/ppermute | solution.py:26
  2.1 11.8 %collective-permute-start.1 = (bf16[256,512]{1,0:T(8,128)(2,1)S(1)}, bf16[256,512]{1,0:T(8,128)(2,1)S(1)}, u32[]{:S(2)}, u32[]{:S(2)}) collective-permute-start(bf16[256,512]{1,0:T(8,128)(2,1)S(1)} %slice.18), channel_id=1, source_target_pairs={{0,16},{8,24},{16,0},{24,8},{1,17},{9,25},{17,1},{25,9},{2,18},{10... | collective-permute-start | bytes 786440 | tf_op jit(solution)/shard_map/ppermute | solution.py:400
  7.2 8.2 %collective-permute-start = (bf16[160,512]{1,0:T(8,128)(2,1)}, bf16[160,512]{1,0:T(8,128)(2,1)S(1)}, u32[]{:S(2)}, u32[]{:S(2)}) collective-permute-start(bf16[160,512]{1,0:T(8,128)(2,1)} %get-tuple-element.36), channel_id=1, source_target_pairs={{0,16},{8,24},{16,0},{24,8},{1,17},{9,25},{17,1},{25,9},{2,18},{10... | collective-permute-start | bytes 491528 | tf_op jit(solution)/shard_map/ppermute | solution.py:400
  7.3 4.5 %copy-start.23 = (bf16[112,4,512]{2,1,0:T(4,128)(2,1)S(1)}, bf16[112,4,512]{2,1,0:T(4,128)(2,1)}, u32[]{:S(2)}) copy-start(bf16[112,4,512]{2,1,0:T(4,128)(2,1)} %param.14) | copy-start | bytes 1376260
  9.7 34.4 %collective-permute-start.7 = (bf16[1280,512]{1,0:T(8,128)(2,1)}, bf16[1280,512]{1,0:T(8,128)(2,1)S(1)}, u32[]{:S(2)}, u32[]{:S(2)}) collective-permute-start(bf16[1280,512]{1,0:T(8,128)(2,1)} %get-tuple-element.50), channel_id=1, source_target_pairs={{0,16},{8,24},{16,0},{24,8},{1,17},{9,25},{17,1},{25,9},{2,18},{10... | collective-permute-start | bytes 3932168 | tf_op jit(solution)/shard_map/ppermute | solution.py:400
  13.3 0.7 copy-start.16
  13.9 1.5 %copy-start.25 = (bf16[32,512]{1,0:T(8,128)(2,1)S(1)}, bf16[32,512]{1,0:T(8,128)(2,1)}, u32[]{:S(2)}) copy-start(bf16[32,512]{1,0:T(8,128)(2,1)} %get-tuple-element.35) | copy-start | bytes 98308
  13.9 4.6 %copy-start.24 = (bf16[32,2048]{1,0:T(8,128)(2,1)S(1)}, bf16[32,2048]{1,0:T(8,128)(2,1)}, u32[]{:S(2)}) copy-start(bf16[32,2048]{1,0:T(8,128)(2,1)} %get-tuple-element.44) | copy-start | bytes 393220
  14.0 7.9 %copy-start.9 = (bf16[256,512]{1,0:T(8,128)(2,1)}, bf16[256,512]{1,0:T(8,128)(2,1)S(1)}, u32[]{:S(2)}) copy-start(bf16[256,512]{1,0:T(8,128)(2,1)S(1)} %get-tuple-element.59) | copy-start | bytes 786436
  15.4 3.1 %copy-start.20 = (f32[8,128]{1,0:T(8,128)}, f32[8,128]{1,0:T(8,128)S(1)}, u32[]{:S(2)}) copy-start(f32[8,128]{1,0:T(8,128)S(1)} %get-tuple-element.45.after) | copy-start | bytes 12292
  15.4 6.4 %collective-permute-start.3 = (bf16[1,64,512]{2,1,0:T(8,128)(2,1)S(1)}, bf16[1,64,512]{2,1,0:T(8,128)(2,1)S(1)}, u32[]{:S(2)}, u32[]{:S(2)}) collective-permute-start(bf16[1,64,512]{2,1,0:T(8,128)(2,1)S(1)} %get-tuple-element.43), channel_id=1, source_target_pairs={{0,4},{1,5},{2,6},{3,7},{4,0},{5,1},{6,2},{7,3},{8,12},{9,13},{10,... | collective-permute-start | bytes 196616 | tf_op jit(solution)/shard_map/ppermute | solution.py:26
  21.8 0.7 copy-start.14
  22.6 0.6 copy-start.21
  23.2 12.7 %collective-permute-start.4 = (bf16[2,64,512]{2,1,0:T(8,128)(2,1)S(1)}, bf16[2,64,512]{2,1,0:T(8,128)(2,1)}, u32[]{:S(2)}, u32[]{:S(2)}) collective-permute-start(bf16[2,64,512]{2,1,0:T(8,128)(2,1)S(1)} %get-tuple-element.46), channel_id=1, source_target_pairs={{0,2},{1,3},{2,0},{3,1},{4,6},{5,7},{6,4},{7,5},{8,10},{9,11},{10,... | collective-permute-start | bytes 393224 | tf_op jit(solution)/shard_map/ppermute | solution.py:26
  24.8 10.2 %collective-permute-start.5 = (f32[8,896]{1,0:T(8,128)}, f32[8,896]{1,0:T(8,128)}, u32[]{:S(2)}, u32[]{:S(2)}) collective-permute-start(f32[8,896]{1,0:T(8,128)} %shard_map.101.refs_2_), channel_id=1, source_target_pairs={{0,4},{1,5},{2,6},{3,7},{4,0},{5,1},{6,2},{7,3},{8,12},{9,13},{10,... | collective-permute-start | bytes 86024 | tf_op jit(solution)/shard_map/ppermute | solution.py:26
  30.4 6.5 %copy-start.18 = (f32[8,128]{1,0:T(8,128)S(1)}, f32[8,128]{1,0:T(8,128)}, u32[]{:S(2)}) copy-start(f32[8,128]{1,0:T(8,128)} %get-tuple-element.48.refs_2_) | copy-start | bytes 12292
  30.4 63.5 %collective-permute-start.13 = (bf16[2304,512]{1,0:T(8,128)(2,1)}, bf16[2304,512]{1,0:T(8,128)(2,1)}, u32[]{:S(2)}, u32[]{:S(2)}) collective-permute-start(bf16[2304,512]{1,0:T(8,128)(2,1)} %get-tuple-element.58), channel_id=1, source_target_pairs={{0,16},{8,24},{16,0},{24,8},{1,17},{9,25},{17,1},{25,9},{2,18},{10... | collective-permute-start | bytes 7077896 | tf_op jit(solution)/shard_map/ppermute | solution.py:400
  34.9 9.1 %copy-start.3 = (bf16[448,2048]{1,0:T(8,128)(2,1)}, bf16[448,2048]{1,0:T(8,128)(2,1)S(1)}, u32[]{:S(2)}) copy-start(bf16[448,2048]{1,0:T(8,128)(2,1)S(1)} %reshape.28.refs_3_.rights.refs_1_) | copy-start | bytes 5505028
  34.9 3.5 %copy-start.10 = (bf16[256,512]{1,0:T(8,128)(2,1)S(1)}, bf16[256,512]{1,0:T(8,128)(2,1)}, u32[]{:S(2)}) copy-start(bf16[256,512]{1,0:T(8,128)(2,1)} %copy-done.9) | copy-start | bytes 786436
  36.9 5.4 %copy-start.17 = (f32[8,128]{1,0:T(8,128)}, f32[8,128]{1,0:T(8,128)S(1)}, u32[]{:S(2)}) copy-start(f32[8,128]{1,0:T(8,128)S(1)} %get-tuple-element.51.after) | copy-start | bytes 12292
  36.9 7.1 %collective-permute-start.6 = (bf16[4,64,512]{2,1,0:T(8,128)(2,1)S(1)}, bf16[4,64,512]{2,1,0:T(8,128)(2,1)S(1)}, u32[]{:S(2)}, u32[]{:S(2)}) collective-permute-start(bf16[4,64,512]{2,1,0:T(8,128)(2,1)S(1)} %get-tuple-element.49), channel_id=1, source_target_pairs={{0,1},{1,0},{2,3},{3,2},{4,5},{5,4},{6,7},{7,6},{8,9},{9,8},{10,11... | collective-permute-start | bytes 786440 | tf_op jit(solution)/shard_map/ppermute | solution.py:26
  38.4 3.9 %collective-permute-start.8 = (f32[8,896]{1,0:T(8,128)S(1)}, f32[8,896]{1,0:T(8,128)S(1)}, u32[]{:S(2)}, u32[]{:S(2)}) collective-permute-start(f32[8,896]{1,0:T(8,128)S(1)} %add.17.refs_1_), channel_id=1, source_target_pairs={{0,2},{1,3},{2,0},{3,1},{4,6},{5,7},{6,4},{7,5},{8,10},{9,11},{10,... | collective-permute-start | bytes 86024 | tf_op jit(solution)/shard_map/ppermute | solution.py:26
  44.1 1.0 copy-start.11
  45.0 0.7 copy-start.19
  46.3 0.7 copy-start.12
  48.2 37.5 %collective-permute-start.14 = (bf16[1536,512]{1,0:T(8,128)(2,1)}, bf16[1536,512]{1,0:T(8,128)(2,1)}, u32[]{:S(2)}, u32[]{:S(2)}) collective-permute-start(bf16[1536,512]{1,0:T(8,128)(2,1)} %constant_dynamic-update-slice_fusion.2.wt), channel_id=1, source_target_pairs={{0,8},{8,0},{16,24},{24,16},{1,9},{9,1},{17,25},{25,17},{2,10},{10... | collective-permute-start | bytes 4718600 | tf_op jit(solution)/shard_map/ppermute | solution.py:26
  48.2 4.6 %collective-permute-start.9 = (bf16[8,64,512]{2,1,0:T(8,128)(2,1)S(1)}, bf16[8,64,512]{2,1,0:T(8,128)(2,1)S(1)}, u32[]{:S(2)}, u32[]{:S(2)}) collective-permute-start(bf16[8,64,512]{2,1,0:T(8,128)(2,1)S(1)} %get-tuple-element.54), channel_id=1, source_target_pairs={{0,8},{8,0},{16,24},{24,16},{1,9},{9,1},{17,25},{25,17},{2,10},{10... | collective-permute-start | bytes 1572872 | tf_op jit(solution)/shard_map/ppermute | solution.py:26
  48.7 3.9 %collective-permute-start.11 = (f32[8,896]{1,0:T(8,128)S(1)}, f32[8,896]{1,0:T(8,128)S(1)}, u32[]{:S(2)}, u32[]{:S(2)}) collective-permute-start(f32[8,896]{1,0:T(8,128)S(1)} %add.18.refs_3_), channel_id=1, source_target_pairs={{0,1},{1,0},{2,3},{3,2},{4,5},{5,4},{6,7},{7,6},{8,9},{9,8},{10,11... | collective-permute-start | bytes 86024 | tf_op jit(solution)/shard_map/ppermute | solution.py:26
  50.0 2.8 %collective-permute-start.10 = (bf16[64,2048]{1,0:T(8,128)(2,1)S(1)}, bf16[64,2048]{1,0:T(8,128)(2,1)S(1)}, u32[]{:S(2)}, u32[]{:S(2)}) collective-permute-start(bf16[64,2048]{1,0:T(8,128)(2,1)S(1)} %get-tuple-element.55), channel_id=1, source_target_pairs={{0,8},{8,0},{16,24},{24,16},{1,9},{9,1},{17,25},{25,17},{2,10},{10... | collective-permute-start | bytes 786440 | tf_op jit(solution)/shard_map/ppermute | solution.py:26
  52.6 1.1 %copy-start.15 = (s32[2]{0:T(128)S(1)}, s32[2]{0:T(128)}, u32[]{:S(2)}) copy-start(s32[2]{0:T(128)} %pad_add_fusion.where.refs_0_) | copy-start | bytes 28
  52.7 0.9 copy-start.7
  53.7 2.4 %copy-start.5 = (bf16[128,2048]{1,0:T(8,128)(2,1)}, bf16[128,2048]{1,0:T(8,128)(2,1)S(1)}, u32[]{:S(2)}) copy-start(bf16[128,2048]{1,0:T(8,128)(2,1)S(1)} %constant_dynamic-update-slice_fusion.right) | copy-start | bytes 1572868
  55.1 1.0 copy-start.1
  67.3 10.6 %copy-start.2 = (bf16[4096,128]{1,0:T(8,128)(2,1)S(1)}, bf16[4096,128]{1,0:T(8,128)(2,1)}, u32[]{:S(2)}) copy-start(bf16[4096,128]{1,0:T(8,128)(2,1)} %copy-done.1) | copy-start | bytes 3145732
  67.3 10.6 %copy-start.4 = (bf16[448,2048]{1,0:T(8,128)(2,1)S(1)}, bf16[448,2048]{1,0:T(8,128)(2,1)}, u32[]{:S(2)}) copy-start(bf16[448,2048]{1,0:T(8,128)(2,1)} %copy-done.3) | copy-start | bytes 5505028
  67.3 10.6 %copy-start.6 = (bf16[128,2048]{1,0:T(8,128)(2,1)S(1)}, bf16[128,2048]{1,0:T(8,128)(2,1)}, u32[]{:S(2)}) copy-start(bf16[128,2048]{1,0:T(8,128)(2,1)} %copy-done.5) | copy-start | bytes 1572868
  67.4 10.6 %copy-start.8 = (bf16[896,448]{1,0:T(8,128)(2,1)S(1)}, bf16[896,448]{1,0:T(8,128)(2,1)}, u32[]{:S(2)}) copy-start(bf16[896,448]{1,0:T(8,128)(2,1)} %copy-done.7) | copy-start | bytes 2408452
  78.0 3.1 %copy-start = (bf16[896,4096]{1,0:T(8,128)(2,1)S(1)}, bf16[896,4096]{1,0:T(8,128)(2,1)}, u32[]{:S(2)}) copy-start(bf16[896,4096]{1,0:T(8,128)(2,1)} %tok.17) | copy-start | bytes 22020100
  81.1 0.7 copy-start.22
  89.5 5.0 %copy-start.13 = (bf16[256,512]{1,0:T(8,128)(2,1)S(1)}, bf16[256,512]{1,0:T(8,128)(2,1)}, u32[]{:S(2)}) copy-start(bf16[256,512]{1,0:T(8,128)(2,1)} %copy-done.12) | copy-start | bytes 786436
  94.5 6.3 %collective-permute-start.15 = (bf16[2304,512]{1,0:T(8,128)(2,1)}, bf16[2304,512]{1,0:T(8,128)(2,1)S(1)}, u32[]{:S(2)}, u32[]{:S(2)}) collective-permute-start(bf16[2304,512]{1,0:T(8,128)(2,1)} %get-tuple-element.65.wt), channel_id=1, source_target_pairs={{0,8},{8,0},{16,24},{24,16},{1,9},{9,1},{17,25},{25,17},{2,10},{10... | collective-permute-start | bytes 7077896 | tf_op jit(solution)/shard_map/ppermute | solution.py:26
  94.5 9.3 %collective-permute-start.12 = (bf16[256,512]{1,0:T(8,128)(2,1)S(1)}, bf16[256,512]{1,0:T(8,128)(2,1)S(1)}, u32[]{:S(2)}, u32[]{:S(2)}) collective-permute-start(bf16[256,512]{1,0:T(8,128)(2,1)S(1)} %copy-done.13), channel_id=1, source_target_pairs={{0,16},{8,24},{16,0},{24,8},{1,17},{9,25},{17,1},{25,9},{2,18},{10... | collective-permute-start | bytes 786440 | tf_op jit(solution)/shard_map/ppermute | solution.py:400
  104.5 1.7 %collective-permute-start.16 = (bf16[256,512]{1,0:T(8,128)(2,1)S(1)}, bf16[256,512]{1,0:T(8,128)(2,1)S(1)}, u32[]{:S(2)}, u32[]{:S(2)}) collective-permute-start(bf16[256,512]{1,0:T(8,128)(2,1)S(1)} %get-tuple-element.66.wt), channel_id=1, source_target_pairs={{0,8},{8,0},{16,24},{24,16},{1,9},{9,1},{17,25},{25,17},{2,10},{10... | collective-permute-start | bytes 786440 | tf_op jit(solution)/shard_map/ppermute | solution.py:26

commit v5 on v4

--- a/solution.py
+++ b/solution.py
@@ -12,6 +12,7 @@
 PIECES = (1, 5, 9, 1)
 LIMIT = 20 * 2**20
 WIDE = 58 * 2**20
+BROAD = 50 * 2**20
 
 
 def params(limit=LIMIT):
@@ -63,6 +64,22 @@
 
 def gate(array, *after):
     return gate_all([array], *after)
+
+
+def hold_kernel(*refs):
+    pass
+
+
+def hold(array, *after):
+    return pl.pallas_call(
+        hold_kernel,
+        in_specs=[anywhere()] * (1 + len(after)),
+        out_specs=anywhere(),
+        out_shape=jax.ShapeDtypeStruct(array.shape, array.dtype),
+        input_output_aliases={0: 0},
+        compiler_params=pltpu.CompilerParams(vmem_limit_bytes=2**20),
+        cost_estimate=cost(),
+    )(array, *after)
 
 
 def cut_kernel(start, wt, after, out, mark, sem):
@@ -281,20 +298,28 @@
 
 def sum_kernel(scale, start, where, tok, wt, left, right, *refs):
     out = refs[-1]
-    if start == 0:
-        before = begin(scale, refs[0][...], columns(refs[1], where[0], wt.shape[1]))
-    else:
-        before = refs[0][...]
-    out[...] = before + product(start, where, tok, wt, left, right)(0, tok.shape[0])
+    unit, width = wt.shape
+    step = pl.program_id(0)
+
+    @pl.when(step == 0)
+    def _():
+        if start == 0:
+            out[...] = begin(scale, refs[0][...], columns(refs[1], where[0], width))
+        else:
+            out[...] = refs[0][...]
+
+    at = pl.multiple_of(start + step * unit, 128)
+    fresh = refresh(wt[...], left[pl.ds(at, unit), :], columns(right, where[0], width))
+    out[...] += jnp.dot(tok[:, pl.ds(at, unit)], fresh, preferred_element_type=jnp.float32)
 
 
 def last_kernel(start, where, tok, wt, left, right, before, acts, out, kept, sems):
     width = wt.shape[1]
     got = product(start, where, tok, wt, left, right)
-    part = kept.shape[0] // 2
+    part = kept.shape[0] // 4
     place = pl.ds(pl.multiple_of(where[0] * width, width), width)
     copies = []
-    for half in range(2):
+    for half in range(4):
         rows = pl.ds(half * part, part)
         kept[rows, :] = finish(before[rows, :] + got(half * part, part))
         copies.append(pltpu.make_async_copy(kept.at[rows], out.at[rows, place], sems.at[half]))
@@ -354,13 +379,16 @@
         return call(
             functools.partial(full_kernel, scale, keep, begun),
             where, (4,), specs, args, out_specs, out_shape, aliases,
-            [pltpu.VMEM((rows, width), jnp.float32)], WIDE,
+            [pltpu.VMEM((rows, width), jnp.float32)], BROAD,
         )
     if not last:
         extra = [spread, rights] if first else [before]
+        unit = depth
         return call(
             functools.partial(sum_kernel, scale, start),
-            where, (1,), [vmem()] * (4 + len(extra)) + [anywhere()],
+            where, (depth // unit,),
+            [vmem(), pl.BlockSpec((unit, width), lambda k, at: (k, 0))]
+            + [vmem()] * (2 + len(extra)) + [anywhere()],
             [tokens, wt, left, right, *extra, after], vmem(),
             jax.ShapeDtypeStruct((rows, width), jnp.float32), {} if first else {5: 0},
         )
@@ -369,7 +397,7 @@
         where, (1,), [vmem()] * 5 + [anywhere()],
         [tokens, wt, left, right, before, acts], anywhere(),
         jax.ShapeDtypeStruct(acts.shape, jnp.bfloat16), {6: 0},
-        [pltpu.VMEM((rows, width), jnp.bfloat16), pltpu.SemaphoreType.DMA((2,))],
+        [pltpu.VMEM((rows, width), jnp.bfloat16), pltpu.SemaphoreType.DMA((4,))],
     )
 
 
@@ -463,9 +491,10 @@
     for index, (hop, start, size) in enumerate(plan):
         part = arrived[index]
         if index > 1:
-            part, mark = gate(part, done)
+            part = hold(part, done)
             arrived[index] = part
             if index + 2 < len(plan):
+                part, mark = gate(part, done)
                 piece, _ = cut(weight, *plan[index + 2][1:], mark)
                 arrived.append(send(index + 2, piece))
         if index in many:

time: 108 us -> 107 us (level)
  waiting for transfers between devices: 11.5 us -> 15.7 us
  local copies, waits for them, and re-layouts: 16.7 us -> 13.8 us
  Pallas kernels: 56.3 us -> 53.6 us
    ppermute x5, waiting for transfers between devices: 5.81 us -> 10.6 us  [send(): return lax.ppermute(piece, 'pop', turn)]
    unnamed x54 -> x42, local copies, waits for them, and re-layouts: 10.7 us -> 6.52 us
    pallas_call x8, Pallas kernels: 40 us -> 38.5 us  [call(): pl.pallas_call(kernel, grid_spec=pltpu.PrefetchScalarGridSpec(num_scalar_...]
    concatenate x1, other arithmetic: 0.07 us -> 1.44 us  [local(): left = turn(jnp.concatenate([left, swap(left, 'pop', 1)], 1), where)]
    concatenate x1, local copies, waits for them, and re-layouts: 1.15 us -> 2.46 us  [local(): part = jnp.concatenate([arrived[i] for i in many[:-1]] + [part], 0)]
    pallas_call x9 -> x7, Pallas kernels: 1.78 us -> 0.61 us  [gate_all(): pl.pallas_call(functools.partial(gate_kernel, 2 * count + len(after)), in...]
  transfers between devices with their start and end apart: 17 -> 17, of which waited for: 4 -> 5; matrix products, arithmetic and copies ran while one was open for 9% -> 10% of each run, Pallas kernels for 50% -> 49%
where the time goes in v5:
time: 107 us
  Pallas kernels  53.6 us (50%)
  starting transfers between devices  20 us (19%)
  waiting for transfers between devices  15.7 us (15%)
  local copies, waits for them, and re-layouts  13.8 us (13%)
  other arithmetic  2.22 us (2%)
  between operations  1.22 us (1%)
    pallas_call x8, Pallas kernels, call(): pl.pallas_call(kernel, grid_spec=pltpu.PrefetchScalarGridSpec(num_scalar_...  38.5 us
    ppermute x12, starting transfers between devices, swap(): lax.ppermute(array, axis, [(i, i ^ bit) for i in range(lax.axis_size(axis...  11.9 us
    ppermute x5, waiting for transfers between devices, send(): return lax.ppermute(piece, 'pop', turn)  10.6 us
    ppermute x5, starting transfers between devices, send(): return lax.ppermute(piece, 'pop', turn)  8.07 us
    pallas_call x3, Pallas kernels, cut(): pl.pallas_call(functools.partial(cut_kernel, start), in_specs=[anywhere()...  7.29 us
    unnamed x42, local copies, waits for them, and re-layouts  6.52 us
    ppermute x12, waiting for transfers between devices, swap(): lax.ppermute(array, axis, [(i, i ^ bit) for i in range(lax.axis_size(axis...  5.11 us
    pallas_call x1, Pallas kernels, project(): pl.pallas_call(functools.partial(proj_kernel, rank, each), grid_spec=pltp...  3.26 us
  transfers between devices with their start and end apart: 17, of which 5 were waited for; matrix products, arithmetic and copies ran while one was open for 10% of the time, Pallas kernels for 49%

profile of v5, /device:TPU:0, one launch (start us, length us, event | category | flops | bytes accessed | tf_op | source)
XLA Modules:
  0.0 106.5 jit_solution(3171147150812704506)
XLA Ops:
  0.6 0.5 collective-permute-start.2
  1.1 1.0 slice.18
  2.1 2.6 %collective-permute-start.1 = (bf16[256,512]{1,0:T(8,128)(2,1)S(1)}, bf16[256,512]{1,0:T(8,128)(2,1)S(1)}, u32[]{:S(2)}, u32[]{:S(2)}) collective-permute-start(bf16[256,512]{1,0:T(8,128)(2,1)S(1)} %slice.18), channel_id=1, source_target_pairs={{0,16},{8,24},{16,0},{24,8},{1,17},{9,25},{17,1},{25,9},{2,18},{10... | collective-permute-start | bytes 786440 | tf_op jit(solution)/shard_map/ppermute | solution.py:428
  4.7 2.5 %shard_map.95 = (bf16[160,512]{1,0:T(8,128)(2,1)}, bf16[32,512]{1,0:T(8,128)(2,1)}, bf16[32,2048]{1,0:T(8,128)(2,1)}, f32[8,128]{1,0:T(8,128)}) custom-call(s32[1,8]{1,0:T(1,128)} %after.1, f32[1,8]{1,0:T(1,128)} %shaping.1, bf16[112,4,512]{2,1,0:T(4,128)(2,1)} %lefts.1, bf16[112,4,2048]{2,1,0:T(4,128)(2,1)} %rights.1, s32[1,8]{1,0:T(1,128)} %after.1), custom_call_target="tpu_custom_call" | custom-call | flops 1 | bytes 1 | tf_op jit(solution)/shard_map/pallas_call | solution.py:140
  7.2 0.1 collective-permute-start
  7.3 2.4 %shard_map.96 = (bf16[1280,512]{1,0:T(8,128)(2,1)}, f32[8,128]{1,0:T(8,128)}) custom-call(bf16[4096,512]{1,0:T(8,128)(2,1)} %wt.7, f32[8,128]{1,0:T(8,128)} %get-tuple-element.35.after), custom_call_target="tpu_custom_call" | custom-call | flops 1 | bytes 5242880 | tf_op jit(solution)/shard_map/pallas_call | solution.py:93
  9.7 2.1 %collective-permute-start.7 = (bf16[1280,512]{1,0:T(8,128)(2,1)}, bf16[1280,512]{1,0:T(8,128)(2,1)}, u32[]{:S(2)}, u32[]{:S(2)}) collective-permute-start(bf16[1280,512]{1,0:T(8,128)(2,1)} %get-tuple-element.48), channel_id=1, source_target_pairs={{0,16},{8,24},{16,0},{24,8},{1,17},{9,25},{17,1},{25,9},{2,18},{10... | collective-permute-start | bytes 3932168 | tf_op jit(solution)/shard_map/ppermute | solution.py:428
  11.8 0.9 reshape.27.left
  12.7 0.6 pad_add_fusion.where.refs_0_
  13.3 0.7 copy-done.9
  14.0 1.4 %collective-permute-done.refs_0_ = bf16[160,512]{1,0:T(8,128)(2,1)S(1)} collective-permute-done((bf16[160,512]{1,0:T(8,128)(2,1)}, bf16[160,512]{1,0:T(8,128)(2,1)S(1)}, u32[]{:S(2)}, u32[]{:S(2)}) %collective-permute-start) | collective-permute-done | bytes 163872 | tf_op jit(solution)/shard_map/ppermute | solution.py:428
  15.4 3.1 %collective-permute-start.3 = (bf16[1,64,512]{2,1,0:T(8,128)(2,1)S(1)}, bf16[1,64,512]{2,1,0:T(8,128)(2,1)S(1)}, u32[]{:S(2)}, u32[]{:S(2)}) collective-permute-start(bf16[1,64,512]{2,1,0:T(8,128)(2,1)S(1)} %get-tuple-element.41), channel_id=1, source_target_pairs={{0,4},{1,5},{2,6},{3,7},{4,0},{5,1},{6,2},{7,3},{8,12},{9,13},{10,... | collective-permute-start | bytes 196616 | tf_op jit(solution)/shard_map/ppermute | solution.py:27
  18.6 3.3 %shard_map.101.refs_2_ = f32[8,896]{1,0:T(8,128)} custom-call(s32[2]{0:T(128)} %pad_add_fusion.where.refs_0_, bf16[448,512]{1,0:T(8,128)(2,1)} %reshape.27.left, bf16[896,4096]{1,0:T(8,128)(2,1)} %tok.17, f32[8,128]{1,0:T(8,128)} %copy-done.13), custom_call_target="tpu_custom_call" | custom-call | flops 411041792 | bytes 3670016 | tf_op jit(solution)/shard_map/pallas_call | solution.py:188
  21.9 0.7 copy-done.7
  22.6 0.6 copy-done.14
  23.2 1.6 %collective-permute-start.4 = (bf16[2,64,512]{2,1,0:T(8,128)(2,1)S(1)}, bf16[2,64,512]{2,1,0:T(8,128)(2,1)S(1)}, u32[]{:S(2)}, u32[]{:S(2)}) collective-permute-start(bf16[2,64,512]{2,1,0:T(8,128)(2,1)S(1)} %get-tuple-element.44), channel_id=1, source_target_pairs={{0,2},{1,3},{2,0},{3,1},{4,6},{5,7},{6,4},{7,5},{8,10},{9,11},{10,... | collective-permute-start | bytes 393224 | tf_op jit(solution)/shard_map/ppermute | solution.py:27
  24.8 2.5 %collective-permute-start.5 = (f32[8,896]{1,0:T(8,128)S(1)}, f32[8,896]{1,0:T(8,128)S(1)}, u32[]{:S(2)}, u32[]{:S(2)}) collective-permute-start(f32[8,896]{1,0:T(8,128)S(1)} %copy-done.7), channel_id=1, source_target_pairs={{0,4},{1,5},{2,6},{3,7},{4,0},{5,1},{6,2},{7,3},{8,12},{9,13},{10,... | collective-permute-start | bytes 86024 | tf_op jit(solution)/shard_map/ppermute | solution.py:27
  27.2 3.2 %shard_map.103 = (bf16[2304,512]{1,0:T(8,128)(2,1)}, f32[8,128]{1,0:T(8,128)}) custom-call(bf16[4096,512]{1,0:T(8,128)(2,1)} %wt.7, f32[8,128]{1,0:T(8,128)} %copy-done.14), custom_call_target="tpu_custom_call" | custom-call | flops 1 | bytes 9437184 | tf_op jit(solution)/shard_map/pallas_call | solution.py:93
  30.4 1.6 %collective-permute-start.13 = (bf16[2304,512]{1,0:T(8,128)(2,1)}, bf16[2304,512]{1,0:T(8,128)(2,1)}, u32[]{:S(2)}, u32[]{:S(2)}) collective-permute-start(bf16[2304,512]{1,0:T(8,128)(2,1)} %get-tuple-element.56), channel_id=1, source_target_pairs={{0,16},{8,24},{16,0},{24,8},{1,17},{9,25},{17,1},{25,9},{2,18},{10... | collective-permute-start | bytes 7077896 | tf_op jit(solution)/shard_map/ppermute | solution.py:428
  32.0 2.9 %reshape.28.refs_3_.rights.refs_1_ = bf16[448,2048]{1,0:T(8,128)(2,1)S(1)} reshape(bf16[112,4,2048]{2,1,0:T(4,128)(2,1)} %param.15) | data formatting | bytes 3670016 | tf_op jit(solution)/shard_map/reshape | solution.py:448
  35.0 1.6 %collective-permute-start.6 = (bf16[4,64,512]{2,1,0:T(8,128)(2,1)S(1)}, bf16[4,64,512]{2,1,0:T(8,128)(2,1)S(1)}, u32[]{:S(2)}, u32[]{:S(2)}) collective-permute-start(bf16[4,64,512]{2,1,0:T(8,128)(2,1)S(1)} %get-tuple-element.47), channel_id=1, source_target_pairs={{0,1},{1,0},{2,3},{3,2},{4,5},{5,4},{6,7},{7,6},{8,9},{9,8},{10,11... | collective-permute-start | bytes 786440 | tf_op jit(solution)/shard_map/ppermute | solution.py:27
  36.6 0.7 constant_dynamic-update-slice_fusion.3
  37.3 3.1 %collective-permute-done.8 = f32[8,896]{1,0:T(8,128)S(1)} collective-permute-done((f32[8,896]{1,0:T(8,128)S(1)}, f32[8,896]{1,0:T(8,128)S(1)}, u32[]{:S(2)}, u32[]{:S(2)}) %collective-permute-start.8) | collective-permute-done | bytes 28704 | tf_op jit(solution)/shard_map/ppermute | solution.py:27
  40.5 1.7 %shard_map.105 = (bf16[256,512]{1,0:T(8,128)(2,1)}, f32[8,128]{1,0:T(8,128)}) custom-call(bf16[4096,512]{1,0:T(8,128)(2,1)} %wt.7, f32[8,128]{1,0:T(8,128)} %copy-done.10), custom_call_target="tpu_custom_call" | custom-call | flops 1 | bytes 1048576 | tf_op jit(solution)/shard_map/pallas_call | solution.py:93
  42.2 1.3 %collective-permute-done.7.refs_1_ = bf16[1280,512]{1,0:T(8,128)(2,1)} collective-permute-done((bf16[1280,512]{1,0:T(8,128)(2,1)}, bf16[1280,512]{1,0:T(8,128)(2,1)}, u32[]{:S(2)}, u32[]{:S(2)}) %collective-permute-start.7) | collective-permute-done | bytes 1310752 | tf_op jit(solution)/shard_map/ppermute | solution.py:428
  43.6 0.9 copy-done.4
  44.5 0.7 copy-done.12
  45.2 0.6 shard_map.106
  45.8 0.7 copy-done.5
  46.5 2.5 %constant_dynamic-update-slice_fusion.2.wt = bf16[1536,512]{1,0:T(8,128)(2,1)} fusion(bf16[1536,512]{1,0:T(8,128)(2,1)} %constant_dynamic-update-slice_fusion.3, bf16[1280,512]{1,0:T(8,128)(2,1)} %get-tuple-element.58), kind=kLoop, calls=%fused_computation.8 | loop fusion | bytes 2621440 | tf_op jit(solution)/shard_map/concatenate | solution.py:503
  49.0 0.5 collective-permute-start.9
  49.5 1.9 %collective-permute-start.11 = (f32[8,896]{1,0:T(8,128)S(1)}, f32[8,896]{1,0:T(8,128)S(1)}, u32[]{:S(2)}, u32[]{:S(2)}) collective-permute-start(f32[8,896]{1,0:T(8,128)S(1)} %add.18.refs_3_), channel_id=1, source_target_pairs={{0,1},{1,0},{2,3},{3,2},{4,5},{5,4},{6,7},{7,6},{8,9},{9,8},{10,11... | collective-permute-start | bytes 86024 | tf_op jit(solution)/shard_map/ppermute | solution.py:27
  51.4 2.0 %collective-permute-done.11 = f32[8,896]{1,0:T(8,128)S(1)} collective-permute-done((f32[8,896]{1,0:T(8,128)S(1)}, f32[8,896]{1,0:T(8,128)S(1)}, u32[]{:S(2)}, u32[]{:S(2)}) %collective-permute-start.11) | collective-permute-done | bytes 28704 | tf_op jit(solution)/shard_map/ppermute | solution.py:27
  53.4 0.1 shard_map.108.spread.refs_0_
  53.6 1.4 %pad_maximum_fusion.left = bf16[8,128,512]{2,1,0:T(8,128)(2,1)S(1)} fusion(bf16[8,64,512]{2,1,0:T(8,128)(2,1)} %collective-permute-done.9, bf16[8,64,512]{2,1,0:T(8,128)(2,1)S(1)} %get-tuple-element.52), kind=kLoop, calls=%fused_computation | loop fusion | flops 2097152 | bytes 2097152 | tf_op jit(solution)/shard_map/concatenate | solution.py:465
  55.1 1.4 %shard_map.107.left = bf16[4096,128]{1,0:T(8,128)(2,1)S(1)} custom-call(s32[2]{0:T(128)S(1)} %copy-done.8, bf16[8,128,512]{2,1,0:T(8,128)(2,1)S(1)} %pad_maximum_fusion.left), custom_call_target="tpu_custom_call" | custom-call | flops 1 | bytes 1 | tf_op jit(solution)/shard_map/pallas_call | solution.py:221
  56.5 10.5 %shard_map.109 = (bf16[896,2048]{1,0:T(8,128)(2,1)}, bf16[4096,512]{1,0:T(8,128)(2,1)}, f32[8,128]{1,0:T(8,128)S(1)}) custom-call(s32[1]{0:T(128)} %bitcast.where, bf16[896,4096]{1,0:T(8,128)(2,1)} %tok.17, bf16[4096,512]{1,0:T(8,128)(2,1)} %wt.7, bf16[4096,128]{1,0:T(8,128)(2,1)S(1)} %shard_map.107.left, ...), custom_call_target="tpu_custom_call" | custom-call | flops 1 | bytes 1 | tf_op jit(solution)/shard_map/pallas_call | solution.py:334
  67.0 1.3 %copy-done.3 = bf16[896,448]{1,0:T(8,128)(2,1)S(1)} copy-done((bf16[896,448]{1,0:T(8,128)(2,1)S(1)}, bf16[896,448]{1,0:T(8,128)(2,1)}, u32[]{:S(2)}) %copy-start.3) | copy-done | bytes 802840
  68.3 9.9 %shard_map.110 = (bf16[896,2048]{1,0:T(8,128)(2,1)}, f32[8,128]{1,0:T(8,128)S(1)}) custom-call(s32[1]{0:T(128)} %bitcast.5.where, bf16[896,4096]{1,0:T(8,128)(2,1)} %tok.17, bf16[4096,512]{1,0:T(8,128)(2,1)} %get-tuple-element.59.wt, bf16[4096,128]{1,0:T(8,128)(2,1)S(1)} %shard_map.107.left, ...), custom_call_target="tpu_custom_call", output_to_operand_aliasing={{0}: (8, {})} | custom-call | flops 1 | bytes 1 | tf_op jit(solution)/shard_map/pallas_call | solution.py:334
  78.2 3.9 %shard_map.111.refs_2_.refs_0_ = f32[896,512]{1,0:T(8,128)S(1)} custom-call(s32[1]{0:T(128)} %bitcast.4.where, bf16[896,4096]{1,0:T(8,128)(2,1)S(1)} %bitcast.8, bf16[1536,512]{1,0:T(8,128)(2,1)} %constant_dynamic-update-slice_fusion.2.wt, bf16[4096,128]{1,0:T(8,128)(2,1)S(1)} %shard_map.107.left, ...), custom_call_target="tpu_custom_call" | custom-call | flops 1 | bytes 1 | tf_op jit(solution)/shard_map/pallas_call | solution.py:334
  82.1 3.9 %shard_map.112.refs_1_.refs_0_ = f32[896,512]{1,0:T(8,128)S(1)} custom-call(s32[1]{0:T(128)} %bitcast.3.where, bf16[896,4096]{1,0:T(8,128)(2,1)S(1)} %bitcast.8, bf16[1536,512]{1,0:T(8,128)(2,1)} %collective-permute-done.14.wt, bf16[4096,128]{1,0:T(8,128)(2,1)S(1)} %shard_map.107.left, bf16[128,2048]{1,0:T(8,128)(2,1)S(1)} %constant_dynamic-update-slice_fusion.right, ...), custom_call_target="tpu_custom_call" | custom-call | flops 1 | bytes 1 | tf_op jit(solution)/shard_map/pallas_call | solution.py:334
  86.0 7.9 %collective-permute-done.13.refs_0_ = bf16[2304,512]{1,0:T(8,128)(2,1)} collective-permute-done((bf16[2304,512]{1,0:T(8,128)(2,1)}, bf16[2304,512]{1,0:T(8,128)(2,1)}, u32[]{:S(2)}, u32[]{:S(2)}) %collective-permute-start.13) | collective-permute-done | bytes 2359328 | tf_op jit(solution)/shard_map/ppermute | solution.py:428
  93.9 1.7 %collective-permute-start.12 = (bf16[256,512]{1,0:T(8,128)(2,1)S(1)}, bf16[256,512]{1,0:T(8,128)(2,1)S(1)}, u32[]{:S(2)}, u32[]{:S(2)}) collective-permute-start(bf16[256,512]{1,0:T(8,128)(2,1)S(1)} %copy-done.6), channel_id=1, source_target_pairs={{0,16},{8,24},{16,0},{24,8},{1,17},{9,25},{17,1},{25,9},{2,18},{10... | collective-permute-start | bytes 786440 | tf_op jit(solution)/shard_map/ppermute | solution.py:428
  95.7 4.6 %shard_map.114.refs_1_.before = f32[896,512]{1,0:T(8,128)S(1)} custom-call(s32[1]{0:T(128)} %bitcast.4.where, bf16[896,4096]{1,0:T(8,128)(2,1)S(1)} %bitcast.8, bf16[2304,512]{1,0:T(8,128)(2,1)} %shard_map.113.wt, bf16[4096,128]{1,0:T(8,128)(2,1)S(1)} %shard_map.107.left, ...), custom_call_target="tpu_custom_call", output_to_operand_aliasing={{}: (5, {})} | custom-call | flops 1 | bytes 1 | tf_op jit(solution)/shard_map/pallas_call | solution.py:334
  100.3 3.0 %shard_map.115.refs_1_.before = f32[896,512]{1,0:T(8,128)S(1)} custom-call(s32[1]{0:T(128)} %bitcast.3.where, bf16[896,4096]{1,0:T(8,128)(2,1)S(1)} %bitcast.8, bf16[2304,512]{1,0:T(8,128)(2,1)S(1)} %collective-permute-done.15.wt, bf16[4096,128]{1,0:T(8,128)(2,1)S(1)} %shard_map.107.left, ...), custom_call_target="tpu_custom_call", output_to_operand_aliasing={{}: (5, {})} | custom-call | flops 1 | bytes 1 | tf_op jit(solution)/shard_map/pallas_call | solution.py:334
  103.3 0.3 collective-permute-start.16
  103.6 1.4 %shard_map.117.acts = bf16[896,2048]{1,0:T(8,128)(2,1)} custom-call(s32[1]{0:T(128)} %bitcast.4.where, bf16[896,4096]{1,0:T(8,128)(2,1)S(1)} %bitcast.8, bf16[256,512]{1,0:T(8,128)(2,1)S(1)} %shard_map.116.wt, bf16[4096,128]{1,0:T(8,128)(2,1)S(1)} %shard_map.107.left, ...), custom_call_target="tpu_custom_call", output_to_operand_aliasing={{}: (6, {})} | custom-call | flops 1 | bytes 1 | tf_op jit(solution)/shard_map/pallas_call | solution.py:334
  105.0 1.4 %shard_map.118 = bf16[896,2048]{1,0:T(8,128)(2,1)} custom-call(s32[1]{0:T(128)} %bitcast.3.where, bf16[896,4096]{1,0:T(8,128)(2,1)S(1)} %bitcast.8, bf16[256,512]{1,0:T(8,128)(2,1)S(1)} %collective-permute-done.16.wt, bf16[4096,128]{1,0:T(8,128)(2,1)S(1)} %shard_map.107.left, ...), custom_call_target="tpu_custom_call", output_to_operand_aliasing={{}: (6, {})} | custom-call | flops 1 | bytes 1 | tf_op jit(solution)/shard_map/pallas_call | solution.py:334
  (69 shorter events, 0.3 us)
Async XLA Ops:
  0.6 12.7 %collective-permute-start.2 = (bf16[4096,512]{1,0:T(8,128)(2,1)}, bf16[4096,512]{1,0:T(8,128)(2,1)}, u32[]{:S(2)}, u32[]{:S(2)}) collective-permute-start(bf16[4096,512]{1,0:T(8,128)(2,1)} %wt.7), channel_id=1, source_target_pairs={{0,8},{8,0},{16,24},{24,16},{1,9},{9,1},{17,25},{25,17},{2,10},{10... | collective-permute-start | bytes 12582920 | tf_op jit(solution)/shard_map/ppermute | solution.py:27
  2.1 11.9 %collective-permute-start.1 = (bf16[256,512]{1,0:T(8,128)(2,1)S(1)}, bf16[256,512]{1,0:T(8,128)(2,1)S(1)}, u32[]{:S(2)}, u32[]{:S(2)}) collective-permute-start(bf16[256,512]{1,0:T(8,128)(2,1)S(1)} %slice.18), channel_id=1, source_target_pairs={{0,16},{8,24},{16,0},{24,8},{1,17},{9,25},{17,1},{25,9},{2,18},{10... | collective-permute-start | bytes 786440 | tf_op jit(solution)/shard_map/ppermute | solution.py:428
  7.2 8.2 %collective-permute-start = (bf16[160,512]{1,0:T(8,128)(2,1)}, bf16[160,512]{1,0:T(8,128)(2,1)S(1)}, u32[]{:S(2)}, u32[]{:S(2)}) collective-permute-start(bf16[160,512]{1,0:T(8,128)(2,1)} %get-tuple-element.34), channel_id=1, source_target_pairs={{0,16},{8,24},{16,0},{24,8},{1,17},{9,25},{17,1},{25,9},{2,18},{10... | collective-permute-start | bytes 491528 | tf_op jit(solution)/shard_map/ppermute | solution.py:428
  7.3 4.5 %copy-start.15 = (bf16[112,4,512]{2,1,0:T(4,128)(2,1)S(1)}, bf16[112,4,512]{2,1,0:T(4,128)(2,1)}, u32[]{:S(2)}) copy-start(bf16[112,4,512]{2,1,0:T(4,128)(2,1)} %param.14) | copy-start | bytes 1376260
  9.7 33.9 %collective-permute-start.7 = (bf16[1280,512]{1,0:T(8,128)(2,1)}, bf16[1280,512]{1,0:T(8,128)(2,1)}, u32[]{:S(2)}, u32[]{:S(2)}) collective-permute-start(bf16[1280,512]{1,0:T(8,128)(2,1)} %get-tuple-element.48), channel_id=1, source_target_pairs={{0,16},{8,24},{16,0},{24,8},{1,17},{9,25},{17,1},{25,9},{2,18},{10... | collective-permute-start | bytes 3932168 | tf_op jit(solution)/shard_map/ppermute | solution.py:428
  13.3 0.7 copy-start.9
  14.0 1.4 %copy-start.17 = (bf16[32,512]{1,0:T(8,128)(2,1)S(1)}, bf16[32,512]{1,0:T(8,128)(2,1)}, u32[]{:S(2)}) copy-start(bf16[32,512]{1,0:T(8,128)(2,1)} %get-tuple-element.33) | copy-start | bytes 98308
  14.0 4.5 %copy-start.16 = (bf16[32,2048]{1,0:T(8,128)(2,1)S(1)}, bf16[32,2048]{1,0:T(8,128)(2,1)}, u32[]{:S(2)}) copy-start(bf16[32,2048]{1,0:T(8,128)(2,1)} %get-tuple-element.42) | copy-start | bytes 393220
  15.4 3.1 %copy-start.13 = (f32[8,128]{1,0:T(8,128)}, f32[8,128]{1,0:T(8,128)S(1)}, u32[]{:S(2)}) copy-start(f32[8,128]{1,0:T(8,128)S(1)} %get-tuple-element.43.after) | copy-start | bytes 12292
  15.4 6.4 %collective-permute-start.3 = (bf16[1,64,512]{2,1,0:T(8,128)(2,1)S(1)}, bf16[1,64,512]{2,1,0:T(8,128)(2,1)S(1)}, u32[]{:S(2)}, u32[]{:S(2)}) collective-permute-start(bf16[1,64,512]{2,1,0:T(8,128)(2,1)S(1)} %get-tuple-element.41), channel_id=1, source_target_pairs={{0,4},{1,5},{2,6},{3,7},{4,0},{5,1},{6,2},{7,3},{8,12},{9,13},{10,... | collective-permute-start | bytes 196616 | tf_op jit(solution)/shard_map/ppermute | solution.py:27
  21.8 0.7 copy-start.7
  22.6 0.6 copy-start.14
  23.2 11.8 %collective-permute-start.4 = (bf16[2,64,512]{2,1,0:T(8,128)(2,1)S(1)}, bf16[2,64,512]{2,1,0:T(8,128)(2,1)S(1)}, u32[]{:S(2)}, u32[]{:S(2)}) collective-permute-start(bf16[2,64,512]{2,1,0:T(8,128)(2,1)S(1)} %get-tuple-element.44), channel_id=1, source_target_pairs={{0,2},{1,3},{2,0},{3,1},{4,6},{5,7},{6,4},{7,5},{8,10},{9,11},{10,... | collective-permute-start | bytes 393224 | tf_op jit(solution)/shard_map/ppermute | solution.py:27
  24.8 10.2 %collective-permute-start.5 = (f32[8,896]{1,0:T(8,128)S(1)}, f32[8,896]{1,0:T(8,128)S(1)}, u32[]{:S(2)}, u32[]{:S(2)}) collective-permute-start(f32[8,896]{1,0:T(8,128)S(1)} %copy-done.7), channel_id=1, source_target_pairs={{0,4},{1,5},{2,6},{3,7},{4,0},{5,1},{6,2},{7,3},{8,12},{9,13},{10,... | collective-permute-start | bytes 86024 | tf_op jit(solution)/shard_map/ppermute | solution.py:27
  30.4 4.6 %copy-start.11 = (f32[8,128]{1,0:T(8,128)S(1)}, f32[8,128]{1,0:T(8,128)}, u32[]{:S(2)}) copy-start(f32[8,128]{1,0:T(8,128)} %get-tuple-element.46.refs_2_) | copy-start | bytes 12292
  30.4 63.5 %collective-permute-start.13 = (bf16[2304,512]{1,0:T(8,128)(2,1)}, bf16[2304,512]{1,0:T(8,128)(2,1)}, u32[]{:S(2)}, u32[]{:S(2)}) collective-permute-start(bf16[2304,512]{1,0:T(8,128)(2,1)} %get-tuple-element.56), channel_id=1, source_target_pairs={{0,16},{8,24},{16,0},{24,8},{1,17},{9,25},{17,1},{25,9},{2,18},{10... | collective-permute-start | bytes 7077896 | tf_op jit(solution)/shard_map/ppermute | solution.py:428
  34.9 7.2 %copy-start = (bf16[448,2048]{1,0:T(8,128)(2,1)}, bf16[448,2048]{1,0:T(8,128)(2,1)S(1)}, u32[]{:S(2)}) copy-start(bf16[448,2048]{1,0:T(8,128)(2,1)S(1)} %reshape.28.refs_3_.rights.refs_1_) | copy-start | bytes 5505028
  35.0 5.4 %copy-start.10 = (f32[8,128]{1,0:T(8,128)}, f32[8,128]{1,0:T(8,128)S(1)}, u32[]{:S(2)}) copy-start(f32[8,128]{1,0:T(8,128)S(1)} %get-tuple-element.49.after) | copy-start | bytes 12292
  35.0 7.1 %collective-permute-start.6 = (bf16[4,64,512]{2,1,0:T(8,128)(2,1)S(1)}, bf16[4,64,512]{2,1,0:T(8,128)(2,1)S(1)}, u32[]{:S(2)}, u32[]{:S(2)}) collective-permute-start(bf16[4,64,512]{2,1,0:T(8,128)(2,1)S(1)} %get-tuple-element.47), channel_id=1, source_target_pairs={{0,1},{1,0},{2,3},{3,2},{4,5},{5,4},{6,7},{7,6},{8,9},{9,8},{10,11... | collective-permute-start | bytes 786440 | tf_op jit(solution)/shard_map/ppermute | solution.py:27
  36.6 3.9 %collective-permute-start.8 = (f32[8,896]{1,0:T(8,128)S(1)}, f32[8,896]{1,0:T(8,128)S(1)}, u32[]{:S(2)}, u32[]{:S(2)}) collective-permute-start(f32[8,896]{1,0:T(8,128)S(1)} %add.17.refs_1_), channel_id=1, source_target_pairs={{0,2},{1,3},{2,0},{3,1},{4,6},{5,7},{6,4},{7,5},{8,10},{9,11},{10,... | collective-permute-start | bytes 86024 | tf_op jit(solution)/shard_map/ppermute | solution.py:27
  43.6 1.0 copy-start.4
  44.5 0.7 copy-start.12
  45.8 0.7 copy-start.5
  49.0 33.1 %collective-permute-start.14 = (bf16[1536,512]{1,0:T(8,128)(2,1)}, bf16[1536,512]{1,0:T(8,128)(2,1)}, u32[]{:S(2)}, u32[]{:S(2)}) collective-permute-start(bf16[1536,512]{1,0:T(8,128)(2,1)} %constant_dynamic-update-slice_fusion.2.wt), channel_id=1, source_target_pairs={{0,8},{8,0},{16,24},{24,16},{1,9},{9,1},{17,25},{25,17},{2,10},{10... | collective-permute-start | bytes 4718600 | tf_op jit(solution)/shard_map/ppermute | solution.py:27
  49.0 4.6 %collective-permute-start.9 = (bf16[8,64,512]{2,1,0:T(8,128)(2,1)S(1)}, bf16[8,64,512]{2,1,0:T(8,128)(2,1)}, u32[]{:S(2)}, u32[]{:S(2)}) collective-permute-start(bf16[8,64,512]{2,1,0:T(8,128)(2,1)S(1)} %get-tuple-element.52), channel_id=1, source_target_pairs={{0,8},{8,0},{16,24},{24,16},{1,9},{9,1},{17,25},{25,17},{2,10},{10... | collective-permute-start | bytes 1572872 | tf_op jit(solution)/shard_map/ppermute | solution.py:27
  49.5 3.9 %collective-permute-start.11 = (f32[8,896]{1,0:T(8,128)S(1)}, f32[8,896]{1,0:T(8,128)S(1)}, u32[]{:S(2)}, u32[]{:S(2)}) collective-permute-start(f32[8,896]{1,0:T(8,128)S(1)} %add.18.refs_3_), channel_id=1, source_target_pairs={{0,1},{1,0},{2,3},{3,2},{4,5},{5,4},{6,7},{7,6},{8,9},{9,8},{10,11... | collective-permute-start | bytes 86024 | tf_op jit(solution)/shard_map/ppermute | solution.py:27
  51.4 3.6 %collective-permute-start.10 = (bf16[64,2048]{1,0:T(8,128)(2,1)S(1)}, bf16[64,2048]{1,0:T(8,128)(2,1)S(1)}, u32[]{:S(2)}, u32[]{:S(2)}) collective-permute-start(bf16[64,2048]{1,0:T(8,128)(2,1)S(1)} %get-tuple-element.53), channel_id=1, source_target_pairs={{0,8},{8,0},{16,24},{24,16},{1,9},{9,1},{17,25},{25,17},{2,10},{10... | collective-permute-start | bytes 786440 | tf_op jit(solution)/shard_map/ppermute | solution.py:27
  53.4 1.7 %copy-start.8 = (s32[2]{0:T(128)S(1)}, s32[2]{0:T(128)}, u32[]{:S(2)}) copy-start(s32[2]{0:T(128)} %pad_add_fusion.where.refs_0_) | copy-start | bytes 28
  53.6 2.9 %copy-start.2 = (bf16[896,448]{1,0:T(8,128)(2,1)}, bf16[896,448]{1,0:T(8,128)(2,1)S(1)}, u32[]{:S(2)}) copy-start(bf16[896,448]{1,0:T(8,128)(2,1)S(1)} %shard_map.108.spread.refs_0_) | copy-start | bytes 2408452
  67.0 11.2 %slice-start = ((s8[7340032]{0:T(1024)(128)(4,1)}), s8[4194304]{0:T(1024)(128)(4,1)S(1)}, s32[]{:S(2)}) async-start(s8[7340032]{0:T(1024)(128)(4,1)} %bitcast.7), calls=%async_computation | async-start | bytes 8388608
  67.0 1.3 %copy-start.3 = (bf16[896,448]{1,0:T(8,128)(2,1)S(1)}, bf16[896,448]{1,0:T(8,128)(2,1)}, u32[]{:S(2)}) copy-start(bf16[896,448]{1,0:T(8,128)(2,1)} %copy-done.2) | copy-start | bytes 2408452
  68.3 9.9 %slice-start.1 = ((s8[7340032]{0:T(1024)(128)(4,1)}), s8[3145728]{0:T(1024)(128)(4,1)S(1)}, s32[]{:S(2)}) async-start(s8[7340032]{0:T(1024)(128)(4,1)} %bitcast.7), calls=%async_computation.1 | async-start | bytes 6291456
  68.3 9.9 %copy-start.1 = (bf16[448,2048]{1,0:T(8,128)(2,1)S(1)}, bf16[448,2048]{1,0:T(8,128)(2,1)}, u32[]{:S(2)}) copy-start(bf16[448,2048]{1,0:T(8,128)(2,1)} %copy-done) | copy-start | bytes 5505028
  86.0 7.9 %copy-start.6 = (bf16[256,512]{1,0:T(8,128)(2,1)S(1)}, bf16[256,512]{1,0:T(8,128)(2,1)}, u32[]{:S(2)}) copy-start(bf16[256,512]{1,0:T(8,128)(2,1)} %copy-done.5) | copy-start | bytes 786436
  93.9 6.4 %collective-permute-start.15 = (bf16[2304,512]{1,0:T(8,128)(2,1)}, bf16[2304,512]{1,0:T(8,128)(2,1)S(1)}, u32[]{:S(2)}, u32[]{:S(2)}) collective-permute-start(bf16[2304,512]{1,0:T(8,128)(2,1)} %shard_map.113.wt), channel_id=1, source_target_pairs={{0,8},{8,0},{16,24},{24,16},{1,9},{9,1},{17,25},{25,17},{2,10},{10... | collective-permute-start | bytes 7077896 | tf_op jit(solution)/shard_map/ppermute | solution.py:27
  93.9 9.4 %collective-permute-start.12 = (bf16[256,512]{1,0:T(8,128)(2,1)S(1)}, bf16[256,512]{1,0:T(8,128)(2,1)S(1)}, u32[]{:S(2)}, u32[]{:S(2)}) collective-permute-start(bf16[256,512]{1,0:T(8,128)(2,1)S(1)} %copy-done.6), channel_id=1, source_target_pairs={{0,16},{8,24},{16,0},{24,8},{1,17},{9,25},{17,1},{25,9},{2,18},{10... | collective-permute-start | bytes 786440 | tf_op jit(solution)/shard_map/ppermute | solution.py:428
  103.3 1.7 %collective-permute-start.16 = (bf16[256,512]{1,0:T(8,128)(2,1)S(1)}, bf16[256,512]{1,0:T(8,128)(2,1)S(1)}, u32[]{:S(2)}, u32[]{:S(2)}) collective-permute-start(bf16[256,512]{1,0:T(8,128)(2,1)S(1)} %shard_map.116.wt), channel_id=1, source_target_pairs={{0,8},{8,0},{16,24},{24,16},{1,9},{9,1},{17,25},{25,17},{2,10},{10... | collective-permute-start | bytes 786440 | tf_op jit(solution)/shard_map/ppermute | solution.py:27

commit v6 on v5

--- a/solution.py
+++ b/solution.py
@@ -436,9 +436,9 @@
     piece, mark = cut(weight, *plan[1][1:], mark)
     arrived.append(send(1, piece))
     tall = count * rank
-    sibling, mark = gate(swap(weight, "pop", 1), mark)
     arrived[0], mark = gate(arrived[0], mark)
     packed, mark = gate(packed, mark)
+    sibling = swap(weight, "pop", 1)
     lefts, rights = unpack(packed, tall, slab, old_right.shape[2])
     left, right = jnp.concatenate([left, lefts], 0), jnp.concatenate([right, rights], 0)
     for bit in bits(chips, 2):
@@ -453,7 +453,7 @@
         partial = proj
         proj = proj + swap(proj, "col", bit)
         if turn_at == 0:
-            left, right, mark = gate_all([left, right], partial)
+            left, right, sibling, mark = gate_all([left, right, sibling], partial)
             right = jnp.concatenate([right, swap(right, "pop", 1)], 0)
             piece, early = cut(weight, *plan[2][1:], mark)
             arrived.append(send(2, piece))

time: 107 us -> 107 us (level)
  other arithmetic: 2.22 us -> 0.78 us
  waiting for transfers between devices: 15.7 us -> 17 us
    concatenate x1, other arithmetic: 1.44 us -> 0.07 us  [local(): left = turn(jnp.concatenate([left, swap(left, 'pop', 1)], 1), where)]
    ppermute x12, waiting for transfers between devices: 5.11 us -> 6.36 us  [swap(): lax.ppermute(array, axis, [(i, i ^ bit) for i in range(lax.axis_size(axis...]
    unnamed x42 -> x44, local copies, waits for them, and re-layouts: 6.52 us -> 6.5 us
  transfers between devices with their start and end apart: 17 -> 17, of which waited for: 5 -> 6; matrix products, arithmetic and copies ran while one was open for 10% -> 8% of each run, Pallas kernels for 49% -> 49%
where the time goes in v6:
time: 107 us
  Pallas kernels  53.6 us (50%)
  starting transfers between devices  20.2 us (19%)
  waiting for transfers between devices  17 us (16%)
  local copies, waits for them, and re-layouts  13.8 us (13%)
  between operations  1.22 us (1%)
    pallas_call x8, Pallas kernels, call(): pl.pallas_call(kernel, grid_spec=pltpu.PrefetchScalarGridSpec(num_scalar_...  38.5 us
    ppermute x12, starting transfers between devices, swap(): lax.ppermute(array, axis, [(i, i ^ bit) for i in range(lax.axis_size(axis...  12.1 us
    ppermute x5, waiting for transfers between devices, send(): return lax.ppermute(piece, 'pop', turn)  10.6 us
    ppermute x5, starting transfers between devices, send(): return lax.ppermute(piece, 'pop', turn)  8.07 us
    pallas_call x3, Pallas kernels, cut(): pl.pallas_call(functools.partial(cut_kernel, start), in_specs=[anywhere()...  7.28 us
    unnamed x44, local copies, waits for them, and re-layouts  6.5 us
    ppermute x12, waiting for transfers between devices, swap(): lax.ppermute(array, axis, [(i, i ^ bit) for i in range(lax.axis_size(axis...  6.36 us
    pallas_call x1, Pallas kernels, project(): pl.pallas_call(functools.partial(proj_kernel, rank, each), grid_spec=pltp...  3.26 us
  transfers between devices with their start and end apart: 17, of which 6 were waited for; matrix products, arithmetic and copies ran while one was open for 8% of the time, Pallas kernels for 49%

profile of v6, /device:TPU:0, one launch (start us, length us, event | category | flops | bytes accessed | tf_op | source)
XLA Modules:
  0.0 106.5 jit_solution(5095738854977259876)
XLA Ops:
  0.6 0.5 collective-permute-start.3
  1.1 1.0 slice.18
  2.1 2.6 %collective-permute-start.1 = (bf16[256,512]{1,0:T(8,128)(2,1)S(1)}, bf16[256,512]{1,0:T(8,128)(2,1)S(1)}, u32[]{:S(2)}, u32[]{:S(2)}) collective-permute-start(bf16[256,512]{1,0:T(8,128)(2,1)S(1)} %slice.18), channel_id=1, source_target_pairs={{0,16},{8,24},{16,0},{24,8},{1,17},{9,25},{17,1},{25,9},{2,18},{10... | collective-permute-start | bytes 786440 | tf_op jit(solution)/shard_map/ppermute | solution.py:428
  4.7 2.5 %shard_map.95 = (bf16[160,512]{1,0:T(8,128)(2,1)}, bf16[32,512]{1,0:T(8,128)(2,1)}, bf16[32,2048]{1,0:T(8,128)(2,1)}, f32[8,128]{1,0:T(8,128)}) custom-call(s32[1,8]{1,0:T(1,128)} %after.1, f32[1,8]{1,0:T(1,128)} %shaping.1, bf16[112,4,512]{2,1,0:T(4,128)(2,1)} %lefts.1, bf16[112,4,2048]{2,1,0:T(4,128)(2,1)} %rights.1, s32[1,8]{1,0:T(1,128)} %after.1), custom_call_target="tpu_custom_call" | custom-call | flops 1 | bytes 1 | tf_op jit(solution)/shard_map/pallas_call | solution.py:140
  7.3 2.4 %shard_map.96 = (bf16[1280,512]{1,0:T(8,128)(2,1)}, f32[8,128]{1,0:T(8,128)}) custom-call(bf16[4096,512]{1,0:T(8,128)(2,1)} %wt.7, f32[8,128]{1,0:T(8,128)} %get-tuple-element.34.after), custom_call_target="tpu_custom_call" | custom-call | flops 1 | bytes 5242880 | tf_op jit(solution)/shard_map/pallas_call | solution.py:93
  9.7 2.1 %collective-permute-start.7 = (bf16[1280,512]{1,0:T(8,128)(2,1)}, bf16[1280,512]{1,0:T(8,128)(2,1)}, u32[]{:S(2)}, u32[]{:S(2)}) collective-permute-start(bf16[1280,512]{1,0:T(8,128)(2,1)} %get-tuple-element.46), channel_id=1, source_target_pairs={{0,16},{8,24},{16,0},{24,8},{1,17},{9,25},{17,1},{25,9},{2,18},{10... | collective-permute-start | bytes 3932168 | tf_op jit(solution)/shard_map/ppermute | solution.py:428
  11.8 0.9 reshape.27.left
  12.7 0.6 pad_add_fusion.where.refs_0_
  13.3 0.7 copy-done.10
  13.9 1.4 %collective-permute-done.refs_0_ = bf16[160,512]{1,0:T(8,128)(2,1)S(1)} collective-permute-done((bf16[160,512]{1,0:T(8,128)(2,1)}, bf16[160,512]{1,0:T(8,128)(2,1)S(1)}, u32[]{:S(2)}, u32[]{:S(2)}) %collective-permute-start) | collective-permute-done | bytes 163872 | tf_op jit(solution)/shard_map/ppermute | solution.py:428
  15.4 3.1 %collective-permute-start.2 = (bf16[1,64,512]{2,1,0:T(8,128)(2,1)S(1)}, bf16[1,64,512]{2,1,0:T(8,128)(2,1)S(1)}, u32[]{:S(2)}, u32[]{:S(2)}) collective-permute-start(bf16[1,64,512]{2,1,0:T(8,128)(2,1)S(1)} %get-tuple-element.39), channel_id=1, source_target_pairs={{0,4},{1,5},{2,6},{3,7},{4,0},{5,1},{6,2},{7,3},{8,12},{9,13},{10,... | collective-permute-start | bytes 196616 | tf_op jit(solution)/shard_map/ppermute | solution.py:27
  18.6 3.3 %shard_map.100.refs_3_ = f32[8,896]{1,0:T(8,128)} custom-call(s32[2]{0:T(128)} %pad_add_fusion.where.refs_0_, bf16[448,512]{1,0:T(8,128)(2,1)} %reshape.27.left, bf16[896,4096]{1,0:T(8,128)(2,1)} %tok.17, f32[8,128]{1,0:T(8,128)} %copy-done.14), custom_call_target="tpu_custom_call" | custom-call | flops 411041792 | bytes 3670016 | tf_op jit(solution)/shard_map/pallas_call | solution.py:188
  21.9 0.7 copy-done.7
  22.6 0.6 copy-done.15
  23.2 1.6 %collective-permute-start.4 = (bf16[2,64,512]{2,1,0:T(8,128)(2,1)S(1)}, bf16[2,64,512]{2,1,0:T(8,128)(2,1)S(1)}, u32[]{:S(2)}, u32[]{:S(2)}) collective-permute-start(bf16[2,64,512]{2,1,0:T(8,128)(2,1)S(1)} %get-tuple-element.42), channel_id=1, source_target_pairs={{0,2},{1,3},{2,0},{3,1},{4,6},{5,7},{6,4},{7,5},{8,10},{9,11},{10,... | collective-permute-start | bytes 393224 | tf_op jit(solution)/shard_map/ppermute | solution.py:27
  24.8 2.5 %collective-permute-start.5 = (f32[8,896]{1,0:T(8,128)S(1)}, f32[8,896]{1,0:T(8,128)S(1)}, u32[]{:S(2)}, u32[]{:S(2)}) collective-permute-start(f32[8,896]{1,0:T(8,128)S(1)} %copy-done.8), channel_id=1, source_target_pairs={{0,4},{1,5},{2,6},{3,7},{4,0},{5,1},{6,2},{7,3},{8,12},{9,13},{10,... | collective-permute-start | bytes 86024 | tf_op jit(solution)/shard_map/ppermute | solution.py:27
  27.2 3.2 %shard_map.102 = (bf16[2304,512]{1,0:T(8,128)(2,1)}, f32[8,128]{1,0:T(8,128)}) custom-call(bf16[4096,512]{1,0:T(8,128)(2,1)} %wt.7, f32[8,128]{1,0:T(8,128)} %copy-done.15), custom_call_target="tpu_custom_call" | custom-call | flops 1 | bytes 9437184 | tf_op jit(solution)/shard_map/pallas_call | solution.py:93
  30.4 1.6 %collective-permute-start.13 = (bf16[2304,512]{1,0:T(8,128)(2,1)}, bf16[2304,512]{1,0:T(8,128)(2,1)}, u32[]{:S(2)}, u32[]{:S(2)}) collective-permute-start(bf16[2304,512]{1,0:T(8,128)(2,1)} %get-tuple-element.54), channel_id=1, source_target_pairs={{0,16},{8,24},{16,0},{24,8},{1,17},{9,25},{17,1},{25,9},{2,18},{10... | collective-permute-start | bytes 7077896 | tf_op jit(solution)/shard_map/ppermute | solution.py:428
  32.0 2.9 %reshape.28.refs_3_.rights.refs_1_ = bf16[448,2048]{1,0:T(8,128)(2,1)S(1)} reshape(bf16[112,4,2048]{2,1,0:T(4,128)(2,1)} %param.15) | data formatting | bytes 3670016 | tf_op jit(solution)/shard_map/reshape | solution.py:448
  35.1 1.6 %collective-permute-start.6 = (bf16[4,64,512]{2,1,0:T(8,128)(2,1)S(1)}, bf16[4,64,512]{2,1,0:T(8,128)(2,1)S(1)}, u32[]{:S(2)}, u32[]{:S(2)}) collective-permute-start(bf16[4,64,512]{2,1,0:T(8,128)(2,1)S(1)} %get-tuple-element.45), channel_id=1, source_target_pairs={{0,1},{1,0},{2,3},{3,2},{4,5},{5,4},{6,7},{7,6},{8,9},{9,8},{10,11... | collective-permute-start | bytes 786440 | tf_op jit(solution)/shard_map/ppermute | solution.py:27
  36.6 0.2 collective-permute-start.8
  36.8 0.7 constant_dynamic-update-slice_fusion.3
  37.5 3.0 %collective-permute-done.8 = f32[8,896]{1,0:T(8,128)S(1)} collective-permute-done((f32[8,896]{1,0:T(8,128)S(1)}, f32[8,896]{1,0:T(8,128)S(1)}, u32[]{:S(2)}, u32[]{:S(2)}) %collective-permute-start.8) | collective-permute-done | bytes 28704 | tf_op jit(solution)/shard_map/ppermute | solution.py:27
  40.5 1.7 %shard_map.104 = (bf16[256,512]{1,0:T(8,128)(2,1)}, f32[8,128]{1,0:T(8,128)}) custom-call(bf16[4096,512]{1,0:T(8,128)(2,1)} %wt.7, f32[8,128]{1,0:T(8,128)} %copy-done.11), custom_call_target="tpu_custom_call" | custom-call | flops 1 | bytes 1048576 | tf_op jit(solution)/shard_map/pallas_call | solution.py:93
  42.2 1.3 %collective-permute-done.7.refs_1_ = bf16[1280,512]{1,0:T(8,128)(2,1)} collective-permute-done((bf16[1280,512]{1,0:T(8,128)(2,1)}, bf16[1280,512]{1,0:T(8,128)(2,1)}, u32[]{:S(2)}, u32[]{:S(2)}) %collective-permute-start.7) | collective-permute-done | bytes 1310752 | tf_op jit(solution)/shard_map/ppermute | solution.py:428
  43.6 0.9 copy-done.4
  44.5 0.7 copy-done.13
  45.2 0.6 shard_map.105
  45.8 0.7 copy-done.5
  46.5 2.5 %constant_dynamic-update-slice_fusion.2.wt = bf16[1536,512]{1,0:T(8,128)(2,1)} fusion(bf16[1536,512]{1,0:T(8,128)(2,1)} %constant_dynamic-update-slice_fusion.3, bf16[1280,512]{1,0:T(8,128)(2,1)} %get-tuple-element.56), kind=kLoop, calls=%fused_computation.8 | loop fusion | bytes 2621440 | tf_op jit(solution)/shard_map/concatenate | solution.py:503
  49.0 0.5 collective-permute-start.9
  49.5 1.9 %collective-permute-start.11 = (f32[8,896]{1,0:T(8,128)S(1)}, f32[8,896]{1,0:T(8,128)S(1)}, u32[]{:S(2)}, u32[]{:S(2)}) collective-permute-start(f32[8,896]{1,0:T(8,128)S(1)} %add.18.refs_3_), channel_id=1, source_target_pairs={{0,1},{1,0},{2,3},{3,2},{4,5},{5,4},{6,7},{7,6},{8,9},{9,8},{10,11... | collective-permute-start | bytes 86024 | tf_op jit(solution)/shard_map/ppermute | solution.py:27
  51.4 2.0 %collective-permute-done.11 = f32[8,896]{1,0:T(8,128)S(1)} collective-permute-done((f32[8,896]{1,0:T(8,128)S(1)}, f32[8,896]{1,0:T(8,128)S(1)}, u32[]{:S(2)}, u32[]{:S(2)}) %collective-permute-start.11) | collective-permute-done | bytes 28704 | tf_op jit(solution)/shard_map/ppermute | solution.py:27
  53.4 0.1 shard_map.107.spread.refs_0_
  53.7 1.4 %collective-permute-done.10 = bf16[64,2048]{1,0:T(8,128)(2,1)S(1)} collective-permute-done((bf16[64,2048]{1,0:T(8,128)(2,1)S(1)}, bf16[64,2048]{1,0:T(8,128)(2,1)S(1)}, u32[]{:S(2)}, u32[]{:S(2)}) %collective-permute-start.10) | collective-permute-done | bytes 262176 | tf_op jit(solution)/shard_map/ppermute | solution.py:27
  55.2 1.4 %shard_map.106.left = bf16[4096,128]{1,0:T(8,128)(2,1)S(1)} custom-call(s32[2]{0:T(128)S(1)} %copy-done.9, bf16[8,128,512]{2,1,0:T(8,128)(2,1)S(1)} %pad_maximum_fusion.left), custom_call_target="tpu_custom_call" | custom-call | flops 1 | bytes 1 | tf_op jit(solution)/shard_map/pallas_call | solution.py:221
  56.6 10.5 %shard_map.108 = (bf16[896,2048]{1,0:T(8,128)(2,1)}, bf16[4096,512]{1,0:T(8,128)(2,1)}, f32[8,128]{1,0:T(8,128)S(1)}) custom-call(s32[1]{0:T(128)} %bitcast.where, bf16[896,4096]{1,0:T(8,128)(2,1)} %tok.17, bf16[4096,512]{1,0:T(8,128)(2,1)} %wt.7, bf16[4096,128]{1,0:T(8,128)(2,1)S(1)} %shard_map.106.left, ...), custom_call_target="tpu_custom_call" | custom-call | flops 1 | bytes 1 | tf_op jit(solution)/shard_map/pallas_call | solution.py:334
  67.1 1.3 %copy-done.3 = bf16[896,448]{1,0:T(8,128)(2,1)S(1)} copy-done((bf16[896,448]{1,0:T(8,128)(2,1)S(1)}, bf16[896,448]{1,0:T(8,128)(2,1)}, u32[]{:S(2)}) %copy-start.3) | copy-done | bytes 802840
  68.4 9.9 %shard_map.109 = (bf16[896,2048]{1,0:T(8,128)(2,1)}, f32[8,128]{1,0:T(8,128)S(1)}) custom-call(s32[1]{0:T(128)} %bitcast.5.where, bf16[896,4096]{1,0:T(8,128)(2,1)} %tok.17, bf16[4096,512]{1,0:T(8,128)(2,1)} %get-tuple-element.57.wt, bf16[4096,128]{1,0:T(8,128)(2,1)S(1)} %shard_map.106.left, ...), custom_call_target="tpu_custom_call", output_to_operand_aliasing={{0}: (8, {})} | custom-call | flops 1 | bytes 1 | tf_op jit(solution)/shard_map/pallas_call | solution.py:334
  78.3 3.9 %shard_map.110.refs_2_.refs_0_ = f32[896,512]{1,0:T(8,128)S(1)} custom-call(s32[1]{0:T(128)} %bitcast.4.where, bf16[896,4096]{1,0:T(8,128)(2,1)S(1)} %bitcast.8, bf16[1536,512]{1,0:T(8,128)(2,1)} %constant_dynamic-update-slice_fusion.2.wt, bf16[4096,128]{1,0:T(8,128)(2,1)S(1)} %shard_map.106.left, ...), custom_call_target="tpu_custom_call" | custom-call | flops 1 | bytes 1 | tf_op jit(solution)/shard_map/pallas_call | solution.py:334
  82.2 3.9 %shard_map.111.refs_1_.refs_0_ = f32[896,512]{1,0:T(8,128)S(1)} custom-call(s32[1]{0:T(128)} %bitcast.3.where, bf16[896,4096]{1,0:T(8,128)(2,1)S(1)} %bitcast.8, bf16[1536,512]{1,0:T(8,128)(2,1)} %collective-permute-done.14.wt, bf16[4096,128]{1,0:T(8,128)(2,1)S(1)} %shard_map.106.left, bf16[128,2048]{1,0:T(8,128)(2,1)S(1)} %constant_dynamic-update-slice_fusion.right, ...), custom_call_target="tpu_custom_call" | custom-call | flops 1 | bytes 1 | tf_op jit(solution)/shard_map/pallas_call | solution.py:334
  86.1 7.8 %collective-permute-done.13.refs_0_ = bf16[2304,512]{1,0:T(8,128)(2,1)} collective-permute-done((bf16[2304,512]{1,0:T(8,128)(2,1)}, bf16[2304,512]{1,0:T(8,128)(2,1)}, u32[]{:S(2)}, u32[]{:S(2)}) %collective-permute-start.13) | collective-permute-done | bytes 2359328 | tf_op jit(solution)/shard_map/ppermute | solution.py:428
  93.9 1.7 %collective-permute-start.12 = (bf16[256,512]{1,0:T(8,128)(2,1)S(1)}, bf16[256,512]{1,0:T(8,128)(2,1)S(1)}, u32[]{:S(2)}, u32[]{:S(2)}) collective-permute-start(bf16[256,512]{1,0:T(8,128)(2,1)S(1)} %copy-done.6), channel_id=1, source_target_pairs={{0,16},{8,24},{16,0},{24,8},{1,17},{9,25},{17,1},{25,9},{2,18},{10... | collective-permute-start | bytes 786440 | tf_op jit(solution)/shard_map/ppermute | solution.py:428
  95.7 4.6 %shard_map.113.refs_1_.before = f32[896,512]{1,0:T(8,128)S(1)} custom-call(s32[1]{0:T(128)} %bitcast.4.where, bf16[896,4096]{1,0:T(8,128)(2,1)S(1)} %bitcast.8, bf16[2304,512]{1,0:T(8,128)(2,1)} %shard_map.112.wt, bf16[4096,128]{1,0:T(8,128)(2,1)S(1)} %shard_map.106.left, ...), custom_call_target="tpu_custom_call", output_to_operand_aliasing={{}: (5, {})} | custom-call | flops 1 | bytes 1 | tf_op jit(solution)/shard_map/pallas_call | solution.py:334
  100.3 3.0 %shard_map.114.refs_1_.before = f32[896,512]{1,0:T(8,128)S(1)} custom-call(s32[1]{0:T(128)} %bitcast.3.where, bf16[896,4096]{1,0:T(8,128)(2,1)S(1)} %bitcast.8, bf16[2304,512]{1,0:T(8,128)(2,1)S(1)} %collective-permute-done.15.wt, bf16[4096,128]{1,0:T(8,128)(2,1)S(1)} %shard_map.106.left, ...), custom_call_target="tpu_custom_call", output_to_operand_aliasing={{}: (5, {})} | custom-call | flops 1 | bytes 1 | tf_op jit(solution)/shard_map/pallas_call | solution.py:334
  103.3 0.3 collective-permute-start.16
  103.6 1.4 %shard_map.116.acts = bf16[896,2048]{1,0:T(8,128)(2,1)} custom-call(s32[1]{0:T(128)} %bitcast.4.where, bf16[896,4096]{1,0:T(8,128)(2,1)S(1)} %bitcast.8, bf16[256,512]{1,0:T(8,128)(2,1)S(1)} %shard_map.115.wt, bf16[4096,128]{1,0:T(8,128)(2,1)S(1)} %shard_map.106.left, ...), custom_call_target="tpu_custom_call", output_to_operand_aliasing={{}: (6, {})} | custom-call | flops 1 | bytes 1 | tf_op jit(solution)/shard_map/pallas_call | solution.py:334
  105.0 1.4 %shard_map.117 = bf16[896,2048]{1,0:T(8,128)(2,1)} custom-call(s32[1]{0:T(128)} %bitcast.3.where, bf16[896,4096]{1,0:T(8,128)(2,1)S(1)} %bitcast.8, bf16[256,512]{1,0:T(8,128)(2,1)S(1)} %collective-permute-done.16.wt, bf16[4096,128]{1,0:T(8,128)(2,1)S(1)} %shard_map.106.left, ...), custom_call_target="tpu_custom_call", output_to_operand_aliasing={{}: (6, {})} | custom-call | flops 1 | bytes 1 | tf_op jit(solution)/shard_map/pallas_call | solution.py:334
  (70 shorter events, 0.5 us)
Async XLA Ops:
  0.6 21.2 %collective-permute-start.3 = (bf16[4096,512]{1,0:T(8,128)(2,1)}, bf16[4096,512]{1,0:T(8,128)(2,1)}, u32[]{:S(2)}, u32[]{:S(2)}) collective-permute-start(bf16[4096,512]{1,0:T(8,128)(2,1)} %wt.7), channel_id=1, source_target_pairs={{0,8},{8,0},{16,24},{24,16},{1,9},{9,1},{17,25},{25,17},{2,10},{10... | collective-permute-start | bytes 12582920 | tf_op jit(solution)/shard_map/ppermute | solution.py:27
  2.1 11.1 %collective-permute-start.1 = (bf16[256,512]{1,0:T(8,128)(2,1)S(1)}, bf16[256,512]{1,0:T(8,128)(2,1)S(1)}, u32[]{:S(2)}, u32[]{:S(2)}) collective-permute-start(bf16[256,512]{1,0:T(8,128)(2,1)S(1)} %slice.18), channel_id=1, source_target_pairs={{0,16},{8,24},{16,0},{24,8},{1,17},{9,25},{17,1},{25,9},{2,18},{10... | collective-permute-start | bytes 786440 | tf_op jit(solution)/shard_map/ppermute | solution.py:428
  7.2 8.2 %collective-permute-start = (bf16[160,512]{1,0:T(8,128)(2,1)}, bf16[160,512]{1,0:T(8,128)(2,1)S(1)}, u32[]{:S(2)}, u32[]{:S(2)}) collective-permute-start(bf16[160,512]{1,0:T(8,128)(2,1)} %get-tuple-element.33), channel_id=1, source_target_pairs={{0,16},{8,24},{16,0},{24,8},{1,17},{9,25},{17,1},{25,9},{2,18},{10... | collective-permute-start | bytes 491528 | tf_op jit(solution)/shard_map/ppermute | solution.py:428
  7.3 4.5 %copy-start.16 = (bf16[112,4,512]{2,1,0:T(4,128)(2,1)S(1)}, bf16[112,4,512]{2,1,0:T(4,128)(2,1)}, u32[]{:S(2)}) copy-start(bf16[112,4,512]{2,1,0:T(4,128)(2,1)} %param.14) | copy-start | bytes 1376260
  7.3 8.1 %copy-start.18 = (bf16[32,512]{1,0:T(8,128)(2,1)S(1)}, bf16[32,512]{1,0:T(8,128)(2,1)}, u32[]{:S(2)}) copy-start(bf16[32,512]{1,0:T(8,128)(2,1)} %get-tuple-element.32) | copy-start | bytes 98308
  9.7 8.8 %copy-start.17 = (bf16[32,2048]{1,0:T(8,128)(2,1)S(1)}, bf16[32,2048]{1,0:T(8,128)(2,1)}, u32[]{:S(2)}) copy-start(bf16[32,2048]{1,0:T(8,128)(2,1)} %get-tuple-element.40) | copy-start | bytes 393220
  9.7 33.8 %collective-permute-start.7 = (bf16[1280,512]{1,0:T(8,128)(2,1)}, bf16[1280,512]{1,0:T(8,128)(2,1)}, u32[]{:S(2)}, u32[]{:S(2)}) collective-permute-start(bf16[1280,512]{1,0:T(8,128)(2,1)} %get-tuple-element.46), channel_id=1, source_target_pairs={{0,16},{8,24},{16,0},{24,8},{1,17},{9,25},{17,1},{25,9},{2,18},{10... | collective-permute-start | bytes 3932168 | tf_op jit(solution)/shard_map/ppermute | solution.py:428
  13.3 0.7 copy-start.10
  15.4 3.1 %copy-start.14 = (f32[8,128]{1,0:T(8,128)}, f32[8,128]{1,0:T(8,128)S(1)}, u32[]{:S(2)}) copy-start(f32[8,128]{1,0:T(8,128)S(1)} %get-tuple-element.41.after) | copy-start | bytes 12292
  15.4 6.4 %collective-permute-start.2 = (bf16[1,64,512]{2,1,0:T(8,128)(2,1)S(1)}, bf16[1,64,512]{2,1,0:T(8,128)(2,1)S(1)}, u32[]{:S(2)}, u32[]{:S(2)}) collective-permute-start(bf16[1,64,512]{2,1,0:T(8,128)(2,1)S(1)} %get-tuple-element.39), channel_id=1, source_target_pairs={{0,4},{1,5},{2,6},{3,7},{4,0},{5,1},{6,2},{7,3},{8,12},{9,13},{10,... | collective-permute-start | bytes 196616 | tf_op jit(solution)/shard_map/ppermute | solution.py:27
  21.9 0.7 copy-start.7
  22.6 2.2 %copy-start.8 = (f32[8,896]{1,0:T(8,128)S(1)}, f32[8,896]{1,0:T(8,128)}, u32[]{:S(2)}) copy-start(f32[8,896]{1,0:T(8,128)} %shard_map.100.refs_3_) | copy-start | bytes 86020
  22.6 0.6 copy-start.15
  23.2 11.8 %collective-permute-start.4 = (bf16[2,64,512]{2,1,0:T(8,128)(2,1)S(1)}, bf16[2,64,512]{2,1,0:T(8,128)(2,1)S(1)}, u32[]{:S(2)}, u32[]{:S(2)}) collective-permute-start(bf16[2,64,512]{2,1,0:T(8,128)(2,1)S(1)} %get-tuple-element.42), channel_id=1, source_target_pairs={{0,2},{1,3},{2,0},{3,1},{4,6},{5,7},{6,4},{7,5},{8,10},{9,11},{10,... | collective-permute-start | bytes 393224 | tf_op jit(solution)/shard_map/ppermute | solution.py:27
  24.8 10.2 %collective-permute-start.5 = (f32[8,896]{1,0:T(8,128)S(1)}, f32[8,896]{1,0:T(8,128)S(1)}, u32[]{:S(2)}, u32[]{:S(2)}) collective-permute-start(f32[8,896]{1,0:T(8,128)S(1)} %copy-done.8), channel_id=1, source_target_pairs={{0,4},{1,5},{2,6},{3,7},{4,0},{5,1},{6,2},{7,3},{8,12},{9,13},{10,... | collective-permute-start | bytes 86024 | tf_op jit(solution)/shard_map/ppermute | solution.py:27
  30.4 4.6 %copy-start.12 = (f32[8,128]{1,0:T(8,128)S(1)}, f32[8,128]{1,0:T(8,128)}, u32[]{:S(2)}) copy-start(f32[8,128]{1,0:T(8,128)} %get-tuple-element.44.refs_2_) | copy-start | bytes 12292
  30.4 63.5 %collective-permute-start.13 = (bf16[2304,512]{1,0:T(8,128)(2,1)}, bf16[2304,512]{1,0:T(8,128)(2,1)}, u32[]{:S(2)}, u32[]{:S(2)}) collective-permute-start(bf16[2304,512]{1,0:T(8,128)(2,1)} %get-tuple-element.54), channel_id=1, source_target_pairs={{0,16},{8,24},{16,0},{24,8},{1,17},{9,25},{17,1},{25,9},{2,18},{10... | collective-permute-start | bytes 7077896 | tf_op jit(solution)/shard_map/ppermute | solution.py:428
  35.0 7.2 %copy-start = (bf16[448,2048]{1,0:T(8,128)(2,1)}, bf16[448,2048]{1,0:T(8,128)(2,1)S(1)}, u32[]{:S(2)}) copy-start(bf16[448,2048]{1,0:T(8,128)(2,1)S(1)} %reshape.28.refs_3_.rights.refs_1_) | copy-start | bytes 5505028
  35.1 2.5 %copy-start.11 = (f32[8,128]{1,0:T(8,128)}, f32[8,128]{1,0:T(8,128)S(1)}, u32[]{:S(2)}) copy-start(f32[8,128]{1,0:T(8,128)S(1)} %get-tuple-element.47.after) | copy-start | bytes 12292
  35.1 7.1 %collective-permute-start.6 = (bf16[4,64,512]{2,1,0:T(8,128)(2,1)S(1)}, bf16[4,64,512]{2,1,0:T(8,128)(2,1)S(1)}, u32[]{:S(2)}, u32[]{:S(2)}) collective-permute-start(bf16[4,64,512]{2,1,0:T(8,128)(2,1)S(1)} %get-tuple-element.45), channel_id=1, source_target_pairs={{0,1},{1,0},{2,3},{3,2},{4,5},{5,4},{6,7},{7,6},{8,9},{9,8},{10,11... | collective-permute-start | bytes 786440 | tf_op jit(solution)/shard_map/ppermute | solution.py:27
  36.6 3.9 %collective-permute-start.8 = (f32[8,896]{1,0:T(8,128)S(1)}, f32[8,896]{1,0:T(8,128)S(1)}, u32[]{:S(2)}, u32[]{:S(2)}) collective-permute-start(f32[8,896]{1,0:T(8,128)S(1)} %add.17.refs_1_), channel_id=1, source_target_pairs={{0,2},{1,3},{2,0},{3,1},{4,6},{5,7},{6,4},{7,5},{8,10},{9,11},{10,... | collective-permute-start | bytes 86024 | tf_op jit(solution)/shard_map/ppermute | solution.py:27
  43.6 1.0 copy-start.4
  44.5 0.7 copy-start.13
  45.8 0.7 copy-start.5
  49.0 33.2 %collective-permute-start.14 = (bf16[1536,512]{1,0:T(8,128)(2,1)}, bf16[1536,512]{1,0:T(8,128)(2,1)}, u32[]{:S(2)}, u32[]{:S(2)}) collective-permute-start(bf16[1536,512]{1,0:T(8,128)(2,1)} %constant_dynamic-update-slice_fusion.2.wt), channel_id=1, source_target_pairs={{0,8},{8,0},{16,24},{24,16},{1,9},{9,1},{17,25},{25,17},{2,10},{10... | collective-permute-start | bytes 4718600 | tf_op jit(solution)/shard_map/ppermute | solution.py:27
  49.0 4.7 %collective-permute-start.9 = (bf16[8,64,512]{2,1,0:T(8,128)(2,1)S(1)}, bf16[8,64,512]{2,1,0:T(8,128)(2,1)S(1)}, u32[]{:S(2)}, u32[]{:S(2)}) collective-permute-start(bf16[8,64,512]{2,1,0:T(8,128)(2,1)S(1)} %get-tuple-element.50), channel_id=1, source_target_pairs={{0,8},{8,0},{16,24},{24,16},{1,9},{9,1},{17,25},{25,17},{2,10},{10... | collective-permute-start | bytes 1572872 | tf_op jit(solution)/shard_map/ppermute | solution.py:27
  49.5 3.9 %collective-permute-start.11 = (f32[8,896]{1,0:T(8,128)S(1)}, f32[8,896]{1,0:T(8,128)S(1)}, u32[]{:S(2)}, u32[]{:S(2)}) collective-permute-start(f32[8,896]{1,0:T(8,128)S(1)} %add.18.refs_3_), channel_id=1, source_target_pairs={{0,1},{1,0},{2,3},{3,2},{4,5},{5,4},{6,7},{7,6},{8,9},{9,8},{10,11... | collective-permute-start | bytes 86024 | tf_op jit(solution)/shard_map/ppermute | solution.py:27
  53.4 1.8 %copy-start.9 = (s32[2]{0:T(128)S(1)}, s32[2]{0:T(128)}, u32[]{:S(2)}) copy-start(s32[2]{0:T(128)} %pad_add_fusion.where.refs_0_) | copy-start | bytes 28
  53.5 3.1 %copy-start.2 = (bf16[896,448]{1,0:T(8,128)(2,1)}, bf16[896,448]{1,0:T(8,128)(2,1)S(1)}, u32[]{:S(2)}) copy-start(bf16[896,448]{1,0:T(8,128)(2,1)S(1)} %shard_map.107.spread.refs_0_) | copy-start | bytes 2408452
  53.5 1.6 %collective-permute-start.10 = (bf16[64,2048]{1,0:T(8,128)(2,1)S(1)}, bf16[64,2048]{1,0:T(8,128)(2,1)S(1)}, u32[]{:S(2)}, u32[]{:S(2)}) collective-permute-start(bf16[64,2048]{1,0:T(8,128)(2,1)S(1)} %get-tuple-element.51), channel_id=1, source_target_pairs={{0,8},{8,0},{16,24},{24,16},{1,9},{9,1},{17,25},{25,17},{2,10},{10... | collective-permute-start | bytes 786440 | tf_op jit(solution)/shard_map/ppermute | solution.py:27
  67.1 11.2 %slice-start = ((s8[7340032]{0:T(1024)(128)(4,1)}), s8[4194304]{0:T(1024)(128)(4,1)S(1)}, s32[]{:S(2)}) async-start(s8[7340032]{0:T(1024)(128)(4,1)} %bitcast.7), calls=%async_computation | async-start | bytes 8388608
  67.1 1.3 %copy-start.3 = (bf16[896,448]{1,0:T(8,128)(2,1)S(1)}, bf16[896,448]{1,0:T(8,128)(2,1)}, u32[]{:S(2)}) copy-start(bf16[896,448]{1,0:T(8,128)(2,1)} %copy-done.2) | copy-start | bytes 2408452
  68.4 9.9 %slice-start.1 = ((s8[7340032]{0:T(1024)(128)(4,1)}), s8[3145728]{0:T(1024)(128)(4,1)S(1)}, s32[]{:S(2)}) async-start(s8[7340032]{0:T(1024)(128)(4,1)} %bitcast.7), calls=%async_computation.1 | async-start | bytes 6291456
  68.4 9.9 %copy-start.1 = (bf16[448,2048]{1,0:T(8,128)(2,1)S(1)}, bf16[448,2048]{1,0:T(8,128)(2,1)}, u32[]{:S(2)}) copy-start(bf16[448,2048]{1,0:T(8,128)(2,1)} %copy-done) | copy-start | bytes 5505028
  86.1 7.8 %copy-start.6 = (bf16[256,512]{1,0:T(8,128)(2,1)S(1)}, bf16[256,512]{1,0:T(8,128)(2,1)}, u32[]{:S(2)}) copy-start(bf16[256,512]{1,0:T(8,128)(2,1)} %copy-done.5) | copy-start | bytes 786436
  93.9 6.4 %collective-permute-start.15 = (bf16[2304,512]{1,0:T(8,128)(2,1)}, bf16[2304,512]{1,0:T(8,128)(2,1)S(1)}, u32[]{:S(2)}, u32[]{:S(2)}) collective-permute-start(bf16[2304,512]{1,0:T(8,128)(2,1)} %shard_map.112.wt), channel_id=1, source_target_pairs={{0,8},{8,0},{16,24},{24,16},{1,9},{9,1},{17,25},{25,17},{2,10},{10... | collective-permute-start | bytes 7077896 | tf_op jit(solution)/shard_map/ppermute | solution.py:27
  93.9 9.4 %collective-permute-start.12 = (bf16[256,512]{1,0:T(8,128)(2,1)S(1)}, bf16[256,512]{1,0:T(8,128)(2,1)S(1)}, u32[]{:S(2)}, u32[]{:S(2)}) collective-permute-start(bf16[256,512]{1,0:T(8,128)(2,1)S(1)} %copy-done.6), channel_id=1, source_target_pairs={{0,16},{8,24},{16,0},{24,8},{1,17},{9,25},{17,1},{25,9},{2,18},{10... | collective-permute-start | bytes 786440 | tf_op jit(solution)/shard_map/ppermute | solution.py:428
  103.3 1.7 %collective-permute-start.16 = (bf16[256,512]{1,0:T(8,128)(2,1)S(1)}, bf16[256,512]{1,0:T(8,128)(2,1)S(1)}, u32[]{:S(2)}, u32[]{:S(2)}) collective-permute-start(bf16[256,512]{1,0:T(8,128)(2,1)S(1)} %shard_map.115.wt), channel_id=1, source_target_pairs={{0,8},{8,0},{16,24},{24,16},{1,9},{9,1},{17,25},{25,17},{2,10},{10... | collective-permute-start | bytes 786440 | tf_op jit(solution)/shard_map/ppermute | solution.py:27
